TPU v7x, 32 devices: a whole 2x2x4 slice. The times are simulated.
32 devices in a mesh: narrow: 4 (over x, core), wide: 8 (over z, y).
Axes of the slice: x: 2, y: 2, z: 4, core: 2. Of those that a mesh axis runs over, the one named last changes fastest.
Arguments:
- start_block: bfloat16 [4, 8, 32, 3584], P('narrow', 'wide'), may hold values from -360 to 360
- weights: bfloat16 [4, 8, 28, 12, 128, 128], P('narrow', 'wide'), may hold values from 0.049804688 to 1
- pattern: int32 [4, 8, 28, 12], P('narrow', 'wide'), may hold values from 0 to 33, as said below
Outputs:
- filtered_basis: float32 [4, 8, 32, 3584], P('narrow', 'wide')
Inputs may be any that keep to these rules, and one draw needn't show every extreme that they name: `pattern`: slot 0 of each row block names the block itself; slots below 9, and every slot of blocks from 24 on, name blocks of the own tile; the other slots of a rim block name block value - 28 of the facing neighbour's rim that faces it.
All inputs are finite; a program needn't handle non-finite values.
Results may differ from a plain program's by a relative error of at most 0.0031.
Values may be sent and summed in bfloat16 or wider, within the bound.
No kernel may reach another device: no remote copies, remote signals or barrier semaphores. Data moves between devices by JAX's collectives and lax.ppermute only.
A program may use at most 64 MiB of HBM per device.

v0:
```python
import math

import jax
import jax.numpy as jnp
from jax import lax
from jax.sharding import PartitionSpec as P

RIM = 6


lower_edge = 0.3
center = (2.0 + lower_edge) / 2.0
half_width = (2.0 - lower_edge) / 2.0
highest = lax.Precision.HIGHEST
selecting = lax.Precision.HIGH
opposite_rim = (1, 0, 3, 2)


def from_behind(shard, axis, by):
    peers = lax.axis_size(axis)
    pairs = [(i, i + by) for i in range(peers) if 0 <= i + by < peers]
    return lax.ppermute(shard, axis, pairs)


def rim_slice(values, rim_index, rim_blocks):
    return values[:, rim_index * rim_blocks : (rim_index + 1) * rim_blocks]


def narrow_rims(sent_values, sent_terms, step_by):
    return from_behind((sent_values, sent_terms), "narrow", step_by)


def wide_rims(sent_values, sent_terms, step_by):
    return from_behind((sent_values, sent_terms), "wide", step_by)


def body(start_block, weights, pattern):
    weight_tile = weights[0, 0]
    pattern_tile = pattern[0, 0]
    block_count = weight_tile.shape[0]
    block_size = weight_tile.shape[2]
    vec_count = start_block.shape[2]
    rim_blocks = RIM
    extended = block_count + 4 * rim_blocks
    block_ids = jnp.arange(block_count, dtype=jnp.int32)
    facing = jnp.minimum(block_ids // rim_blocks, 3)
    target = jnp.where(
        pattern_tile < block_count,
        pattern_tile,
        block_count + facing[:, None] * rim_blocks + (pattern_tile - block_count),
    )
    selector = (target[:, :, None] == jnp.arange(extended, dtype=jnp.int32)[None, None, :]).astype(
        jnp.float32
    )

    def affinity(values):
        vec_rows = values.shape[0]
        transposed = jnp.einsum(
            "bsrc,nbr->bsnc", weight_tile, values, preferred_element_type=jnp.float32
        )
        segments = []
        grouped = jnp.einsum("bse,bsnc->nec", selector, transposed, precision=selecting)
        outgoing = grouped[:, block_count:].astype(jnp.bfloat16)
        rim_added = []
        for direction in range(4):
            source = opposite_rim[direction]
            sent = rim_slice(values, source, rim_blocks)
            sent_terms = rim_slice(outgoing, source, rim_blocks)
            if direction < 2:
                received, rim_terms = narrow_rims(sent, sent_terms, 1 - 2 * direction)
            else:
                received, rim_terms = wide_rims(sent, sent_terms, 5 - 2 * direction)
            segments.append(received)
            rim_added.append(rim_terms.astype(jnp.float32))
        interior = jnp.zeros((vec_rows, block_count - 4 * rim_blocks, block_size), jnp.float32)
        back_terms = grouped[:, :block_count] + jnp.concatenate(rim_added + [interior], axis=1)
        extended_values = jnp.concatenate([values] + segments, axis=1)
        gathered = jnp.take(extended_values, target, axis=1)
        forward = jnp.einsum(
            "bsrc,nbsc->nbr", weight_tile, gathered, preferred_element_type=jnp.float32
        )
        return 0.5 * (forward + back_terms)

    ones_block = jnp.ones((1, block_count, block_size), jnp.bfloat16)
    degree = affinity(ones_block)
    inv_root = 1.0 / jnp.sqrt(degree)

    def laplace(vectors):
        scaled = (inv_root * vectors).astype(jnp.bfloat16)
        return vectors - inv_root * affinity(scaled)

    initial = start_block[0, 0].reshape(vec_count, block_count, block_size).astype(jnp.float32)
    previous = initial
    current = (laplace(initial) - center * initial) / half_width
    for repeat in range(2):
        following = 2.0 * (laplace(current) - center * current) / half_width - previous
        previous, current = (current, following)
    filtered = current.reshape(vec_count, block_count * block_size)
    local_gram = jnp.dot(filtered, filtered.T, precision=highest)
    factor = jnp.linalg.cholesky(lax.psum(local_gram, ("narrow", "wide")))
    inverse = lax.linalg.triangular_solve(
        factor, jnp.eye(vec_count, dtype=jnp.float32), left_side=True, lower=True
    )
    doc_count = lax.axis_size("narrow") * lax.axis_size("wide") * block_count * block_size
    result_basis = jnp.dot(inverse, filtered, precision=highest) * math.sqrt(doc_count)
    return result_basis.reshape(1, 1, vec_count, block_count * block_size)


def solution(mesh):
    placed = (
        P("narrow", "wide", None, None),
        P("narrow", "wide", None, None, None, None),
        P("narrow", "wide", None, None),
    )
    return jax.shard_map(
        body, mesh=mesh, in_specs=placed, out_specs=P("narrow", "wide", None, None), check_vma=False
    )
```

profile of v0, /device:TPU:0, one launch (start us, length us, event | category | flops | bytes accessed | tf_op | source)
XLA Modules:
  0.0 239.8 jit_solution(3484885843351426211)
XLA Ops:
  0.0 2.3 collective-permute-start
  2.4 1.3 collective-permute-start.1
  3.7 4.3 %collective-permute-start.2 = (bf16[1,6,128]{2,1,0:T(8,128)(2,1)S(1)}, bf16[1,6,128]{2,1,0:T(8,128)(2,1)S(1)}, u32[]{:S(2)}, u32[]{:S(2)}) collective-permute-start(bf16[1,6,128]{2,1,0:T(8,128)(2,1)S(1)} %broadcast.232), channel_id=1, source_target_pairs={{0,1},{1,2},{2,3},{3,4},{4,5},{5,6},{6,7},{8,9},{9,10},{10,11},{11... | collective-permute-start | bytes 4616 | tf_op jit(solution)/shard_map/ppermute | solution.py:22
  7.9 1.3 collective-permute-start.3
  9.3 5.7 %fusion.12 = f32[28,1,12,128]{3,1,2,0:T(1,128)S(1)} fusion(bf16[1,1,28,12,128,128]{5,4,3,2,1,0:T(8,128)(2,1)} %param.6), kind=kOutput, calls=%fused_computation.16 | convolution fusion | flops 11010048 | bytes 11182080 | tf_op jit(solution)/shard_map/bsrc,nbr->bsnc/dot_general | solution.py:58
  15.3 4.0 %collective-permute-start.4 = (bf16[1,6,128]{2,1,0:T(8,128)(2,1)S(1)}, bf16[1,6,128]{2,1,0:T(8,128)(2,1)S(1)}, u32[]{:S(2)}, u32[]{:S(2)}) collective-permute-start(bf16[1,6,128]{2,1,0:T(8,128)(2,1)S(1)} %get-tuple-element.47), channel_id=1, source_target_pairs={{0,8},{8,16},{16,24},{1,9},{9,17},{17,25},{2,10},{10,18},{18,26},{... | collective-permute-start | bytes 4616 | tf_op jit(solution)/shard_map/ppermute | solution.py:22
  20.1 1.3 collective-permute-start.5
  21.4 4.3 %collective-permute-start.6 = (bf16[1,6,128]{2,1,0:T(8,128)(2,1)S(1)}, bf16[1,6,128]{2,1,0:T(8,128)(2,1)S(1)}, u32[]{:S(2)}, u32[]{:S(2)}) collective-permute-start(bf16[1,6,128]{2,1,0:T(8,128)(2,1)S(1)} %get-tuple-element.45), channel_id=1, source_target_pairs={{0,1},{1,2},{2,3},{3,4},{4,5},{5,6},{6,7},{8,9},{9,10},{10,11},{11... | collective-permute-start | bytes 4616 | tf_op jit(solution)/shard_map/ppermute | solution.py:22
  25.7 1.3 collective-permute-start.7
  27.3 1.4 gather_fusion
  28.8 5.8 %fusion.14 = f32[28,1,128,1]{2,1,3,0:T(1,128)S(1)} fusion(bf16[1,1,28,12,128,128]{5,4,3,2,1,0:T(8,128)(2,1)} %param.6, bf16[28,12,128,1]{2,1,0,3:T(8,128)(2,1)S(1)} %select_bitcast_fusion), kind=kOutput, calls=%fused_computation.18 | convolution fusion | flops 11010048 | bytes 11110400 | tf_op jit(solution)/shard_map/bsrc,nbsc->nbr/dot_general | solution.py:79
  35.8 5.1 %fusion.8 = f32[28,32,12,128]{3,1,2,0:T(8,128)S(1)} fusion(bf16[1,1,28,12,128,128]{5,4,3,2,1,0:T(8,128)(2,1)} %param.6, bf16[32,28,128]{2,0,1:T(8,128)(2,1)S(1)} %get-tuple-element.19), kind=kOutput, calls=%fused_computation.12 | convolution fusion | flops 352321536 | bytes 16744448 | tf_op jit(solution)/shard_map/bsrc,nbr->bsnc/dot_general | solution.py:58
  40.9 4.8 %fusion.38 = f32[32,128,52]{1,2,0:T(8,128)S(1)} fusion(f32[28,32,12,128]{3,1,2,0:T(8,128)S(1)} %fusion.8, s32[28,12]{0,1:T(8,128)S(1)} %get-tuple-element.49), kind=kOutput, calls=%fused_computation.43 | convolution fusion | flops 429409344 | bytes 6358336 | tf_op jit(solution)/shard_map/bse,bsnc->nec/dot_general | solution.py:62
  45.8 1.1 fusion.179
  46.9 4.6 %collective-permute-start.12 = (bf16[32,6,128]{2,0,1:T(8,128)(2,1)S(1)}, bf16[32,6,128]{2,0,1:T(8,128)(2,1)S(1)}, u32[]{:S(2)}, u32[]{:S(2)}) collective-permute-start(bf16[32,6,128]{2,0,1:T(8,128)(2,1)S(1)} %get-tuple-element.31), channel_id=1, source_target_pairs={{0,8},{8,16},{16,24},{1,9},{9,17},{17,25},{2,10},{10,18},{18,26},{... | collective-permute-start | bytes 147464 | tf_op jit(solution)/shard_map/ppermute | solution.py:22
  51.4 1.3 collective-permute-start.13
  52.7 5.0 %collective-permute-start.14 = (bf16[32,6,128]{2,0,1:T(8,128)(2,1)S(1)}, bf16[32,6,128]{2,0,1:T(8,128)(2,1)S(1)}, u32[]{:S(2)}, u32[]{:S(2)}) collective-permute-start(bf16[32,6,128]{2,0,1:T(8,128)(2,1)S(1)} %get-tuple-element.29), channel_id=1, source_target_pairs={{0,1},{1,2},{2,3},{3,4},{4,5},{5,6},{6,7},{8,9},{9,10},{10,11},{11... | collective-permute-start | bytes 147464 | tf_op jit(solution)/shard_map/ppermute | solution.py:22
  57.7 1.3 collective-permute-start.15
  59.0 4.3 %collective-permute-start.8 = (bf16[32,6,128]{2,0,1:T(8,128)(2,1)S(1)}, bf16[32,6,128]{2,0,1:T(8,128)(2,1)S(1)}, u32[]{:S(2)}, u32[]{:S(2)}) collective-permute-start(bf16[32,6,128]{2,0,1:T(8,128)(2,1)S(1)} %get-tuple-element.43), channel_id=1, source_target_pairs={{0,8},{8,16},{16,24},{1,9},{9,17},{17,25},{2,10},{10,18},{18,26},{... | collective-permute-start | bytes 147464 | tf_op jit(solution)/shard_map/ppermute | solution.py:22
  63.3 1.3 collective-permute-start.9
  64.6 5.4 %collective-permute-start.10 = (bf16[32,6,128]{2,0,1:T(8,128)(2,1)S(1)}, bf16[32,6,128]{2,0,1:T(8,128)(2,1)S(1)}, u32[]{:S(2)}, u32[]{:S(2)}) collective-permute-start(bf16[32,6,128]{2,0,1:T(8,128)(2,1)S(1)} %get-tuple-element.41), channel_id=1, source_target_pairs={{0,1},{1,2},{2,3},{3,4},{4,5},{5,6},{6,7},{8,9},{9,10},{10,11},{11... | collective-permute-start | bytes 147464 | tf_op jit(solution)/shard_map/ppermute | solution.py:22
  70.1 1.5 collective-permute-start.11
  71.8 4.9 %collective-permute-done.11 = bf16[32,6,128]{2,0,1:T(8,128)(2,1)S(1)} collective-permute-done((bf16[32,6,128]{2,0,1:T(8,128)(2,1)S(1)}, bf16[32,6,128]{2,0,1:T(8,128)(2,1)S(1)}, u32[]{:S(2)}, u32[]{:S(2)}) %collective-permute-start.11) | collective-permute-done | bytes 49184 | tf_op jit(solution)/shard_map/ppermute | solution.py:22
  76.7 3.0 %gather_fusion.1 = bf16[336,32,128]{2,1,0:T(8,128)(2,1)} fusion(bf16[32,52,128]{2,0,1:T(8,128)(2,1)S(1)} %constant_dynamic-update-slice_fusion, s32[1024]{0:T(1024)S(1)} %pad_clamp_fusion), kind=kCustom, calls=%fused_computation.clone | custom fusion | bytes 5506368 | tf_op jit(solution)/shard_map/jit(_take)/gather | solution.py:78
  79.8 10.2 %constant_dynamic-update-slice_fusion.10 = (bf16[32,52,128]{2,0,1:T(8,128)(2,1)S(1)}, bf16[32,28,128]{2,0,1:T(8,128)(2,1)}, f32[32,28,128]{2,0,1:T(8,128)}) fusion(f32[28,128]{1,0:T(8,128)} %get-tuple-element.14, f32[28,128]{1,0:T(8,128)S(1)} %broadcast_multiply_fusion.1, f32[32,28,128]{2,0,1:T(8,128)} %copy-done.3, f32[32,52,128]{2,0,1:T(8,128)} %get-tuple-element.17, ...), kind=kOutput, calls=%fused_computation.113 | convolution fusion | flops 354615296 | bytes 16085328 | tf_op jit(solution)/shard_map/bsrc,nbsc->nbr/dot_general | solution.py:79
  90.0 2.5 %fusion.4 = f32[28,32,12,128]{3,1,2,0:T(8,128)S(1)} fusion(bf16[1,1,28,12,128,128]{5,4,3,2,1,0:T(8,128)(2,1)S(1)} %bitcast.280, bf16[32,28,128]{2,0,1:T(8,128)(2,1)} %get-tuple-element.13), kind=kOutput, calls=%fused_computation.8 | convolution fusion | flops 352321536 | bytes 16744448 | tf_op jit(solution)/shard_map/bsrc,nbr->bsnc/dot_general | solution.py:58
  92.5 4.8 %fusion.41 = f32[32,128,52]{1,2,0:T(8,128)S(1)} fusion(f32[28,32,12,128]{3,1,2,0:T(8,128)S(1)} %fusion.4, s32[28,12]{0,1:T(8,128)S(1)} %get-tuple-element.49), kind=kOutput, calls=%fused_computation.44 | convolution fusion | flops 429409344 | bytes 6358336 | tf_op jit(solution)/shard_map/bse,bsnc->nec/dot_general | solution.py:62
  97.3 1.1 fusion.177
  98.4 3.7 %collective-permute-start.20 = (bf16[32,6,128]{2,0,1:T(8,128)(2,1)S(1)}, bf16[32,6,128]{2,0,1:T(8,128)(2,1)S(1)}, u32[]{:S(2)}, u32[]{:S(2)}) collective-permute-start(bf16[32,6,128]{2,0,1:T(8,128)(2,1)S(1)} %get-tuple-element.27), channel_id=1, source_target_pairs={{0,8},{8,16},{16,24},{1,9},{9,17},{17,25},{2,10},{10,18},{18,26},{... | collective-permute-start | bytes 147464 | tf_op jit(solution)/shard_map/ppermute | solution.py:22
  102.1 1.3 collective-permute-start.21
  103.4 4.5 %collective-permute-start.22 = (bf16[32,6,128]{2,0,1:T(8,128)(2,1)S(1)}, bf16[32,6,128]{2,0,1:T(8,128)(2,1)S(1)}, u32[]{:S(2)}, u32[]{:S(2)}) collective-permute-start(bf16[32,6,128]{2,0,1:T(8,128)(2,1)S(1)} %get-tuple-element.25), channel_id=1, source_target_pairs={{0,1},{1,2},{2,3},{3,4},{4,5},{5,6},{6,7},{8,9},{9,10},{10,11},{11... | collective-permute-start | bytes 147464 | tf_op jit(solution)/shard_map/ppermute | solution.py:22
  108.0 1.3 collective-permute-start.23
  109.3 5.4 %collective-permute-start.16 = (bf16[32,6,128]{2,0,1:T(8,128)(2,1)S(1)}, bf16[32,6,128]{2,0,1:T(8,128)(2,1)S(1)}, u32[]{:S(2)}, u32[]{:S(2)}) collective-permute-start(bf16[32,6,128]{2,0,1:T(8,128)(2,1)S(1)} %get-tuple-element.39), channel_id=1, source_target_pairs={{0,8},{8,16},{16,24},{1,9},{9,17},{17,25},{2,10},{10,18},{18,26},{... | collective-permute-start | bytes 147464 | tf_op jit(solution)/shard_map/ppermute | solution.py:22
  114.7 1.3 collective-permute-start.17
  116.0 4.3 %collective-permute-start.18 = (bf16[32,6,128]{2,0,1:T(8,128)(2,1)S(1)}, bf16[32,6,128]{2,0,1:T(8,128)(2,1)S(1)}, u32[]{:S(2)}, u32[]{:S(2)}) collective-permute-start(bf16[32,6,128]{2,0,1:T(8,128)(2,1)S(1)} %get-tuple-element.37), channel_id=1, source_target_pairs={{0,1},{1,2},{2,3},{3,4},{4,5},{5,6},{6,7},{8,9},{9,10},{10,11},{11... | collective-permute-start | bytes 147464 | tf_op jit(solution)/shard_map/ppermute | solution.py:22
  120.3 1.5 collective-permute-start.19
  122.1 4.3 %collective-permute-done.19 = bf16[32,6,128]{2,0,1:T(8,128)(2,1)S(1)} collective-permute-done((bf16[32,6,128]{2,0,1:T(8,128)(2,1)S(1)}, bf16[32,6,128]{2,0,1:T(8,128)(2,1)S(1)}, u32[]{:S(2)}, u32[]{:S(2)}) %collective-permute-start.19) | collective-permute-done | bytes 49184 | tf_op jit(solution)/shard_map/ppermute | solution.py:22
  126.3 3.0 %gather_fusion.2 = bf16[336,32,128]{2,1,0:T(8,128)(2,1)} fusion(bf16[32,52,128]{2,0,1:T(8,128)(2,1)S(1)} %constant_dynamic-update-slice_fusion.6, s32[1024]{0:T(1024)S(1)} %pad_clamp_fusion), kind=kCustom, calls=%fused_computation.1.clone | custom fusion | bytes 5506368 | tf_op jit(solution)/shard_map/jit(_take)/gather | solution.py:78
  129.4 10.2 %constant_dynamic-update-slice_fusion.16 = (bf16[32,52,128]{2,0,1:T(8,128)(2,1)S(1)}, bf16[32,28,128]{2,0,1:T(8,128)(2,1)}, f32[32,28,128]{2,0,1:T(8,128)}) fusion(f32[28,128]{1,0:T(8,128)S(1)} %get-tuple-element.15, f32[32,28,128]{2,1,0:T(8,128)} %copy-done, f32[32,28,128]{2,0,1:T(8,128)} %get-tuple-element.52, ...), kind=kOutput, calls=%fused_computation.119 | convolution fusion | flops 354959360 | bytes 16544080 | tf_op jit(solution)/shard_map/bsrc,nbsc->nbr/dot_general | solution.py:79
  139.6 2.5 %fusion = f32[28,32,12,128]{3,1,2,0:T(8,128)S(1)} fusion(bf16[1,1,28,12,128,128]{5,4,3,2,1,0:T(8,128)(2,1)S(1)} %bitcast.282, bf16[32,28,128]{2,0,1:T(8,128)(2,1)} %get-tuple-element.9), kind=kOutput, calls=%fused_computation.4 | convolution fusion | flops 352321536 | bytes 16744448 | tf_op jit(solution)/shard_map/bsrc,nbr->bsnc/dot_general | solution.py:58
  142.1 4.8 %fusion.44 = f32[32,128,52]{1,2,0:T(8,128)S(1)} fusion(f32[28,32,12,128]{3,1,2,0:T(8,128)S(1)} %fusion, s32[28,12]{0,1:T(8,128)S(1)} %get-tuple-element.49), kind=kOutput, calls=%fused_computation.45 | convolution fusion | flops 429409344 | bytes 6358336 | tf_op jit(solution)/shard_map/bse,bsnc->nec/dot_general | solution.py:62
  147.0 1.1 fusion.176
  148.1 3.4 %collective-permute-start.28 = (bf16[32,6,128]{2,0,1:T(8,128)(2,1)S(1)}, bf16[32,6,128]{2,0,1:T(8,128)(2,1)S(1)}, u32[]{:S(2)}, u32[]{:S(2)}) collective-permute-start(bf16[32,6,128]{2,0,1:T(8,128)(2,1)S(1)} %get-tuple-element.23), channel_id=1, source_target_pairs={{0,8},{8,16},{16,24},{1,9},{9,17},{17,25},{2,10},{10,18},{18,26},{... | collective-permute-start | bytes 147464 | tf_op jit(solution)/shard_map/ppermute | solution.py:22
  151.6 5.1 %collective-permute-start.24 = (bf16[32,6,128]{2,0,1:T(8,128)(2,1)S(1)}, bf16[32,6,128]{2,0,1:T(8,128)(2,1)S(1)}, u32[]{:S(2)}, u32[]{:S(2)}) collective-permute-start(bf16[32,6,128]{2,0,1:T(8,128)(2,1)S(1)} %get-tuple-element.35), channel_id=1, source_target_pairs={{0,8},{8,16},{16,24},{1,9},{9,17},{17,25},{2,10},{10,18},{18,26},{... | collective-permute-start | bytes 147464 | tf_op jit(solution)/shard_map/ppermute | solution.py:22
  156.6 1.3 collective-permute-start.25
  157.9 3.8 %collective-permute-start.26 = (bf16[32,6,128]{2,0,1:T(8,128)(2,1)S(1)}, bf16[32,6,128]{2,0,1:T(8,128)(2,1)S(1)}, u32[]{:S(2)}, u32[]{:S(2)}) collective-permute-start(bf16[32,6,128]{2,0,1:T(8,128)(2,1)S(1)} %get-tuple-element.33), channel_id=1, source_target_pairs={{0,1},{1,2},{2,3},{3,4},{4,5},{5,6},{6,7},{8,9},{9,10},{10,11},{11... | collective-permute-start | bytes 147464 | tf_op jit(solution)/shard_map/ppermute | solution.py:22
  161.8 1.3 collective-permute-start.27
  163.1 1.3 collective-permute-start.29
  164.4 2.2 collective-permute-done.29
  166.6 4.3 %collective-permute-start.30 = (bf16[32,6,128]{2,0,1:T(8,128)(2,1)S(1)}, bf16[32,6,128]{2,0,1:T(8,128)(2,1)S(1)}, u32[]{:S(2)}, u32[]{:S(2)}) collective-permute-start(bf16[32,6,128]{2,0,1:T(8,128)(2,1)S(1)} %get-tuple-element.21), channel_id=1, source_target_pairs={{0,1},{1,2},{2,3},{3,4},{4,5},{5,6},{6,7},{8,9},{9,10},{10,11},{11... | collective-permute-start | bytes 147464 | tf_op jit(solution)/shard_map/ppermute | solution.py:22
  170.8 1.7 collective-permute-done.30
  172.6 1.5 collective-permute-start.31
  174.2 0.7 copy-done.5
  174.9 2.4 gather_fusion.3
  177.3 1.6 collective-permute-done.31
  178.8 0.7 convert_dynamic-update-slice_fusion
  179.5 0.6 constant_dynamic-update-slice_fusion.17
  180.1 7.3 %fusion.137 = f32[32,28,128]{2,0,1:T(8,128)S(1)} fusion(f32[32,28,128]{2,0,1:T(8,128)} %get-tuple-element.53, bf16[1,1,28,12,128,128]{5,4,3,2,1,0:T(8,128)(2,1)} %param.6, bf16[28,12,32,128]{3,2,1,0:T(8,128)(2,1)S(1)} %bitcast.284, pred[28,12]{1,0:T(8,128)(4,1)S(1)} %copy.13, f32[32,28,128]{2,0,1:T(8,128)} %constant_dynamic-update-slice_fusion.17, ...), kind=kOutput, calls=%fused_computation.64 | convolution fusion | flops 354729984 | bytes 16070992 | tf_op jit(solution)/shard_map/bsrc,nbsc->nbr/dot_general | solution.py:79
  187.9 43.6 %psum.7 = f32[32,32]{0,1:T(8,128)S(1)} all-reduce(f32[32,32]{0,1:T(8,128)S(1)} %convolution_bitcast_fusion.1), channel_id=1, replica_groups=mesh['narrow'=4,'wide'=8] {'narrow','wide'}, use_global_device_ids=true, to_apply=%region_0.2 | all-reduce | flops 1024 | bytes 8192 | tf_op jit(solution)/shard_map/psum | solution.py:100
  231.6 2.9 %cholesky.17 = f32[32,32]{1,0:T(8,128)S(1)} custom-call(f32[32,32]{1,0:T(8,128)S(1)} %fusion.165), custom_call_target="Cholesky" | custom-call | tf_op jit(solution)/shard_map/jit(cholesky)/cholesky | solution.py:100
  234.6 0.6 compare_reduce_fusion
  235.2 0.7 fusion.158
  235.9 2.4 %custom-call.6 = f32[1,32,32]{1,2,0:T(8,128)S(1)} custom-call(f32[1,32,32]{2,1,0:T(8,128)S(1)} %fusion.158), custom_call_target="InvertDiagBlocksLowerTriangular" | custom-call | tf_op jit(solution)/shard_map/triangular_solve | solution.py:101
  238.5 1.3 fusion.25
  (116 shorter events, 4.0 us)
Async XLA Ops:
  0.0 20.1 %collective-permute-start = (bf16[1,6,128]{2,1,0:T(8,128)(2,1)S(1)}, bf16[1,6,128]{2,1,0:T(8,128)(2,1)S(1)}, u32[]{:S(2)}, u32[]{:S(2)}) collective-permute-start(bf16[1,6,128]{2,1,0:T(8,128)(2,1)S(1)} %broadcast.232), channel_id=1, source_target_pairs={{0,8},{8,16},{16,24},{1,9},{9,17},{17,25},{2,10},{10,18},{18,26},{... | collective-permute-start | bytes 4616 | tf_op jit(solution)/shard_map/ppermute | solution.py:22
  2.4 19.1 %collective-permute-start.1 = (bf16[1,6,128]{2,1,0:T(8,128)(2,1)S(1)}, bf16[1,6,128]{2,1,0:T(8,128)(2,1)S(1)}, u32[]{:S(2)}, u32[]{:S(2)}) collective-permute-start(bf16[1,6,128]{2,1,0:T(8,128)(2,1)S(1)} %broadcast.232), channel_id=1, source_target_pairs={{8,0},{16,8},{24,16},{9,1},{17,9},{25,17},{10,2},{18,10},{26,18},{... | collective-permute-start | bytes 4616 | tf_op jit(solution)/shard_map/ppermute | solution.py:22
  3.7 22.0 %collective-permute-start.2 = (bf16[1,6,128]{2,1,0:T(8,128)(2,1)S(1)}, bf16[1,6,128]{2,1,0:T(8,128)(2,1)S(1)}, u32[]{:S(2)}, u32[]{:S(2)}) collective-permute-start(bf16[1,6,128]{2,1,0:T(8,128)(2,1)S(1)} %broadcast.232), channel_id=1, source_target_pairs={{0,1},{1,2},{2,3},{3,4},{4,5},{5,6},{6,7},{8,9},{9,10},{10,11},{11... | collective-permute-start | bytes 4616 | tf_op jit(solution)/shard_map/ppermute | solution.py:22
  7.9 19.1 %collective-permute-start.3 = (bf16[1,6,128]{2,1,0:T(8,128)(2,1)S(1)}, bf16[1,6,128]{2,1,0:T(8,128)(2,1)S(1)}, u32[]{:S(2)}, u32[]{:S(2)}) collective-permute-start(bf16[1,6,128]{2,1,0:T(8,128)(2,1)S(1)} %broadcast.232), channel_id=1, source_target_pairs={{1,0},{2,1},{3,2},{4,3},{5,4},{6,5},{7,6},{9,8},{10,9},{11,10},{12... | collective-permute-start | bytes 4616 | tf_op jit(solution)/shard_map/ppermute | solution.py:22
  9.2 5.7 %copy-start.7 = (s32[1,1,28,12]{2,1,3,0:T(1,128)S(1)}, s32[1,1,28,12]{2,1,3,0:T(1,128)}, u32[]{:S(2)}) copy-start(s32[1,1,28,12]{2,1,3,0:T(1,128)} %param.7) | copy-start | bytes 4036
  9.2 10.7 %copy-start.6 = (bf16[1,1,32,3584]{3,2,1,0:T(8,128)(2,1)S(1)}, bf16[1,1,32,3584]{3,2,1,0:T(8,128)(2,1)}, u32[]{:S(2)}) copy-start(bf16[1,1,32,3584]{3,2,1,0:T(8,128)(2,1)} %param.5) | copy-start | bytes 688132
  15.3 19.3 %collective-permute-start.4 = (bf16[1,6,128]{2,1,0:T(8,128)(2,1)S(1)}, bf16[1,6,128]{2,1,0:T(8,128)(2,1)S(1)}, u32[]{:S(2)}, u32[]{:S(2)}) collective-permute-start(bf16[1,6,128]{2,1,0:T(8,128)(2,1)S(1)} %get-tuple-element.47), channel_id=1, source_target_pairs={{0,8},{8,16},{16,24},{1,9},{9,17},{17,25},{2,10},{10,18},{18,26},{... | collective-permute-start | bytes 4616 | tf_op jit(solution)/shard_map/ppermute | solution.py:22
  20.1 20.8 %copy-start = (f32[32,28,128]{2,1,0:T(8,128)}, f32[32,28,128]{2,1,0:T(8,128)S(1)}, u32[]{:S(2)}) copy-start(f32[32,28,128]{2,1,0:T(8,128)S(1)} %reshape.152) | copy-start | bytes 1376260
  20.1 14.5 %collective-permute-start.5 = (bf16[1,6,128]{2,1,0:T(8,128)(2,1)S(1)}, bf16[1,6,128]{2,1,0:T(8,128)(2,1)S(1)}, u32[]{:S(2)}, u32[]{:S(2)}) collective-permute-start(bf16[1,6,128]{2,1,0:T(8,128)(2,1)S(1)} %get-tuple-element.46), channel_id=1, source_target_pairs={{8,0},{16,8},{24,16},{9,1},{17,9},{25,17},{10,2},{18,10},{26,18},{... | collective-permute-start | bytes 4616 | tf_op jit(solution)/shard_map/ppermute | solution.py:22
  21.4 13.2 %collective-permute-start.6 = (bf16[1,6,128]{2,1,0:T(8,128)(2,1)S(1)}, bf16[1,6,128]{2,1,0:T(8,128)(2,1)S(1)}, u32[]{:S(2)}, u32[]{:S(2)}) collective-permute-start(bf16[1,6,128]{2,1,0:T(8,128)(2,1)S(1)} %get-tuple-element.45), channel_id=1, source_target_pairs={{0,1},{1,2},{2,3},{3,4},{4,5},{5,6},{6,7},{8,9},{9,10},{10,11},{11... | collective-permute-start | bytes 4616 | tf_op jit(solution)/shard_map/ppermute | solution.py:22
  25.7 8.9 %collective-permute-start.7 = (bf16[1,6,128]{2,1,0:T(8,128)(2,1)S(1)}, bf16[1,6,128]{2,1,0:T(8,128)(2,1)S(1)}, u32[]{:S(2)}, u32[]{:S(2)}) collective-permute-start(bf16[1,6,128]{2,1,0:T(8,128)(2,1)S(1)} %get-tuple-element.44), channel_id=1, source_target_pairs={{1,0},{2,1},{3,2},{4,3},{5,4},{6,5},{7,6},{9,8},{10,9},{11,10},{12... | collective-permute-start | bytes 4616 | tf_op jit(solution)/shard_map/ppermute | solution.py:22
  46.9 16.4 %collective-permute-start.12 = (bf16[32,6,128]{2,0,1:T(8,128)(2,1)S(1)}, bf16[32,6,128]{2,0,1:T(8,128)(2,1)S(1)}, u32[]{:S(2)}, u32[]{:S(2)}) collective-permute-start(bf16[32,6,128]{2,0,1:T(8,128)(2,1)S(1)} %get-tuple-element.31), channel_id=1, source_target_pairs={{0,8},{8,16},{16,24},{1,9},{9,17},{17,25},{2,10},{10,18},{18,26},{... | collective-permute-start | bytes 147464 | tf_op jit(solution)/shard_map/ppermute | solution.py:22
  51.4 13.2 %collective-permute-start.13 = (bf16[32,6,128]{2,0,1:T(8,128)(2,1)S(1)}, bf16[32,6,128]{2,0,1:T(8,128)(2,1)S(1)}, u32[]{:S(2)}, u32[]{:S(2)}) collective-permute-start(bf16[32,6,128]{2,0,1:T(8,128)(2,1)S(1)} %get-tuple-element.30), channel_id=1, source_target_pairs={{8,0},{16,8},{24,16},{9,1},{17,9},{25,17},{10,2},{18,10},{26,18},{... | collective-permute-start | bytes 147464 | tf_op jit(solution)/shard_map/ppermute | solution.py:22
  52.7 17.4 %collective-permute-start.14 = (bf16[32,6,128]{2,0,1:T(8,128)(2,1)S(1)}, bf16[32,6,128]{2,0,1:T(8,128)(2,1)S(1)}, u32[]{:S(2)}, u32[]{:S(2)}) collective-permute-start(bf16[32,6,128]{2,0,1:T(8,128)(2,1)S(1)} %get-tuple-element.29), channel_id=1, source_target_pairs={{0,1},{1,2},{2,3},{3,4},{4,5},{5,6},{6,7},{8,9},{9,10},{10,11},{11... | collective-permute-start | bytes 147464 | tf_op jit(solution)/shard_map/ppermute | solution.py:22
  57.7 13.9 %collective-permute-start.15 = (bf16[32,6,128]{2,0,1:T(8,128)(2,1)S(1)}, bf16[32,6,128]{2,0,1:T(8,128)(2,1)S(1)}, u32[]{:S(2)}, u32[]{:S(2)}) collective-permute-start(bf16[32,6,128]{2,0,1:T(8,128)(2,1)S(1)} %get-tuple-element.28), channel_id=1, source_target_pairs={{1,0},{2,1},{3,2},{4,3},{5,4},{6,5},{7,6},{9,8},{10,9},{11,10},{12... | collective-permute-start | bytes 147464 | tf_op jit(solution)/shard_map/ppermute | solution.py:22
  59.0 12.7 %collective-permute-start.8 = (bf16[32,6,128]{2,0,1:T(8,128)(2,1)S(1)}, bf16[32,6,128]{2,0,1:T(8,128)(2,1)S(1)}, u32[]{:S(2)}, u32[]{:S(2)}) collective-permute-start(bf16[32,6,128]{2,0,1:T(8,128)(2,1)S(1)} %get-tuple-element.43), channel_id=1, source_target_pairs={{0,8},{8,16},{16,24},{1,9},{9,17},{17,25},{2,10},{10,18},{18,26},{... | collective-permute-start | bytes 147464 | tf_op jit(solution)/shard_map/ppermute | solution.py:22
  63.3 8.4 %collective-permute-start.9 = (bf16[32,6,128]{2,0,1:T(8,128)(2,1)S(1)}, bf16[32,6,128]{2,0,1:T(8,128)(2,1)S(1)}, u32[]{:S(2)}, u32[]{:S(2)}) collective-permute-start(bf16[32,6,128]{2,0,1:T(8,128)(2,1)S(1)} %get-tuple-element.42), channel_id=1, source_target_pairs={{8,0},{16,8},{24,16},{9,1},{17,9},{25,17},{10,2},{18,10},{26,18},{... | collective-permute-start | bytes 147464 | tf_op jit(solution)/shard_map/ppermute | solution.py:22
  64.6 7.2 %collective-permute-start.10 = (bf16[32,6,128]{2,0,1:T(8,128)(2,1)S(1)}, bf16[32,6,128]{2,0,1:T(8,128)(2,1)S(1)}, u32[]{:S(2)}, u32[]{:S(2)}) collective-permute-start(bf16[32,6,128]{2,0,1:T(8,128)(2,1)S(1)} %get-tuple-element.41), channel_id=1, source_target_pairs={{0,1},{1,2},{2,3},{3,4},{4,5},{5,6},{6,7},{8,9},{9,10},{10,11},{11... | collective-permute-start | bytes 147464 | tf_op jit(solution)/shard_map/ppermute | solution.py:22
  70.1 6.6 %collective-permute-start.11 = (bf16[32,6,128]{2,0,1:T(8,128)(2,1)S(1)}, bf16[32,6,128]{2,0,1:T(8,128)(2,1)S(1)}, u32[]{:S(2)}, u32[]{:S(2)}) collective-permute-start(bf16[32,6,128]{2,0,1:T(8,128)(2,1)S(1)} %get-tuple-element.40), channel_id=1, source_target_pairs={{1,0},{2,1},{3,2},{4,3},{5,4},{6,5},{7,6},{9,8},{10,9},{11,10},{12... | collective-permute-start | bytes 147464 | tf_op jit(solution)/shard_map/ppermute | solution.py:22
  71.6 5.1 %copy-start.3 = (f32[32,28,128]{2,0,1:T(8,128)}, f32[32,28,128]{2,0,1:T(8,128)S(1)}, u32[]{:S(2)}) copy-start(f32[32,28,128]{2,0,1:T(8,128)S(1)} %constant_dynamic-update-slice_fusion.5) | copy-start | bytes 1376260
  76.7 13.2 %slice-start = ((s8[11010048]{0:T(1024)(128)(4,1)}), s8[2621440]{0:T(1024)(128)(4,1)S(1)}, s32[]{:S(2)}) async-start(s8[11010048]{0:T(1024)(128)(4,1)} %bitcast.279), calls=%async_computation | async-start | bytes 5242880
  79.7 10.2 %slice-start.1 = ((s8[11010048]{0:T(1024)(128)(4,1)}), s8[4194304]{0:T(1024)(128)(4,1)S(1)}, s32[]{:S(2)}) async-start(s8[11010048]{0:T(1024)(128)(4,1)} %bitcast.279), calls=%async_computation.1 | async-start | bytes 8388608
  79.8 10.2 %slice-start.2 = ((s8[11010048]{0:T(1024)(128)(4,1)}), s8[4194304]{0:T(1024)(128)(4,1)S(1)}, s32[]{:S(2)}) async-start(s8[11010048]{0:T(1024)(128)(4,1)} %bitcast.279), calls=%async_computation.2 | async-start | bytes 8388608
  92.5 9.6 %copy-start.2 = (bf16[32,28,128]{2,0,1:T(8,128)(2,1)S(1)}, bf16[32,28,128]{2,0,1:T(8,128)(2,1)}, u32[]{:S(2)}) copy-start(bf16[32,28,128]{2,0,1:T(8,128)(2,1)} %get-tuple-element.13) | copy-start | bytes 688132
  98.4 16.3 %collective-permute-start.20 = (bf16[32,6,128]{2,0,1:T(8,128)(2,1)S(1)}, bf16[32,6,128]{2,0,1:T(8,128)(2,1)S(1)}, u32[]{:S(2)}, u32[]{:S(2)}) collective-permute-start(bf16[32,6,128]{2,0,1:T(8,128)(2,1)S(1)} %get-tuple-element.27), channel_id=1, source_target_pairs={{0,8},{8,16},{16,24},{1,9},{9,17},{17,25},{2,10},{10,18},{18,26},{... | collective-permute-start | bytes 147464 | tf_op jit(solution)/shard_map/ppermute | solution.py:22
  102.1 13.9 %collective-permute-start.21 = (bf16[32,6,128]{2,0,1:T(8,128)(2,1)S(1)}, bf16[32,6,128]{2,0,1:T(8,128)(2,1)S(1)}, u32[]{:S(2)}, u32[]{:S(2)}) collective-permute-start(bf16[32,6,128]{2,0,1:T(8,128)(2,1)S(1)} %get-tuple-element.26), channel_id=1, source_target_pairs={{8,0},{16,8},{24,16},{9,1},{17,9},{25,17},{10,2},{18,10},{26,18},{... | collective-permute-start | bytes 147464 | tf_op jit(solution)/shard_map/ppermute | solution.py:22
  103.4 16.9 %collective-permute-start.22 = (bf16[32,6,128]{2,0,1:T(8,128)(2,1)S(1)}, bf16[32,6,128]{2,0,1:T(8,128)(2,1)S(1)}, u32[]{:S(2)}, u32[]{:S(2)}) collective-permute-start(bf16[32,6,128]{2,0,1:T(8,128)(2,1)S(1)} %get-tuple-element.25), channel_id=1, source_target_pairs={{0,1},{1,2},{2,3},{3,4},{4,5},{5,6},{6,7},{8,9},{9,10},{10,11},{11... | collective-permute-start | bytes 147464 | tf_op jit(solution)/shard_map/ppermute | solution.py:22
  108.0 13.9 %collective-permute-start.23 = (bf16[32,6,128]{2,0,1:T(8,128)(2,1)S(1)}, bf16[32,6,128]{2,0,1:T(8,128)(2,1)S(1)}, u32[]{:S(2)}, u32[]{:S(2)}) collective-permute-start(bf16[32,6,128]{2,0,1:T(8,128)(2,1)S(1)} %get-tuple-element.24), channel_id=1, source_target_pairs={{1,0},{2,1},{3,2},{4,3},{5,4},{6,5},{7,6},{9,8},{10,9},{11,10},{12... | collective-permute-start | bytes 147464 | tf_op jit(solution)/shard_map/ppermute | solution.py:22
  109.3 12.7 %collective-permute-start.16 = (bf16[32,6,128]{2,0,1:T(8,128)(2,1)S(1)}, bf16[32,6,128]{2,0,1:T(8,128)(2,1)S(1)}, u32[]{:S(2)}, u32[]{:S(2)}) collective-permute-start(bf16[32,6,128]{2,0,1:T(8,128)(2,1)S(1)} %get-tuple-element.39), channel_id=1, source_target_pairs={{0,8},{8,16},{16,24},{1,9},{9,17},{17,25},{2,10},{10,18},{18,26},{... | collective-permute-start | bytes 147464 | tf_op jit(solution)/shard_map/ppermute | solution.py:22
  114.7 7.3 %collective-permute-start.17 = (bf16[32,6,128]{2,0,1:T(8,128)(2,1)S(1)}, bf16[32,6,128]{2,0,1:T(8,128)(2,1)S(1)}, u32[]{:S(2)}, u32[]{:S(2)}) collective-permute-start(bf16[32,6,128]{2,0,1:T(8,128)(2,1)S(1)} %get-tuple-element.38), channel_id=1, source_target_pairs={{8,0},{16,8},{24,16},{9,1},{17,9},{25,17},{10,2},{18,10},{26,18},{... | collective-permute-start | bytes 147464 | tf_op jit(solution)/shard_map/ppermute | solution.py:22
  116.0 6.0 %collective-permute-start.18 = (bf16[32,6,128]{2,0,1:T(8,128)(2,1)S(1)}, bf16[32,6,128]{2,0,1:T(8,128)(2,1)S(1)}, u32[]{:S(2)}, u32[]{:S(2)}) collective-permute-start(bf16[32,6,128]{2,0,1:T(8,128)(2,1)S(1)} %get-tuple-element.37), channel_id=1, source_target_pairs={{0,1},{1,2},{2,3},{3,4},{4,5},{5,6},{6,7},{8,9},{9,10},{10,11},{11... | collective-permute-start | bytes 147464 | tf_op jit(solution)/shard_map/ppermute | solution.py:22
  120.3 6.0 %collective-permute-start.19 = (bf16[32,6,128]{2,0,1:T(8,128)(2,1)S(1)}, bf16[32,6,128]{2,0,1:T(8,128)(2,1)S(1)}, u32[]{:S(2)}, u32[]{:S(2)}) collective-permute-start(bf16[32,6,128]{2,0,1:T(8,128)(2,1)S(1)} %get-tuple-element.36), channel_id=1, source_target_pairs={{1,0},{2,1},{3,2},{4,3},{5,4},{6,5},{7,6},{9,8},{10,9},{11,10},{12... | collective-permute-start | bytes 147464 | tf_op jit(solution)/shard_map/ppermute | solution.py:22
  121.9 4.4 %copy-start.4 = (f32[32,28,128]{2,0,1:T(8,128)}, f32[32,28,128]{2,0,1:T(8,128)S(1)}, u32[]{:S(2)}) copy-start(f32[32,28,128]{2,0,1:T(8,128)S(1)} %constant_dynamic-update-slice_fusion.11) | copy-start | bytes 1376260
  126.3 13.3 %slice-start.3 = ((s8[11010048]{0:T(1024)(128)(4,1)}), s8[2621440]{0:T(1024)(128)(4,1)S(1)}, s32[]{:S(2)}) async-start(s8[11010048]{0:T(1024)(128)(4,1)} %bitcast.281), calls=%async_computation.3 | async-start | bytes 5242880
  129.4 10.2 %slice-start.4 = ((s8[11010048]{0:T(1024)(128)(4,1)}), s8[4194304]{0:T(1024)(128)(4,1)S(1)}, s32[]{:S(2)}) async-start(s8[11010048]{0:T(1024)(128)(4,1)} %bitcast.281), calls=%async_computation.4 | async-start | bytes 8388608
  129.4 10.2 %slice-start.5 = ((s8[11010048]{0:T(1024)(128)(4,1)}), s8[4194304]{0:T(1024)(128)(4,1)S(1)}, s32[]{:S(2)}) async-start(s8[11010048]{0:T(1024)(128)(4,1)} %bitcast.281), calls=%async_computation.5 | async-start | bytes 8388608
  142.1 9.4 %copy-start.1 = (bf16[32,28,128]{2,0,1:T(8,128)(2,1)S(1)}, bf16[32,28,128]{2,0,1:T(8,128)(2,1)}, u32[]{:S(2)}) copy-start(bf16[32,28,128]{2,0,1:T(8,128)(2,1)} %get-tuple-element.9) | copy-start | bytes 688132
  148.1 15.0 %collective-permute-start.28 = (bf16[32,6,128]{2,0,1:T(8,128)(2,1)S(1)}, bf16[32,6,128]{2,0,1:T(8,128)(2,1)S(1)}, u32[]{:S(2)}, u32[]{:S(2)}) collective-permute-start(bf16[32,6,128]{2,0,1:T(8,128)(2,1)S(1)} %get-tuple-element.23), channel_id=1, source_target_pairs={{0,8},{8,16},{16,24},{1,9},{9,17},{17,25},{2,10},{10,18},{18,26},{... | collective-permute-start | bytes 147464 | tf_op jit(solution)/shard_map/ppermute | solution.py:22
  151.6 22.6 %collective-permute-start.24 = (bf16[32,6,128]{2,0,1:T(8,128)(2,1)S(1)}, bf16[32,6,128]{2,0,1:T(8,128)(2,1)S(1)}, u32[]{:S(2)}, u32[]{:S(2)}) collective-permute-start(bf16[32,6,128]{2,0,1:T(8,128)(2,1)S(1)} %get-tuple-element.35), channel_id=1, source_target_pairs={{0,8},{8,16},{16,24},{1,9},{9,17},{17,25},{2,10},{10,18},{18,26},{... | collective-permute-start | bytes 147464 | tf_op jit(solution)/shard_map/ppermute | solution.py:22
  156.6 17.5 %collective-permute-start.25 = (bf16[32,6,128]{2,0,1:T(8,128)(2,1)S(1)}, bf16[32,6,128]{2,0,1:T(8,128)(2,1)S(1)}, u32[]{:S(2)}, u32[]{:S(2)}) collective-permute-start(bf16[32,6,128]{2,0,1:T(8,128)(2,1)S(1)} %get-tuple-element.34), channel_id=1, source_target_pairs={{8,0},{16,8},{24,16},{9,1},{17,9},{25,17},{10,2},{18,10},{26,18},{... | collective-permute-start | bytes 147464 | tf_op jit(solution)/shard_map/ppermute | solution.py:22
  157.9 16.3 %collective-permute-start.26 = (bf16[32,6,128]{2,0,1:T(8,128)(2,1)S(1)}, bf16[32,6,128]{2,0,1:T(8,128)(2,1)S(1)}, u32[]{:S(2)}, u32[]{:S(2)}) collective-permute-start(bf16[32,6,128]{2,0,1:T(8,128)(2,1)S(1)} %get-tuple-element.33), channel_id=1, source_target_pairs={{0,1},{1,2},{2,3},{3,4},{4,5},{5,6},{6,7},{8,9},{9,10},{10,11},{11... | collective-permute-start | bytes 147464 | tf_op jit(solution)/shard_map/ppermute | solution.py:22
  161.8 12.4 %collective-permute-start.27 = (bf16[32,6,128]{2,0,1:T(8,128)(2,1)S(1)}, bf16[32,6,128]{2,0,1:T(8,128)(2,1)S(1)}, u32[]{:S(2)}, u32[]{:S(2)}) collective-permute-start(bf16[32,6,128]{2,0,1:T(8,128)(2,1)S(1)} %get-tuple-element.32), channel_id=1, source_target_pairs={{1,0},{2,1},{3,2},{4,3},{5,4},{6,5},{7,6},{9,8},{10,9},{11,10},{12... | collective-permute-start | bytes 147464 | tf_op jit(solution)/shard_map/ppermute | solution.py:22
  163.1 3.5 %collective-permute-start.29 = (bf16[32,6,128]{2,0,1:T(8,128)(2,1)S(1)}, bf16[32,6,128]{2,0,1:T(8,128)(2,1)S(1)}, u32[]{:S(2)}, u32[]{:S(2)}) collective-permute-start(bf16[32,6,128]{2,0,1:T(8,128)(2,1)S(1)} %get-tuple-element.22), channel_id=1, source_target_pairs={{8,0},{16,8},{24,16},{9,1},{17,9},{25,17},{10,2},{18,10},{26,18},{... | collective-permute-start | bytes 147464 | tf_op jit(solution)/shard_map/ppermute | solution.py:22
  166.6 6.0 %collective-permute-start.30 = (bf16[32,6,128]{2,0,1:T(8,128)(2,1)S(1)}, bf16[32,6,128]{2,0,1:T(8,128)(2,1)S(1)}, u32[]{:S(2)}, u32[]{:S(2)}) collective-permute-start(bf16[32,6,128]{2,0,1:T(8,128)(2,1)S(1)} %get-tuple-element.21), channel_id=1, source_target_pairs={{0,1},{1,2},{2,3},{3,4},{4,5},{5,6},{6,7},{8,9},{9,10},{10,11},{11... | collective-permute-start | bytes 147464 | tf_op jit(solution)/shard_map/ppermute | solution.py:22
  172.6 6.3 %collective-permute-start.31 = (bf16[32,6,128]{2,0,1:T(8,128)(2,1)S(1)}, bf16[32,6,128]{2,0,1:T(8,128)(2,1)S(1)}, u32[]{:S(2)}, u32[]{:S(2)}) collective-permute-start(bf16[32,6,128]{2,0,1:T(8,128)(2,1)S(1)} %get-tuple-element.20), channel_id=1, source_target_pairs={{1,0},{2,1},{3,2},{4,3},{5,4},{6,5},{7,6},{9,8},{10,9},{11,10},{12... | collective-permute-start | bytes 147464 | tf_op jit(solution)/shard_map/ppermute | solution.py:22
  174.1 0.8 copy-start.5
where the time goes:
time: 241 us; the launch traced here: 240 us
  starting transfers between devices  89.9 us (37%)
  matrix products  66 us (27%)
  blocking collectives  43.6 us (18%)
  waiting for transfers between devices  14.8 us (6%)
  local copies, waits for them, and re-layouts  12.6 us (5%)
  other arithmetic  11.9 us (5%)
    ppermute x32, starting transfers between devices, from_behind(): return lax.ppermute(shard, axis, pairs)  89.9 us
    psum x1, blocking collectives, body(): factor = jnp.linalg.cholesky(lax.psum(local_gram, ('narrow', 'wide')))  43.6 us
    dot_general x4, matrix products, affinity(): jnp.einsum('bsrc,nbsc->nbr', weight_tile, gathered, preferred_element_typ...  33.4 us
    dot_general x4, matrix products, affinity(): jnp.einsum('bsrc,nbr->bsnc', weight_tile, values, preferred_element_type=...  15.8 us
    ppermute x32, waiting for transfers between devices, from_behind(): return lax.ppermute(shard, axis, pairs)  14.8 us
    dot_general x4, matrix products, affinity(): jnp.einsum('bse,bsnc->nec', selector, transposed, precision=selecting)  14.8 us
    gather x5, local copies, waits for them, and re-layouts, affinity(): gathered = jnp.take(extended_values, target, axis=1)  9.83 us
  transfers between devices with their start and end apart: 32, of which 7 were waited for; matrix products, arithmetic and copies ran while one was open for 7% of the time, Pallas kernels for 0%

commit v1 on v0

v1 whole, which is shorter than its diff:
```python
import functools
import math

import jax
import jax.numpy as jnp
from jax import lax
from jax.experimental import pallas as pl
from jax.experimental.pallas import tpu as pltpu
from jax.sharding import PartitionSpec as P

RIM = 6
RIMS = 4
INNER = 9
LANES = 128
F32 = jnp.float32
BF16 = jnp.bfloat16

lower_edge = 0.3
center = (2.0 + lower_edge) / 2.0
half_width = (2.0 - lower_edge) / 2.0

ROWS_BY_ROWS = (((1,), (1,)), ((), ()))
ROWS_BY_COLS = (((1,), (0,)), ((), ()))


def mm(left, right, dims, precision=None):
    return lax.dot_general(left, right, dims, precision=precision, preferred_element_type=F32)


def beside(parts):
    return parts[0] if len(parts) == 1 else jnp.concatenate(parts, axis=1)


def slot_pairs(first, last):
    return [list(range(s, min(s + 2, last))) for s in range(first, last, 2)]


def column(b):
    return pl.ds(b * LANES, LANES)


def outgoing_ones(pattern_ref, meta_ref, w_hbm, *refs):
    pay_refs, (w_ref, sums, sems) = refs[:4], refs[4:]
    copies = []
    for r in range(RIMS):
        rows = pl.ds(r * RIM, RIM)
        copies.append(pltpu.make_async_copy(w_hbm.at[rows, INNER:], w_ref.at[rows], sems.at[r]))
        copies[-1].start()
    slots = w_ref.shape[1]
    sums[...] = jnp.zeros_like(sums)
    ones = jnp.ones((8, LANES), BF16)
    for r in range(RIMS):
        copies[r].wait()
        for b in range(r * RIM, (r + 1) * RIM):
            part = mm(ones, beside([w_ref[b, s] for s in range(slots)]), ROWS_BY_COLS)
            for s in range(slots):
                q = pattern_ref[b, INNER + s] - pattern_ref.shape[0]
                sums[r, pl.ds(q, 1)] += part[0:1, s * LANES : (s + 1) * LANES]
    for m in range(4):
        pay_refs[m][...] = sums[meta_ref[m]].astype(BF16).astype(F32)


def local_degree(pattern_ref, meta_ref, w_ref, deg_ref, acc):
    blocks, slots = w_ref.shape[:2]
    acc[...] = jnp.zeros_like(acc)
    ones = jnp.ones((8, LANES), BF16)
    for b in range(blocks):
        own = INNER if b < RIMS * RIM else slots
        for group in slot_pairs(0, own):
            part = mm(ones, beside([w_ref[b, s] for s in group]), ROWS_BY_COLS)
            for i, s in enumerate(group):
                acc[pl.ds(pattern_ref[b, s], 1)] += part[0:1, i * LANES : (i + 1) * LANES]
        rows = w_ref[b, 0].astype(F32)
        for s in range(1, own):
            rows = rows + w_ref[b, s].astype(F32)
        if own < slots:
            outer = w_ref[b, own].astype(F32)
            for s in range(own + 1, slots):
                outer = outer + w_ref[b, s].astype(F32)
            rows = rows + meta_ref[8 + b // RIM].astype(F32) * outer
        high = rows.astype(BF16)
        rest = rows - high.astype(F32)
        mid = rest.astype(BF16)
        low = (rest - mid.astype(F32)).astype(BF16)
        wide_ones = jnp.ones((8, 3 * LANES), BF16)
        total = mm(wide_ones, beside([high, mid, low]), ROWS_BY_ROWS)
        deg_ref[pl.ds(b, 1)] = total[0:1]
    deg_ref[...] = deg_ref[...] + acc[...]


def send_out(u_ref, w_ref, pattern_ref, meta_ref, terms, pay_refs):
    blocks, slots = w_ref.shape[:2]
    terms[...] = jnp.zeros_like(terms)
    for b in range(RIMS * RIM):
        part = mm(u_ref[b], beside([w_ref[b, s] for s in range(INNER, slots)]), ROWS_BY_COLS)
        base = (b // RIM) * RIM - blocks
        for s in range(INNER, slots):
            i = s - INNER
            terms[base + pattern_ref[b, s]] += part[:, i * LANES : (i + 1) * LANES]
    for m in range(4):
        first = meta_ref[m] * RIM
        pay_refs[m][0:RIM] = u_ref[pl.ds(first, RIM)]
        pay_refs[m][RIM:] = terms[pl.ds(first, RIM)].astype(BF16)


def first_scaled(pattern_ref, meta_ref, w_ref, deg_ref, x_ref, *refs):
    in_refs, (inv_ref, u_ref), pay_refs, (rims, terms) = refs[:4], refs[4:6], refs[6:10], refs[10:]
    blocks = w_ref.shape[0]
    for m in range(4):
        rims[meta_ref[m]] = in_refs[m][...] * meta_ref[4 + m].astype(F32)
    for b in range(blocks):
        degree = deg_ref[b : b + 1]
        if b < RIMS * RIM:
            degree = degree + rims[b // RIM, b % RIM : b % RIM + 1]
        inv = 1.0 / jnp.sqrt(0.5 * degree)
        inv_ref[b : b + 1] = inv
        u_ref[b] = (inv * x_ref[:, column(b)].astype(F32)).astype(BF16)
    send_out(u_ref, w_ref, pattern_ref, meta_ref, terms, pay_refs)


def own_terms(pattern_ref, meta_ref, w_ref, u_ref, acc_ref, forward):
    blocks, slots = w_ref.shape[:2]
    acc_ref[...] = jnp.zeros_like(acc_ref)
    for b in range(blocks):
        total = None
        own = INNER if b < RIMS * RIM else slots
        for group in slot_pairs(0, own):
            w = beside([w_ref[b, s] for s in group])
            part = mm(u_ref[b], w, ROWS_BY_COLS)
            for i, s in enumerate(group):
                acc_ref[pattern_ref[b, s]] += part[:, i * LANES : (i + 1) * LANES]
            ahead = mm(beside([u_ref[pattern_ref[b, s]] for s in group]), w, ROWS_BY_ROWS)
            total = ahead if total is None else total + ahead
        forward[b] = total
    acc_ref[...] += forward[...]


def combine(step, pattern_ref, meta_ref, w_ref, inv_ref, acc_ref, in_refs, y_ref, before_ref, next_ref, ext, u_ref):
    blocks, slots = w_ref.shape[:2]
    for m in range(4):
        live = meta_ref[4 + m].astype(BF16)
        first = meta_ref[m] * 2 * RIM
        ext[pl.ds(first, 2 * RIM)] = in_refs[m][...] * live
    for b in range(blocks):
        total = acc_ref[b]
        if b < RIMS * RIM:
            base = (b // RIM) * 2 * RIM
            ahead = beside([ext[base + pattern_ref[b, s] - blocks] for s in range(INNER, slots)])
            total = total + mm(ahead, beside([w_ref[b, s] for s in range(INNER, slots)]), ROWS_BY_ROWS)
            total = total + ext[base + RIM + b % RIM].astype(F32)
        inv = inv_ref[b : b + 1]
        y = y_ref[:, column(b)].astype(F32)
        lap = y - inv * (0.5 * total)
        new = (lap - center * y) / half_width
        if step > 0:
            new = 2.0 * new - before_ref[:, column(b)].astype(F32)
        next_ref[:, column(b)] = new
        if u_ref is not None:
            u_ref[b] = (inv * new).astype(BF16)


def advance(step, pattern_ref, meta_ref, w_ref, inv_ref, acc_ref, *refs):
    in_refs, (y_ref, before_ref, next_ref, u_ref) = refs[:4], refs[4:8]
    pay_refs, (ext, terms) = refs[8:12], refs[12:]
    combine(step, pattern_ref, meta_ref, w_ref, inv_ref, acc_ref, in_refs, y_ref, before_ref, next_ref, ext, u_ref)
    send_out(u_ref, w_ref, pattern_ref, meta_ref, terms, pay_refs)


def finish(pattern_ref, meta_ref, w_ref, inv_ref, acc_ref, *refs):
    in_refs, (y_ref, before_ref, next_ref, gram_ref, ext) = refs[:4], refs[4:]
    combine(2, pattern_ref, meta_ref, w_ref, inv_ref, acc_ref, in_refs, y_ref, before_ref, next_ref, ext, None)
    y = next_ref[...]
    gram = mm(y, y, ROWS_BY_ROWS, lax.Precision.HIGHEST)
    packed = beside([gram[8 * i : 8 * i + 8] for i in range(gram.shape[0] // 8)])
    gram_ref[...] = jnp.broadcast_to(packed[None], gram_ref.shape)


def orthonormal(scale, grams_ref, y_ref, out_ref):
    packed = jnp.sum(grams_ref[...], axis=0)
    n = y_ref.shape[0]
    gram = jnp.concatenate([packed[:, n * i : n * (i + 1)] for i in range(n // 8)], axis=0)
    row_id = lax.broadcasted_iota(jnp.int32, (n, n), 0)
    col_id = lax.broadcasted_iota(jnp.int32, (n, n), 1)
    eye = (row_id == col_id).astype(F32)
    both = jnp.concatenate([gram, eye], axis=1)
    rows = lax.broadcasted_iota(jnp.int32, (n, 2 * n), 0)
    roots = jnp.zeros((n, 1), F32)
    row_of = lax.broadcasted_iota(jnp.int32, (n, 1), 0)
    for k in range(n):
        pivot_row = both[k : k + 1]
        pivot = both[k : k + 1, k : k + 1]
        roots = jnp.where(row_of == k, pivot, roots)
        if k < n - 1:
            factor = jnp.where(row_of > k, both[:, k : k + 1] / pivot, 0.0)
            both = both - factor * pivot_row
    inverse = both[:, n:] * (scale / jnp.sqrt(roots))
    out_ref[...] = mm(inverse, y_ref[...], ROWS_BY_COLS, lax.Precision.HIGHEST)


def in_vmem(x):
    return pltpu.with_memory_space_constraint(x, pltpu.VMEM)


def kernel_call(body, name, ins, outs, scratch=(), flops=0, moved=0):
    specs, args = [], []
    for kind, x in ins:
        if kind == "hbm":
            specs.append(pl.BlockSpec(memory_space=pl.ANY))
        elif kind == "smem":
            specs.append(pl.BlockSpec(memory_space=pltpu.SMEM))
        else:
            specs.append(pl.BlockSpec(memory_space=pltpu.VMEM))
            if kind == "held":
                x = in_vmem(x)
        args.append(x)
    return pl.pallas_call(
        body,
        name=name,
        out_shape=[jax.ShapeDtypeStruct(s, d) for s, d in outs],
        in_specs=specs,
        out_specs=[pl.BlockSpec(memory_space=pltpu.VMEM)] * len(outs),
        scratch_shapes=list(scratch),
        compiler_params=pltpu.CompilerParams(vmem_limit_bytes=16 << 20),
        cost_estimate=pl.CostEstimate(flops=flops, bytes_accessed=moved, transcendentals=0),
    )(*args)


def matchings(axis):
    peers = lax.axis_size(axis)
    pairs = []
    for first in (0, 1):
        swaps = []
        for i in range(first, peers, 2):
            j = (i + 1) % peers
            swaps += [(i, j), (j, i)]
        pairs.append(swaps)
    return pairs


def exchange(payloads):
    got = [None] * 4
    for a, axis in ((1, "wide"), (0, "narrow")):
        pairs = matchings(axis)
        for m in (1, 0):
            got[2 * a + m] = lax.ppermute(payloads[2 * a + m], axis, pairs[m])
    return got


def placement():
    sends, live, by_rim = [], [], []
    for a, axis in enumerate(("narrow", "wide")):
        place = lax.axis_index(axis)
        last = lax.axis_size(axis) - 1
        for m in (0, 1):
            after = (place + m) % 2 == 0
            sends.append(2 * a + after.astype(jnp.int32))
            live.append(jnp.where(after, place < last, place > 0).astype(jnp.int32))
        by_rim += [(place > 0).astype(jnp.int32), (place < last).astype(jnp.int32)]
    return jnp.stack(sends + live + by_rim)


def body(start_block, weights, pattern):
    x = start_block[0, 0]
    w = weights[0, 0]
    slots_of = pattern[0, 0]
    meta = placement()
    vecs, docs = x.shape
    blocks, slots = w.shape[:2]
    rows = RIMS * RIM
    ids = [("smem", slots_of), ("smem", meta)]
    tile = ((blocks, vecs, LANES), F32)
    scaled = ((blocks, vecs, LANES), BF16)
    full = ((vecs, docs), F32)
    payload = [((2 * RIM, vecs, LANES), BF16)] * 4
    held = ids + [("held", w)]
    per_block = 2 * LANES * LANES

    pays = kernel_call(
        outgoing_ones, "outgoing_ones", ids + [("hbm", w)], [((8, LANES), F32)] * 4,
        [pltpu.VMEM((rows, slots - INNER, LANES, LANES), BF16), pltpu.VMEM((RIMS, 8, LANES), F32),
         pltpu.SemaphoreType.DMA((RIMS,))],
        flops=rows * 3 * per_block * 32, moved=1 << 20,
    )
    (degree,) = kernel_call(
        local_degree, "local_degree", held, [((blocks, LANES), F32)], [pltpu.VMEM((blocks, LANES), F32)],
        flops=blocks * slots * per_block * 32, moved=8 << 20,
    )
    got = exchange(pays)
    inv, u, *pays = kernel_call(
        first_scaled, "first_scaled",
        held + [("vmem", degree), ("vmem", x)] + [("vmem", g) for g in got],
        [((blocks, LANES), F32), scaled] + payload,
        [pltpu.VMEM((RIMS, 8, LANES), F32), pltpu.VMEM((rows, vecs, LANES), F32)],
        flops=rows * 3 * per_block * 32, moved=1 << 20,
    )
    before, y = x, x
    for step in range(3):
        (acc,) = kernel_call(
            own_terms, "own_terms", held + [("vmem", u)], [tile],
            [pltpu.VMEM(*tile)],
            flops=2 * blocks * slots * per_block * vecs, moved=8 << 20,
        )
        got = exchange(pays)
        common = held + [("vmem", inv), ("vmem", acc)] + [("vmem", g) for g in got] + [("vmem", y), ("vmem", before)]
        ext = pltpu.VMEM((2 * rows, vecs, LANES), BF16)
        if step < 2:
            new, u, *pays = kernel_call(
                functools.partial(advance, step), "advance", common, [full, scaled] + payload,
                [ext, pltpu.VMEM((rows, vecs, LANES), F32)],
                flops=2 * rows * 3 * per_block * 32, moved=1 << 20,
            )
        else:
            peers = lax.axis_size("narrow") * lax.axis_size("wide")
            new, grams = kernel_call(
                finish, "finish", common, [full, ((peers, 8, LANES), F32)], [ext],
                flops=rows * 3 * per_block * 32, moved=1 << 20,
            )
        before, y = y, new
    grams = lax.all_to_all(grams, ("narrow", "wide"), 0, 0)
    (out,) = kernel_call(
        functools.partial(orthonormal, math.sqrt(peers * docs)), "orthonormal",
        [("vmem", grams), ("vmem", y)], [full],
    )
    return out[None, None]


def solution(mesh):
    placed = (
        P("narrow", "wide", None, None),
        P("narrow", "wide", None, None, None, None),
        P("narrow", "wide", None, None),
    )
    return jax.shard_map(
        body, mesh=mesh, in_specs=placed, out_specs=P("narrow", "wide", None, None), check_vma=False
    )
```

time: 241 us -> 68.8 us (0.29)
  starting transfers between devices: 89.9 us -> 19.3 us
  matrix products: 66 us -> 0 us
  Pallas kernels: 0 us -> 32.7 us
  blocking collectives: 43.6 us -> 11.1 us
  waiting for transfers between devices: 14.8 us -> 0.18 us
  other arithmetic: 11.9 us -> 0 us
  local copies, waits for them, and re-layouts: 12.6 us -> 5 us
    ppermute x32 -> x16, starting transfers between devices: 89.9 us -> 19.3 us  [exchange(): got[2 * a + m] = lax.ppermute(payloads[2 * a + m], axis, pairs[m])]
    dot_general x14 -> x0, matrix products: 65.8 us -> none  [the longest x4 33.4 us: affinity(): jnp.einsum('bsrc,nbsc->nbr', weight_tile, gathered, preferred_element_typ...]
    psum x1 -> x0, blocking collectives: 43.6 us -> none  [body(): factor = jnp.linalg.cholesky(lax.psum(local_gram, ('narrow', 'wide')))]
    pallas_call x0 -> x10, Pallas kernels: none -> 32.7 us  [kernel_call(): pl.pallas_call(body, name=name, out_shape=[jax.ShapeDtypeStruct(s, d) for...]
    ppermute x32 -> x16, waiting for transfers between devices: 14.8 us -> 0.18 us  [exchange(): got[2 * a + m] = lax.ppermute(payloads[2 * a + m], axis, pairs[m])]
    all_to_all x0 -> x1, blocking collectives: none -> 11.1 us  [body(): grams = lax.all_to_all(grams, ('narrow', 'wide'), 0, 0)]
    another operation x8 -> x0, other arithmetic: 9.99 us -> none  [the longest x3 3.6 us: body(): factor = jnp.linalg.cholesky(lax.psum(local_gram, ('narrow', 'wide')))]
    gather x5 -> x0, local copies, waits for them, and re-layouts: 9.83 us -> none  [affinity(): gathered = jnp.take(extended_values, target, axis=1)]
  transfers between devices with their start and end apart: 32 -> 16, of which waited for: 7 -> 1; matrix products, arithmetic and copies ran while one was open for 7% -> 0% of each run, Pallas kernels for 0% -> 26%
where the time goes in v1:
time: 68.8 us; the launch traced here: 68.5 us
  Pallas kernels  32.7 us (48%)
  starting transfers between devices  19.3 us (28%)
  blocking collectives  11.1 us (16%)
  local copies, waits for them, and re-layouts  5 us (7%)
    pallas_call x10, Pallas kernels, kernel_call(): pl.pallas_call(body, name=name, out_shape=[jax.ShapeDtypeStruct(s, d) for...  32.7 us
    ppermute x16, starting transfers between devices, exchange(): got[2 * a + m] = lax.ppermute(payloads[2 * a + m], axis, pairs[m])  19.3 us
    all_to_all x1, blocking collectives, body(): grams = lax.all_to_all(grams, ('narrow', 'wide'), 0, 0)  11.1 us
    unnamed x5, local copies, waits for them, and re-layouts  4.91 us
  transfers between devices with their start and end apart: 16, of which 1 were waited for; matrix products, arithmetic and copies ran while one was open for 0% of the time, Pallas kernels for 26%

profile of v1, /device:TPU:0, one launch (start us, length us, event | category | flops | bytes accessed | tf_op | source)
XLA Modules:
  0.0 68.5 jit_solution(4918383810024222888)
XLA Ops:
  0.0 0.8 %copy.4 = s32[1,1,28,12]{3,2,1,0:T(8,128)S(1)} copy(s32[1,1,28,12]{2,1,3,0:T(1,128)} %param.5) | data formatting | bytes 2688 | tf_op args[2]
  0.8 0.1 stack.91.meta_ref
  0.9 0.0 copy-start
  0.9 4.1 %copy-done = bf16[1,1,28,12,128,128]{5,4,3,2,1,0:T(8,128)(2,1)S(1)} copy-done((bf16[1,1,28,12,128,128]{5,4,3,2,1,0:T(8,128)(2,1)S(1)}, bf16[1,1,28,12,128,128]{5,4,3,2,1,0:T(8,128)(2,1)}, u32[]{:S(2)}) %copy-start) | copy-done | bytes 11010072
  5.0 0.0 copy-start.1
  5.0 1.9 %outgoing_ones.1 = (f32[8,128]{1,0:T(8,128)S(1)}, f32[8,128]{1,0:T(8,128)S(1)}, f32[8,128]{1,0:T(8,128)S(1)}, f32[8,128]{1,0:T(8,128)S(1)}) custom-call(s32[28,12]{1,0:T(8,128)S(1)} %bitcast.29, s32[12]{0:T(128)S(1)} %stack.91.meta_ref, bf16[28,12,128,128]{3,2,1,0:T(8,128)(2,1)S(1)} %bitcast.16), custom_call_target="tpu_custom_call" | custom-call | flops 75497472 | bytes 1048576 | tf_op jit(solution)/shard_map/outgoing_ones/pallas_call | solution.py:216
  6.9 0.5 collective-permute-start
  7.4 2.6 %collective-permute-start.1 = (f32[8,128]{1,0:T(8,128)S(1)}, f32[8,128]{1,0:T(8,128)S(1)}, u32[]{:S(2)}, u32[]{:S(2)}) collective-permute-start(f32[8,128]{1,0:T(8,128)S(1)} %get-tuple-element.30), channel_id=1, source_target_pairs={{8,16},{16,8},{24,0},{0,24},{9,17},{17,9},{25,1},{1,25},{10,18},{1... | collective-permute-start | bytes 12296 | tf_op jit(solution)/shard_map/ppermute | solution.py:245
  10.0 1.5 %collective-permute-start.2 = (f32[8,128]{1,0:T(8,128)S(1)}, f32[8,128]{1,0:T(8,128)S(1)}, u32[]{:S(2)}, u32[]{:S(2)}) collective-permute-start(f32[8,128]{1,0:T(8,128)S(1)} %get-tuple-element.31), channel_id=1, source_target_pairs={{0,1},{1,0},{2,3},{3,2},{4,5},{5,4},{6,7},{7,6},{8,9},{9,8},{10,11... | collective-permute-start | bytes 12296 | tf_op jit(solution)/shard_map/ppermute | solution.py:245
  11.6 3.5 %collective-permute-start.3 = (f32[8,128]{1,0:T(8,128)S(1)}, f32[8,128]{1,0:T(8,128)S(1)}, u32[]{:S(2)}, u32[]{:S(2)}) collective-permute-start(f32[8,128]{1,0:T(8,128)S(1)} %get-tuple-element.32), channel_id=1, source_target_pairs={{1,2},{2,1},{3,4},{4,3},{5,6},{6,5},{7,0},{0,7},{9,10},{10,9},{11,... | collective-permute-start | bytes 12296 | tf_op jit(solution)/shard_map/ppermute | solution.py:245
  15.1 3.2 %local_degree.1.deg_ref = f32[28,128]{1,0:T(8,128)S(1)} custom-call(s32[28,12]{1,0:T(8,128)S(1)} %bitcast.30, s32[12]{0:T(128)S(1)} %stack.91.meta_ref, bf16[28,12,128,128]{3,2,1,0:T(8,128)(2,1)S(1)} %bitcast.17), custom_call_target="tpu_custom_call" | custom-call | flops 352321536 | bytes 8388608 | tf_op jit(solution)/shard_map/local_degree/pallas_call | solution.py:216
  18.4 0.0 collective-permute-done.refs_0_
  18.4 0.0 collective-permute-done.1.refs_1_
  18.4 0.0 collective-permute-done.2.refs_2_
  18.4 0.0 collective-permute-done.3.refs_3_
  18.4 0.0 copy-done.1
  18.4 1.4 %first_scaled.1 = (f32[28,128]{1,0:T(8,128)S(1)}, bf16[28,32,128]{2,1,0:T(8,128)(2,1)S(1)}, bf16[12,32,128]{2,1,0:T(8,128)(2,1)S(1)}, bf16[12,32,128]{2,1,0:T(8,...) custom-call(s32[28,12]{1,0:T(8,128)S(1)} %bitcast.31, s32[12]{0:T(128)S(1)} %stack.91.meta_ref, ...), custom_call_target="tpu_custom_call" | custom-call | flops 75497472 | bytes 1048576 | tf_op jit(solution)/shard_map/first_scaled/pallas_call | solution.py:216
  19.9 0.1 collective-permute-start.4
  20.0 0.6 collective-permute-start.5
  20.6 0.0 collective-permute-start.6
  20.6 3.0 %collective-permute-start.7 = (bf16[12,32,128]{2,1,0:T(8,128)(2,1)S(1)}, bf16[12,32,128]{2,1,0:T(8,128)(2,1)S(1)}, u32[]{:S(2)}, u32[]{:S(2)}) collective-permute-start(bf16[12,32,128]{2,1,0:T(8,128)(2,1)S(1)} %get-tuple-element.38), channel_id=1, source_target_pairs={{1,2},{2,1},{3,4},{4,3},{5,6},{6,5},{7,0},{0,7},{9,10},{10,9},{11,... | collective-permute-start | bytes 294920 | tf_op jit(solution)/shard_map/ppermute | solution.py:245
  23.6 4.9 %own_terms.3.acc_ref = f32[28,32,128]{2,1,0:T(8,128)S(1)} custom-call(s32[28,12]{1,0:T(8,128)S(1)} %bitcast.32, s32[12]{0:T(128)S(1)} %stack.91.meta_ref, bf16[28,12,128,128]{3,2,1,0:T(8,128)(2,1)S(1)} %bitcast.19, bf16[28,32,128]{2,1,0:T(8,128)(2,1)S(1)} %get-tuple-element.34.u_ref), custom_call_target="tpu_custom_call" | custom-call | flops 704643072 | bytes 8388608 | tf_op jit(solution)/shard_map/own_terms/pallas_call | solution.py:216
  28.5 0.0 collective-permute-done.4.refs_0_
  28.5 0.0 collective-permute-done.5.refs_1_
  28.5 0.0 collective-permute-done.6.refs_2_
  28.5 0.0 collective-permute-done.7.refs_3_
  28.6 2.3 %advance.2 = (f32[32,3584]{1,0:T(8,128)S(1)}, bf16[28,32,128]{2,1,0:T(8,128)(2,1)S(1)}, bf16[12,32,128]{2,1,0:T(8,128)(2,1)S(1)}, bf16[12,32,128]{2,1,0:T(8,128)...) custom-call(s32[28,12]{1,0:T(8,128)S(1)} %bitcast.33, s32[12]{0:T(128)S(1)} %stack.91.meta_ref, ...), custom_call_target="tpu_custom_call" | custom-call | flops 150994944 | bytes 1048576 | tf_op jit(solution)/shard_map/advance/pallas_call | solution.py:216
  30.8 0.1 collective-permute-start.8
  30.9 1.6 %collective-permute-start.9 = (bf16[12,32,128]{2,1,0:T(8,128)(2,1)S(1)}, bf16[12,32,128]{2,1,0:T(8,128)(2,1)S(1)}, u32[]{:S(2)}, u32[]{:S(2)}) collective-permute-start(bf16[12,32,128]{2,1,0:T(8,128)(2,1)S(1)} %get-tuple-element.41), channel_id=1, source_target_pairs={{8,16},{16,8},{24,0},{0,24},{9,17},{17,9},{25,1},{1,25},{10,18},{1... | collective-permute-start | bytes 294920 | tf_op jit(solution)/shard_map/ppermute | solution.py:245
  32.5 0.0 collective-permute-start.10
  32.5 2.6 %collective-permute-start.11 = (bf16[12,32,128]{2,1,0:T(8,128)(2,1)S(1)}, bf16[12,32,128]{2,1,0:T(8,128)(2,1)S(1)}, u32[]{:S(2)}, u32[]{:S(2)}) collective-permute-start(bf16[12,32,128]{2,1,0:T(8,128)(2,1)S(1)} %get-tuple-element.43), channel_id=1, source_target_pairs={{1,2},{2,1},{3,4},{4,3},{5,6},{6,5},{7,0},{0,7},{9,10},{10,9},{11,... | collective-permute-start | bytes 294920 | tf_op jit(solution)/shard_map/ppermute | solution.py:245
  35.1 5.1 %own_terms.4.acc_ref = f32[28,32,128]{2,1,0:T(8,128)S(1)} custom-call(s32[28,12]{1,0:T(8,128)S(1)} %bitcast.34, s32[12]{0:T(128)S(1)} %stack.91.meta_ref, bf16[28,12,128,128]{3,2,1,0:T(8,128)(2,1)S(1)} %bitcast.21, bf16[28,32,128]{2,1,0:T(8,128)(2,1)S(1)} %get-tuple-element.39.u_ref), custom_call_target="tpu_custom_call" | custom-call | flops 704643072 | bytes 8388608 | tf_op jit(solution)/shard_map/own_terms/pallas_call | solution.py:216
  40.2 0.0 collective-permute-done.8.refs_0_
  40.2 0.0 collective-permute-done.9.refs_1_
  40.2 0.0 collective-permute-done.10.refs_2_
  40.2 0.0 collective-permute-done.11.refs_3_
  40.2 2.3 %advance.3 = (f32[32,3584]{1,0:T(8,128)S(1)}, bf16[28,32,128]{2,1,0:T(8,128)(2,1)S(1)}, bf16[12,32,128]{2,1,0:T(8,128)(2,1)S(1)}, bf16[12,32,128]{2,1,0:T(8,128)...) custom-call(s32[28,12]{1,0:T(8,128)S(1)} %bitcast.35, s32[12]{0:T(128)S(1)} %stack.91.meta_ref, ...), custom_call_target="tpu_custom_call" | custom-call | flops 150994944 | bytes 1048576 | tf_op jit(solution)/shard_map/advance/pallas_call | solution.py:216
  42.5 0.1 collective-permute-start.12
  42.6 0.6 collective-permute-start.13
  43.3 0.0 collective-permute-start.14
  43.3 2.4 %collective-permute-start.15 = (bf16[12,32,128]{2,1,0:T(8,128)(2,1)S(1)}, bf16[12,32,128]{2,1,0:T(8,128)(2,1)S(1)}, u32[]{:S(2)}, u32[]{:S(2)}) collective-permute-start(bf16[12,32,128]{2,1,0:T(8,128)(2,1)S(1)} %get-tuple-element.49), channel_id=1, source_target_pairs={{1,2},{2,1},{3,4},{4,3},{5,6},{6,5},{7,0},{0,7},{9,10},{10,9},{11,... | collective-permute-start | bytes 294920 | tf_op jit(solution)/shard_map/ppermute | solution.py:245
  45.7 4.9 %own_terms.5.acc_ref = f32[28,32,128]{2,1,0:T(8,128)S(1)} custom-call(s32[28,12]{1,0:T(8,128)S(1)} %bitcast.36, s32[12]{0:T(128)S(1)} %stack.91.meta_ref, bf16[28,12,128,128]{3,2,1,0:T(8,128)(2,1)S(1)} %bitcast.23, bf16[28,32,128]{2,1,0:T(8,128)(2,1)S(1)} %get-tuple-element.45.u_ref), custom_call_target="tpu_custom_call" | custom-call | flops 704643072 | bytes 8388608 | tf_op jit(solution)/shard_map/own_terms/pallas_call | solution.py:216
  50.6 0.0 collective-permute-done.12.refs_0_
  50.6 0.0 collective-permute-done.13.refs_1_
  50.6 0.0 collective-permute-done.14.refs_2_
  50.6 0.1 collective-permute-done.15.refs_3_
  50.7 2.6 %finish.1 = (f32[32,3584]{1,0:T(8,128)S(1)}, f32[32,8,128]{2,1,0:T(8,128)S(1)}) custom-call(s32[28,12]{1,0:T(8,128)S(1)} %bitcast.37, s32[12]{0:T(128)S(1)} %stack.91.meta_ref, bf16[28,12,128,128]{3,2,1,0:T(8,128)(2,1)S(1)} %bitcast.24, f32[28,128]{1,0:T(8,128)S(1)} %get-tuple-element.33.inv_ref, f32[28,32,128]{2,1,0:T(8,128)S(1)} %own_terms.5.acc_ref, ...), custom_call_target="tpu_custom_call" | custom-call | flops 75497472 | bytes 1048576 | tf_op jit(solution)/shard_map/finish/pallas_call | solution.py:216
  53.3 11.1 %all_to_all.5.grams_ref = f32[32,8,128]{2,1,0:T(8,128)S(1)} all-to-all(f32[32,8,128]{2,1,0:T(8,128)S(1)} %get-tuple-element.51), channel_id=1, replica_groups=mesh['narrow'=4,'wide'=8] {'narrow','wide'}, dimensions={0} | all-to-all | bytes 262144 | tf_op jit(solution)/shard_map/all_to_all | solution.py:319
  64.4 4.1 %orthonormal.1 = f32[32,3584]{1,0:T(8,128)} custom-call(f32[32,8,128]{2,1,0:T(8,128)S(1)} %all_to_all.5.grams_ref, f32[32,3584]{1,0:T(8,128)S(1)} %get-tuple-element.52.y_ref), custom_call_target="tpu_custom_call" | custom-call | tf_op jit(solution)/shard_map/orthonormal/pallas_call | solution.py:216
Async XLA Ops:
  0.9 4.1 %copy-start = (bf16[1,1,28,12,128,128]{5,4,3,2,1,0:T(8,128)(2,1)S(1)}, bf16[1,1,28,12,128,128]{5,4,3,2,1,0:T(8,128)(2,1)}, u32[]{:S(2)}) copy-start(bf16[1,1,28,12,128,128]{5,4,3,2,1,0:T(8,128)(2,1)} %param.4) | copy-start | bytes 33030148
  5.0 13.4 %copy-start.1 = (bf16[1,1,32,3584]{3,2,1,0:T(8,128)(2,1)S(1)}, bf16[1,1,32,3584]{3,2,1,0:T(8,128)(2,1)}, u32[]{:S(2)}) copy-start(bf16[1,1,32,3584]{3,2,1,0:T(8,128)(2,1)} %param.3) | copy-start | bytes 688132
  6.9 11.5 %collective-permute-start = (f32[8,128]{1,0:T(8,128)S(1)}, f32[8,128]{1,0:T(8,128)S(1)}, u32[]{:S(2)}, u32[]{:S(2)}) collective-permute-start(f32[8,128]{1,0:T(8,128)S(1)} %get-tuple-element.29), channel_id=1, source_target_pairs={{0,8},{8,0},{16,24},{24,16},{1,9},{9,1},{17,25},{25,17},{2,10},{10... | collective-permute-start | bytes 12296 | tf_op jit(solution)/shard_map/ppermute | solution.py:245
  7.4 10.9 %collective-permute-start.1 = (f32[8,128]{1,0:T(8,128)S(1)}, f32[8,128]{1,0:T(8,128)S(1)}, u32[]{:S(2)}, u32[]{:S(2)}) collective-permute-start(f32[8,128]{1,0:T(8,128)S(1)} %get-tuple-element.30), channel_id=1, source_target_pairs={{8,16},{16,8},{24,0},{0,24},{9,17},{17,9},{25,1},{1,25},{10,18},{1... | collective-permute-start | bytes 12296 | tf_op jit(solution)/shard_map/ppermute | solution.py:245
  10.0 8.3 %collective-permute-start.2 = (f32[8,128]{1,0:T(8,128)S(1)}, f32[8,128]{1,0:T(8,128)S(1)}, u32[]{:S(2)}, u32[]{:S(2)}) collective-permute-start(f32[8,128]{1,0:T(8,128)S(1)} %get-tuple-element.31), channel_id=1, source_target_pairs={{0,1},{1,0},{2,3},{3,2},{4,5},{5,4},{6,7},{7,6},{8,9},{9,8},{10,11... | collective-permute-start | bytes 12296 | tf_op jit(solution)/shard_map/ppermute | solution.py:245
  11.6 6.8 %collective-permute-start.3 = (f32[8,128]{1,0:T(8,128)S(1)}, f32[8,128]{1,0:T(8,128)S(1)}, u32[]{:S(2)}, u32[]{:S(2)}) collective-permute-start(f32[8,128]{1,0:T(8,128)S(1)} %get-tuple-element.32), channel_id=1, source_target_pairs={{1,2},{2,1},{3,4},{4,3},{5,6},{6,5},{7,0},{0,7},{9,10},{10,9},{11,... | collective-permute-start | bytes 12296 | tf_op jit(solution)/shard_map/ppermute | solution.py:245
  19.9 8.6 %collective-permute-start.4 = (bf16[12,32,128]{2,1,0:T(8,128)(2,1)S(1)}, bf16[12,32,128]{2,1,0:T(8,128)(2,1)S(1)}, u32[]{:S(2)}, u32[]{:S(2)}) collective-permute-start(bf16[12,32,128]{2,1,0:T(8,128)(2,1)S(1)} %get-tuple-element.35), channel_id=1, source_target_pairs={{0,8},{8,0},{16,24},{24,16},{1,9},{9,1},{17,25},{25,17},{2,10},{10... | collective-permute-start | bytes 294920 | tf_op jit(solution)/shard_map/ppermute | solution.py:245
  20.0 8.6 %collective-permute-start.5 = (bf16[12,32,128]{2,1,0:T(8,128)(2,1)S(1)}, bf16[12,32,128]{2,1,0:T(8,128)(2,1)S(1)}, u32[]{:S(2)}, u32[]{:S(2)}) collective-permute-start(bf16[12,32,128]{2,1,0:T(8,128)(2,1)S(1)} %get-tuple-element.36), channel_id=1, source_target_pairs={{8,16},{16,8},{24,0},{0,24},{9,17},{17,9},{25,1},{1,25},{10,18},{1... | collective-permute-start | bytes 294920 | tf_op jit(solution)/shard_map/ppermute | solution.py:245
  20.6 7.9 %collective-permute-start.6 = (bf16[12,32,128]{2,1,0:T(8,128)(2,1)S(1)}, bf16[12,32,128]{2,1,0:T(8,128)(2,1)S(1)}, u32[]{:S(2)}, u32[]{:S(2)}) collective-permute-start(bf16[12,32,128]{2,1,0:T(8,128)(2,1)S(1)} %get-tuple-element.37), channel_id=1, source_target_pairs={{0,1},{1,0},{2,3},{3,2},{4,5},{5,4},{6,7},{7,6},{8,9},{9,8},{10,11... | collective-permute-start | bytes 294920 | tf_op jit(solution)/shard_map/ppermute | solution.py:245
  20.6 7.9 %collective-permute-start.7 = (bf16[12,32,128]{2,1,0:T(8,128)(2,1)S(1)}, bf16[12,32,128]{2,1,0:T(8,128)(2,1)S(1)}, u32[]{:S(2)}, u32[]{:S(2)}) collective-permute-start(bf16[12,32,128]{2,1,0:T(8,128)(2,1)S(1)} %get-tuple-element.38), channel_id=1, source_target_pairs={{1,2},{2,1},{3,4},{4,3},{5,6},{6,5},{7,0},{0,7},{9,10},{10,9},{11,... | collective-permute-start | bytes 294920 | tf_op jit(solution)/shard_map/ppermute | solution.py:245
  30.8 9.3 %collective-permute-start.8 = (bf16[12,32,128]{2,1,0:T(8,128)(2,1)S(1)}, bf16[12,32,128]{2,1,0:T(8,128)(2,1)S(1)}, u32[]{:S(2)}, u32[]{:S(2)}) collective-permute-start(bf16[12,32,128]{2,1,0:T(8,128)(2,1)S(1)} %get-tuple-element.40), channel_id=1, source_target_pairs={{0,8},{8,0},{16,24},{24,16},{1,9},{9,1},{17,25},{25,17},{2,10},{10... | collective-permute-start | bytes 294920 | tf_op jit(solution)/shard_map/ppermute | solution.py:245
  30.9 9.3 %collective-permute-start.9 = (bf16[12,32,128]{2,1,0:T(8,128)(2,1)S(1)}, bf16[12,32,128]{2,1,0:T(8,128)(2,1)S(1)}, u32[]{:S(2)}, u32[]{:S(2)}) collective-permute-start(bf16[12,32,128]{2,1,0:T(8,128)(2,1)S(1)} %get-tuple-element.41), channel_id=1, source_target_pairs={{8,16},{16,8},{24,0},{0,24},{9,17},{17,9},{25,1},{1,25},{10,18},{1... | collective-permute-start | bytes 294920 | tf_op jit(solution)/shard_map/ppermute | solution.py:245
  32.5 7.7 %collective-permute-start.10 = (bf16[12,32,128]{2,1,0:T(8,128)(2,1)S(1)}, bf16[12,32,128]{2,1,0:T(8,128)(2,1)S(1)}, u32[]{:S(2)}, u32[]{:S(2)}) collective-permute-start(bf16[12,32,128]{2,1,0:T(8,128)(2,1)S(1)} %get-tuple-element.42), channel_id=1, source_target_pairs={{0,1},{1,0},{2,3},{3,2},{4,5},{5,4},{6,7},{7,6},{8,9},{9,8},{10,11... | collective-permute-start | bytes 294920 | tf_op jit(solution)/shard_map/ppermute | solution.py:245
  32.5 7.7 %collective-permute-start.11 = (bf16[12,32,128]{2,1,0:T(8,128)(2,1)S(1)}, bf16[12,32,128]{2,1,0:T(8,128)(2,1)S(1)}, u32[]{:S(2)}, u32[]{:S(2)}) collective-permute-start(bf16[12,32,128]{2,1,0:T(8,128)(2,1)S(1)} %get-tuple-element.43), channel_id=1, source_target_pairs={{1,2},{2,1},{3,4},{4,3},{5,6},{6,5},{7,0},{0,7},{9,10},{10,9},{11,... | collective-permute-start | bytes 294920 | tf_op jit(solution)/shard_map/ppermute | solution.py:245
  42.5 8.0 %collective-permute-start.12 = (bf16[12,32,128]{2,1,0:T(8,128)(2,1)S(1)}, bf16[12,32,128]{2,1,0:T(8,128)(2,1)S(1)}, u32[]{:S(2)}, u32[]{:S(2)}) collective-permute-start(bf16[12,32,128]{2,1,0:T(8,128)(2,1)S(1)} %get-tuple-element.46), channel_id=1, source_target_pairs={{0,8},{8,0},{16,24},{24,16},{1,9},{9,1},{17,25},{25,17},{2,10},{10... | collective-permute-start | bytes 294920 | tf_op jit(solution)/shard_map/ppermute | solution.py:245
  42.6 8.0 %collective-permute-start.13 = (bf16[12,32,128]{2,1,0:T(8,128)(2,1)S(1)}, bf16[12,32,128]{2,1,0:T(8,128)(2,1)S(1)}, u32[]{:S(2)}, u32[]{:S(2)}) collective-permute-start(bf16[12,32,128]{2,1,0:T(8,128)(2,1)S(1)} %get-tuple-element.47), channel_id=1, source_target_pairs={{8,16},{16,8},{24,0},{0,24},{9,17},{17,9},{25,1},{1,25},{10,18},{1... | collective-permute-start | bytes 294920 | tf_op jit(solution)/shard_map/ppermute | solution.py:245
  43.3 7.3 %collective-permute-start.14 = (bf16[12,32,128]{2,1,0:T(8,128)(2,1)S(1)}, bf16[12,32,128]{2,1,0:T(8,128)(2,1)S(1)}, u32[]{:S(2)}, u32[]{:S(2)}) collective-permute-start(bf16[12,32,128]{2,1,0:T(8,128)(2,1)S(1)} %get-tuple-element.48), channel_id=1, source_target_pairs={{0,1},{1,0},{2,3},{3,2},{4,5},{5,4},{6,7},{7,6},{8,9},{9,8},{10,11... | collective-permute-start | bytes 294920 | tf_op jit(solution)/shard_map/ppermute | solution.py:245
  43.3 7.5 %collective-permute-start.15 = (bf16[12,32,128]{2,1,0:T(8,128)(2,1)S(1)}, bf16[12,32,128]{2,1,0:T(8,128)(2,1)S(1)}, u32[]{:S(2)}, u32[]{:S(2)}) collective-permute-start(bf16[12,32,128]{2,1,0:T(8,128)(2,1)S(1)} %get-tuple-element.49), channel_id=1, source_target_pairs={{1,2},{2,1},{3,4},{4,3},{5,6},{6,5},{7,0},{0,7},{9,10},{10,9},{11,... | collective-permute-start | bytes 294920 | tf_op jit(solution)/shard_map/ppermute | solution.py:245

commit v2 on v1

v2 whole, which is shorter than its diff:
```python
import functools
import math

import jax
import jax.numpy as jnp
from jax import lax
from jax.experimental import pallas as pl
from jax.experimental.pallas import tpu as pltpu
from jax.sharding import PartitionSpec as P

RIM = 6
RIMS = 4
INNER = 9
LANES = 128
F32 = jnp.float32
BF16 = jnp.bfloat16

lower_edge = 0.3
center = (2.0 + lower_edge) / 2.0
half_width = (2.0 - lower_edge) / 2.0

ROWS_BY_ROWS = (((1,), (1,)), ((), ()))
ROWS_BY_COLS = (((1,), (0,)), ((), ()))


def mm(left, right, dims, precision=None):
    return lax.dot_general(left, right, dims, precision=precision, preferred_element_type=F32)


def beside(parts):
    return parts[0] if len(parts) == 1 else jnp.concatenate(parts, axis=1)


def over(parts):
    return parts[0] if len(parts) == 1 else jnp.concatenate(parts, axis=0)


def slot_pairs(first, last):
    return [list(range(s, min(s + 2, last))) for s in range(first, last, 2)]


def column(b):
    return pl.ds(b * LANES, LANES)


ORDER = (3, 1, 2, 0)


def outgoing_ones(meta_ref, pattern_hbm, w_hbm, *refs):
    pay_refs, (w_ref, pattern_ref, sums, sems) = refs[:4], refs[4:]
    copies = []
    for r in range(RIMS):
        rows = pl.ds(r * RIM, RIM)
        copies.append(pltpu.make_async_copy(w_hbm.at[rows, INNER:], w_ref.at[rows], sems.at[r]))
        copies[-1].start()
    copies.append(pltpu.make_async_copy(pattern_hbm, pattern_ref, sems.at[RIMS]))
    copies[-1].start()
    copies[-1].wait()
    slots = w_ref.shape[1]
    sums[...] = jnp.zeros_like(sums)
    ones = jnp.ones((8, LANES), BF16)
    for r in range(RIMS):
        copies[r].wait()
        for b in range(r * RIM, (r + 1) * RIM):
            part = mm(ones, beside([w_ref[b, s] for s in range(slots)]), ROWS_BY_COLS)
            for s in range(slots):
                q = pattern_ref[INNER + s, 0, b] - pattern_ref.shape[2]
                sums[r, pl.ds(q, 1)] += part[0:1, s * LANES : (s + 1) * LANES]
    for m in range(4):
        pay_refs[m][...] = sums[meta_ref[m]].astype(BF16).astype(F32)


def local_degree(pattern_ref, meta_ref, w_ref, deg_ref, acc):
    blocks, slots = w_ref.shape[:2]
    acc[...] = jnp.zeros_like(acc)
    ones = jnp.ones((8, LANES), BF16)
    wide_ones = jnp.ones((8, 3 * LANES), BF16)
    for b in range(blocks):
        own = INNER if b < RIMS * RIM else slots
        for group in slot_pairs(0, own):
            part = mm(ones, beside([w_ref[b, s] for s in group]), ROWS_BY_COLS)
            for i, s in enumerate(group):
                acc[pattern_ref[s, 0, b]] += part[:, i * LANES : (i + 1) * LANES]
        rows = w_ref[b, 0].astype(F32)
        for s in range(1, own):
            rows = rows + w_ref[b, s].astype(F32)
        if own < slots:
            outer = w_ref[b, own].astype(F32)
            for s in range(own + 1, slots):
                outer = outer + w_ref[b, s].astype(F32)
            rows = rows + meta_ref[8 + b // RIM].astype(F32) * outer
        high = rows.astype(BF16)
        rest = rows - high.astype(F32)
        mid = rest.astype(BF16)
        low = (rest - mid.astype(F32)).astype(BF16)
        total = mm(wide_ones, beside([high, mid, low]), ROWS_BY_ROWS)
        deg_ref[b : b + 1] = total[0:1]
    for b in range(blocks):
        deg_ref[b : b + 1] += acc[b, 0:1]


def send_out(u_ref, w_ref, pattern_ref, meta_ref, terms, pay_refs):
    blocks, slots = w_ref.shape[:2]
    terms[...] = jnp.zeros_like(terms)
    for b in range(RIMS * RIM):
        part = mm(u_ref[b], beside([w_ref[b, s] for s in range(INNER, slots)]), ROWS_BY_COLS)
        base = (b // RIM) * RIM - blocks
        for s in range(INNER, slots):
            i = s - INNER
            terms[base + pattern_ref[s, 0, b]] += part[:, i * LANES : (i + 1) * LANES]
    for m in range(4):
        first = meta_ref[m] * RIM
        pay_refs[m][0:RIM] = u_ref[pl.ds(first, RIM)]
        pay_refs[m][RIM:] = terms[pl.ds(first, RIM)].astype(BF16)


def first_scaled(pattern_ref, meta_ref, w_ref, deg_ref, x_ref, *refs):
    in_refs, (inv_ref, u_ref), pay_refs, (rims, terms) = refs[:4], refs[4:6], refs[6:10], refs[10:]
    blocks = w_ref.shape[0]
    for m in range(4):
        rims[meta_ref[m]] = in_refs[m][...] * meta_ref[4 + m].astype(F32)
    for b in range(blocks):
        degree = deg_ref[b : b + 1]
        if b < RIMS * RIM:
            degree = degree + rims[b // RIM, b % RIM : b % RIM + 1]
        inv = 1.0 / jnp.sqrt(0.5 * degree)
        inv_ref[b : b + 1] = inv
        u_ref[b] = (inv * x_ref[:, column(b)].astype(F32)).astype(BF16)
    send_out(u_ref, w_ref, pattern_ref, meta_ref, terms, pay_refs)


def own_products(pattern_ref, w_ref, turned, u_ref, acc_ref):
    blocks, slots = w_ref.shape[:2]
    acc_ref[...] = jnp.zeros_like(acc_ref)
    for b in range(blocks):
        total = None
        own = INNER if b < RIMS * RIM else slots
        for group in slot_pairs(0, own):
            part = mm(u_ref[b], beside([w_ref[b, s] for s in group]), ROWS_BY_COLS)
            for i, s in enumerate(group):
                acc_ref[pattern_ref[s, 0, b]] += part[:, i * LANES : (i + 1) * LANES]
            ahead = beside([u_ref[pattern_ref[s, 0, b]] for s in group])
            ahead = mm(ahead, over([turned(b, s) for s in group]), ROWS_BY_COLS)
            total = ahead if total is None else total + ahead
        acc_ref[b] += total


def own_terms(pattern_ref, w_ref, turned_ref, u_ref, acc_ref):
    own_products(pattern_ref, w_ref, lambda b, s: turned_ref[b, s], u_ref, acc_ref)


def own_terms_turning(pattern_ref, w_ref, u_ref, acc_ref, turned_ref):
    blocks, slots = w_ref.shape[:2]

    def turned(b, s):
        block = w_ref[b, s].T
        turned_ref[b, s] = block
        return block

    own_products(pattern_ref, w_ref, turned, u_ref, acc_ref)
    for b in range(RIMS * RIM):
        for s in range(INNER, slots):
            turned(b, s)


def combine(step, pattern_ref, meta_ref, turned_ref, inv_ref, acc_ref, in_refs, y_ref, before_ref, next_ref, ext, u_ref):
    blocks, slots = turned_ref.shape[:2]
    for m in range(4):
        live = meta_ref[4 + m].astype(BF16)
        first = meta_ref[m] * 2 * RIM
        ext[pl.ds(first, 2 * RIM)] = in_refs[m][...] * live
    for b in range(blocks):
        total = acc_ref[b]
        if b < RIMS * RIM:
            base = (b // RIM) * 2 * RIM
            ahead = beside([ext[base + pattern_ref[s, 0, b] - blocks] for s in range(INNER, slots)])
            total = total + mm(ahead, over([turned_ref[b, s] for s in range(INNER, slots)]), ROWS_BY_COLS)
            total = total + ext[base + RIM + b % RIM].astype(F32)
        inv = inv_ref[b : b + 1]
        y = y_ref[:, column(b)].astype(F32)
        lap = y - inv * (0.5 * total)
        new = (lap - center * y) / half_width
        if step > 0:
            new = 2.0 * new - before_ref[:, column(b)].astype(F32)
        next_ref[:, column(b)] = new
        if u_ref is not None:
            u_ref[b] = (inv * new).astype(BF16)


def advance(step, pattern_ref, meta_ref, w_ref, turned_ref, inv_ref, acc_ref, *refs):
    in_refs, (y_ref, before_ref, next_ref, u_ref) = refs[:4], refs[4:8]
    pay_refs, (ext, terms) = refs[8:12], refs[12:]
    combine(step, pattern_ref, meta_ref, turned_ref, inv_ref, acc_ref, in_refs, y_ref, before_ref, next_ref, ext, u_ref)
    send_out(u_ref, w_ref, pattern_ref, meta_ref, terms, pay_refs)


def finish(pattern_ref, meta_ref, turned_ref, inv_ref, acc_ref, *refs):
    in_refs, (y_ref, before_ref, next_ref, gram_ref, ext) = refs[:4], refs[4:]
    combine(2, pattern_ref, meta_ref, turned_ref, inv_ref, acc_ref, in_refs, y_ref, before_ref, next_ref, ext, None)
    y = next_ref[...]
    gram = mm(y, y, ROWS_BY_ROWS, lax.Precision.HIGHEST)
    packed = beside([gram[8 * i : 8 * i + 8] for i in range(gram.shape[0] // 8)])
    gram_ref[...] = jnp.broadcast_to(packed[None], gram_ref.shape)


def inverse_factor(gram, scale):
    n = gram.shape[0]
    tall = 8
    groups = range(n // tall)
    lane = lax.broadcasted_iota(jnp.int32, (tall, LANES), 1)
    sub = lax.broadcasted_iota(jnp.int32, (tall, LANES), 0)

    def spread(values, r):
        return jnp.broadcast_to(values[r : r + 1], (tall, LANES))

    both = []
    for i in groups:
        eye = (lane[:, :n] == sub[:, :n] + tall * i).astype(F32)
        both.append(beside([gram[tall * i : tall * (i + 1)], eye, jnp.zeros((tall, LANES - 2 * n), F32)]))
    parts = []
    for q in groups:
        columns = [
            {i: jnp.broadcast_to(both[i][:, tall * q + j : tall * q + j + 1], (tall, LANES)) for i in groups if i >= q}
            for j in range(tall)
        ]
        pivots = None
        for r in range(tall):
            pivot = spread(columns[r][q], r)
            pivots = pivot if pivots is None else jnp.where(sub == r, pivot, pivots)
            inv = 1.0 / pivot
            row = spread(both[q], r) * inv
            below = dict(columns[r])
            below[q] = jnp.where(sub > r, below[q], 0.0)
            live = [i for i in groups if i > q or (i == q and r < tall - 1)]
            for j in range(r + 1, tall):
                scaled = spread(columns[j][q], r) * inv
                for i in live:
                    columns[j][i] = columns[j][i] - below[i] * scaled
            for i in live:
                both[i] = both[i] - below[i] * row
        parts.append((both[q] * (scale / jnp.sqrt(pivots)))[:, n : 2 * n])
    return over(parts)


def orthonormal(scale, grams_ref, y_ref, out_ref):
    packed = jnp.sum(grams_ref[...], axis=0)
    n = y_ref.shape[0]
    gram = over([packed[:, n * i : n * (i + 1)] for i in range(n // 8)])
    out_ref[...] = mm(inverse_factor(gram, scale), y_ref[...], ROWS_BY_COLS, lax.Precision.HIGHEST)


def in_vmem(x):
    return pltpu.with_memory_space_constraint(x, pltpu.VMEM)


def kernel_call(body, name, ins, outs, scratch=(), flops=0, moved=0):
    specs, args = [], []
    for kind, x in ins:
        if kind == "hbm":
            specs.append(pl.BlockSpec(memory_space=pl.ANY))
            x = pltpu.with_memory_space_constraint(x, pltpu.HBM)
        elif kind == "smem":
            specs.append(pl.BlockSpec(memory_space=pltpu.SMEM))
            x = pltpu.with_memory_space_constraint(x, pltpu.SMEM)
        else:
            specs.append(pl.BlockSpec(memory_space=pltpu.VMEM))
            if kind == "held":
                x = in_vmem(x)
        args.append(x)
    return pl.pallas_call(
        body,
        name=name,
        out_shape=[pltpu.VMEM(s, d) if len(s) == 4 else jax.ShapeDtypeStruct(s, d) for s, d in outs],
        in_specs=specs,
        out_specs=[pl.BlockSpec(memory_space=pltpu.VMEM)] * len(outs),
        scratch_shapes=list(scratch),
        compiler_params=pltpu.CompilerParams(vmem_limit_bytes=16 << 20),
        cost_estimate=pl.CostEstimate(flops=flops, bytes_accessed=moved, transcendentals=0),
    )(*args)


def swaps():
    tall, broad = lax.axis_size("narrow"), lax.axis_size("wide")
    found = []
    for m in (0, 1):
        pairs = []
        for w in range(broad):
            for i in range(m, tall - 1, 2):
                pairs.append(((i, w), (i + 1, w)))
        if m == 1 and tall <= 4:
            pairs += [((0, w), (tall - 1, w)) for w in range(broad)]
        elif m == 1:
            pairs += [((i, w), (i, w + 1)) for i in (0, tall - 1) for w in range(0, broad, 2)]
        found.append(pairs)
    for m in (0, 1):
        pairs = []
        for i in range(tall):
            for w in range(m, broad - 1, 2):
                pairs.append(((i, w), (i, w + 1)))
        if m == 1:
            pairs += [((i, w), (i + 1, w)) for w in (0, broad - 1) for i in range(0, tall, 2)]
        found.append(pairs)
    flat = []
    for pairs in found:
        ends = [(a[0] * broad + a[1], b[0] * broad + b[1]) for a, b in pairs]
        flat.append([p for a, b in ends for p in ((a, b), (b, a))])
    return flat


def exchange(payloads):
    pairs = swaps()
    return [lax.ppermute(payload, ("narrow", "wide"), pairs[m]) for payload, m in zip(payloads, ORDER)]


def placement():
    sends, live, by_rim = [], [], []
    for a, axis in enumerate(("narrow", "wide")):
        place = lax.axis_index(axis)
        last = lax.axis_size(axis) - 1
        for m in (0, 1):
            after = (place + m) % 2 == 0
            sends.append(2 * a + after.astype(jnp.int32))
            live.append(jnp.where(after, place < last, place > 0).astype(jnp.int32))
        by_rim += [(place > 0).astype(jnp.int32), (place < last).astype(jnp.int32)]
    return jnp.stack([sends[m] for m in ORDER] + [live[m] for m in ORDER] + by_rim)


def body(start_block, weights, pattern):
    x = start_block[0, 0]
    w = weights[0, 0]
    slots_of = jnp.transpose(pattern, (0, 3, 1, 2))[0]
    meta = placement()
    vecs, docs = x.shape
    blocks, slots = w.shape[:2]
    rows = RIMS * RIM
    ids = [("smem", slots_of), ("smem", meta)]
    tile = ((blocks, vecs, LANES), F32)
    scaled = ((blocks, vecs, LANES), BF16)
    full = ((vecs, docs), F32)
    payload = [((2 * RIM, vecs, LANES), BF16)] * 4
    per_block = 2 * LANES * LANES

    pays = kernel_call(
        outgoing_ones, "outgoing_ones", ids[1:] + [("hbm", slots_of), ("hbm", w)], [((8, LANES), F32)] * 4,
        [pltpu.VMEM((rows, slots - INNER, LANES, LANES), BF16), pltpu.SMEM(slots_of.shape, jnp.int32),
         pltpu.VMEM((RIMS, 8, LANES), F32), pltpu.SemaphoreType.DMA((RIMS + 1,))],
        flops=rows * 3 * per_block * 32, moved=1 << 20,
    )
    w, *pays = lax.optimization_barrier((w, *pays))
    held = ids + [("held", w)]
    (degree,) = kernel_call(
        local_degree, "local_degree", held, [((blocks, LANES), F32)],
        [pltpu.VMEM((blocks, 8, LANES), F32)],
        flops=blocks * slots * per_block * 32, moved=8 << 20,
    )
    got = exchange(pays)
    inv, u, *pays = kernel_call(
        first_scaled, "first_scaled",
        held + [("vmem", degree), ("vmem", x)] + [("vmem", g) for g in got],
        [((blocks, LANES), F32), scaled] + payload,
        [pltpu.VMEM((RIMS, 8, LANES), F32), pltpu.VMEM((rows, vecs, LANES), F32)],
        flops=rows * 3 * per_block * 32, moved=1 << 20,
    )
    before, y = x, x
    for step in range(3):
        cost = dict(flops=2 * blocks * slots * per_block * vecs, moved=8 << 20)
        if step == 0:
            acc, turned = kernel_call(
                own_terms_turning, "own_terms_turning", ids[:1] + [("held", w), ("vmem", u)], [tile, (w.shape, BF16)], **cost
            )
        else:
            (acc,) = kernel_call(
                own_terms, "own_terms", ids[:1] + [("held", w), ("held", turned), ("vmem", u)], [tile], **cost
            )
        got = exchange(pays)
        common = [("held", turned), ("vmem", inv), ("vmem", acc)] + [("vmem", g) for g in got]
        common += [("vmem", y), ("vmem", before)]
        ext = pltpu.VMEM((2 * rows, vecs, LANES), BF16)
        if step < 2:
            new, u, *pays = kernel_call(
                functools.partial(advance, step), "advance", held + common, [full, scaled] + payload,
                [ext, pltpu.VMEM((rows, vecs, LANES), F32)],
                flops=2 * rows * 3 * per_block * 32, moved=1 << 20,
            )
        else:
            peers = lax.axis_size("narrow") * lax.axis_size("wide")
            new, grams = kernel_call(
                finish, "finish", ids + common, [full, ((peers, 8, LANES), F32)], [ext],
                flops=rows * 3 * per_block * 32, moved=1 << 20,
            )
        before, y = y, new
    grams = lax.all_to_all(grams, ("narrow", "wide"), 0, 0)
    (out,) = kernel_call(
        functools.partial(orthonormal, math.sqrt(peers * docs)), "orthonormal",
        [("vmem", grams), ("vmem", y)], [full],
    )
    return out[None, None]


def solution(mesh):
    placed = (
        P("narrow", "wide", None, None),
        P("narrow", "wide", None, None, None, None),
        P("narrow", "wide", None, None),
    )
    return jax.shard_map(
        body, mesh=mesh, in_specs=placed, out_specs=P("narrow", "wide", None, None), check_vma=False
    )
```

time: 68.8 us -> 55.5 us (0.81)
  Pallas kernels: 32.7 us -> 26.2 us
  local copies, waits for them, and re-layouts: 5 us -> 0.1 us
  starting transfers between devices: 19.3 us -> 18.1 us
    pallas_call x10, Pallas kernels: 32.7 us -> 26.2 us  [kernel_call(): pl.pallas_call(body, name=name, out_shape=[pltpu.VMEM(s, d) if len(s) ==...]
    unnamed x5 -> x6, local copies, waits for them, and re-layouts: 4.91 us -> 0.02 us
    ppermute x16, starting transfers between devices: 19.3 us -> 18.1 us  [exchange(): lax.ppermute(payload, ('narrow', 'wide'), pairs[m])]
  transfers between devices with their start and end apart: 16 -> 16, of which waited for: 1 -> 0; matrix products, arithmetic and copies ran while one was open for 0% -> 0% of each run, Pallas kernels for 26% -> 26%
where the time goes in v2:
time: 55.5 us; the launch traced here: 55.4 us
  Pallas kernels  26.2 us (47%)
  starting transfers between devices  18.1 us (33%)
  blocking collectives  10.7 us (19%)
    pallas_call x10, Pallas kernels, kernel_call(): pl.pallas_call(body, name=name, out_shape=[pltpu.VMEM(s, d) if len(s) ==...  26.2 us
    ppermute x16, starting transfers between devices, exchange(): lax.ppermute(payload, ('narrow', 'wide'), pairs[m])  18.1 us
    all_to_all x1, blocking collectives, body(): grams = lax.all_to_all(grams, ('narrow', 'wide'), 0, 0)  10.7 us
  transfers between devices with their start and end apart: 16, of which 0 were waited for; matrix products, arithmetic and copies ran while one was open for 0% of the time, Pallas kernels for 26%

profile of v2, /device:TPU:0, one launch (start us, length us, event | category | flops | bytes accessed | tf_op | source)
XLA Modules:
  0.0 55.4 jit_solution(16623249656907812342)
XLA Ops:
  0.0 0.0 copy-start.2
  0.0 0.1 stack.91.meta_ref
  0.1 0.0 copy-start
  0.1 0.0 copy-start.1
  0.1 2.8 %outgoing_ones.1 = (f32[8,128]{1,0:T(8,128)S(1)}, f32[8,128]{1,0:T(8,128)S(1)}, f32[8,128]{1,0:T(8,128)S(1)}, f32[8,128]{1,0:T(8,128)S(1)}) custom-call(s32[12]{0:T(128)S(1)} %stack.91.meta_ref, s32[12,1,28]{2,1,0:T(1,128)} %bitcast.30, bf16[28,12,128,128]{3,2,1,0:T(8,128)(2,1)} %bitcast.18), custom_call_target="tpu_custom_call" | custom-call | flops 75497472 | bytes 1048576 | tf_op jit(solution)/shard_map/outgoing_ones/pallas_call | solution.py:270
  2.9 0.5 collective-permute-start
  3.4 2.6 %collective-permute-start.1 = (f32[8,128]{1,0:T(8,128)S(1)}, f32[8,128]{1,0:T(8,128)S(1)}, u32[]{:S(2)}, u32[]{:S(2)}) collective-permute-start(f32[8,128]{1,0:T(8,128)S(1)} %get-tuple-element.42), channel_id=1, source_target_pairs={{8,16},{16,8},{9,17},{17,9},{10,18},{18,10},{11,19},{19,11},{12,20... | collective-permute-start | bytes 12296 | tf_op jit(solution)/shard_map/ppermute | solution.py:312
  6.0 2.1 %collective-permute-start.2 = (f32[8,128]{1,0:T(8,128)S(1)}, f32[8,128]{1,0:T(8,128)S(1)}, u32[]{:S(2)}, u32[]{:S(2)}) collective-permute-start(f32[8,128]{1,0:T(8,128)S(1)} %get-tuple-element.43), channel_id=1, source_target_pairs={{0,1},{1,0},{2,3},{3,2},{4,5},{5,4},{6,7},{7,6},{8,9},{9,8},{10,11... | collective-permute-start | bytes 12296 | tf_op jit(solution)/shard_map/ppermute | solution.py:312
  8.1 0.7 %collective-permute-start.3 = (f32[8,128]{1,0:T(8,128)S(1)}, f32[8,128]{1,0:T(8,128)S(1)}, u32[]{:S(2)}, u32[]{:S(2)}) collective-permute-start(f32[8,128]{1,0:T(8,128)S(1)} %get-tuple-element.44), channel_id=1, source_target_pairs={{0,8},{8,0},{16,24},{24,16},{1,9},{9,1},{17,25},{25,17},{2,10},{10... | collective-permute-start | bytes 12296 | tf_op jit(solution)/shard_map/ppermute | solution.py:312
  8.8 0.0 copy-done.2
  8.8 0.0 copy-done
  8.8 3.1 %local_degree.1.deg_ref = f32[28,128]{1,0:T(8,128)S(1)} custom-call(s32[12,1,28]{2,1,0:T(1,128)S(1)} %bitcast.31, s32[12]{0:T(128)S(1)} %stack.91.meta_ref, bf16[28,12,128,128]{3,2,1,0:T(8,128)(2,1)S(1)} %bitcast.19), custom_call_target="tpu_custom_call" | custom-call | flops 352321536 | bytes 8388608 | tf_op jit(solution)/shard_map/local_degree/pallas_call | solution.py:270
  11.9 0.0 collective-permute-done.refs_0_
  11.9 0.0 collective-permute-done.1.refs_1_
  11.9 0.0 collective-permute-done.2.refs_2_
  11.9 0.0 collective-permute-done.3.refs_3_
  12.0 0.0 copy-done.1
  12.0 1.3 %first_scaled.1 = (f32[28,128]{1,0:T(8,128)S(1)}, bf16[28,32,128]{2,1,0:T(8,128)(2,1)S(1)}, bf16[12,32,128]{2,1,0:T(8,128)(2,1)S(1)}, bf16[12,32,128]{2,1,0:T(8,...) custom-call(s32[12,1,28]{2,1,0:T(1,128)S(1)} %bitcast.32, s32[12]{0:T(128)S(1)} %stack.91.meta_ref, ...), custom_call_target="tpu_custom_call" | custom-call | flops 75497472 | bytes 1048576 | tf_op jit(solution)/shard_map/first_scaled/pallas_call | solution.py:270
  13.2 0.1 collective-permute-start.4
  13.3 0.7 %collective-permute-start.5 = (bf16[12,32,128]{2,1,0:T(8,128)(2,1)S(1)}, bf16[12,32,128]{2,1,0:T(8,128)(2,1)S(1)}, u32[]{:S(2)}, u32[]{:S(2)}) collective-permute-start(bf16[12,32,128]{2,1,0:T(8,128)(2,1)S(1)} %get-tuple-element.50), channel_id=1, source_target_pairs={{8,16},{16,8},{9,17},{17,9},{10,18},{18,10},{11,19},{19,11},{12,20... | collective-permute-start | bytes 294920 | tf_op jit(solution)/shard_map/ppermute | solution.py:312
  14.0 2.4 %collective-permute-start.6 = (bf16[12,32,128]{2,1,0:T(8,128)(2,1)S(1)}, bf16[12,32,128]{2,1,0:T(8,128)(2,1)S(1)}, u32[]{:S(2)}, u32[]{:S(2)}) collective-permute-start(bf16[12,32,128]{2,1,0:T(8,128)(2,1)S(1)} %get-tuple-element.51), channel_id=1, source_target_pairs={{0,1},{1,0},{2,3},{3,2},{4,5},{5,4},{6,7},{7,6},{8,9},{9,8},{10,11... | collective-permute-start | bytes 294920 | tf_op jit(solution)/shard_map/ppermute | solution.py:312
  16.4 0.4 collective-permute-start.7
  16.7 4.4 %own_terms_turning.1 = (f32[28,32,128]{2,1,0:T(8,128)S(1)}, bf16[28,12,128,128]{3,2,1,0:T(8,128)(2,1)S(1)}) custom-call(s32[12,1,28]{2,1,0:T(1,128)S(1)} %bitcast.33, bf16[28,12,128,128]{3,2,1,0:T(8,128)(2,1)S(1)} %bitcast.21, bf16[28,32,128]{2,1,0:T(8,128)(2,1)S(1)} %get-tuple-element.45.u_ref), custom_call_target="tpu_custom_call" | custom-call | flops 704643072 | bytes 8388608 | tf_op jit(solution)/shard_map/own_terms_turning/pallas_call | solution.py:270
  21.1 0.0 collective-permute-done.4.refs_0_
  21.1 0.0 collective-permute-done.5.refs_1_
  21.1 0.0 collective-permute-done.6.refs_2_
  21.1 0.0 collective-permute-done.7.refs_3_
  21.1 1.7 %advance.2 = (f32[32,3584]{1,0:T(8,128)S(1)}, bf16[28,32,128]{2,1,0:T(8,128)(2,1)S(1)}, bf16[12,32,128]{2,1,0:T(8,128)(2,1)S(1)}, bf16[12,32,128]{2,1,0:T(8,128)...) custom-call(s32[12,1,28]{2,1,0:T(1,128)S(1)} %bitcast.34, s32[12]{0:T(128)S(1)} %stack.91.meta_ref, ...), custom_call_target="tpu_custom_call" | custom-call | flops 150994944 | bytes 1048576 | tf_op jit(solution)/shard_map/advance/pallas_call | solution.py:270
  22.9 0.2 collective-permute-start.8
  23.1 1.5 %collective-permute-start.9 = (bf16[12,32,128]{2,1,0:T(8,128)(2,1)S(1)}, bf16[12,32,128]{2,1,0:T(8,128)(2,1)S(1)}, u32[]{:S(2)}, u32[]{:S(2)}) collective-permute-start(bf16[12,32,128]{2,1,0:T(8,128)(2,1)S(1)} %get-tuple-element.55), channel_id=1, source_target_pairs={{8,16},{16,8},{9,17},{17,9},{10,18},{18,10},{11,19},{19,11},{12,20... | collective-permute-start | bytes 294920 | tf_op jit(solution)/shard_map/ppermute | solution.py:312
  24.5 2.2 %collective-permute-start.10 = (bf16[12,32,128]{2,1,0:T(8,128)(2,1)S(1)}, bf16[12,32,128]{2,1,0:T(8,128)(2,1)S(1)}, u32[]{:S(2)}, u32[]{:S(2)}) collective-permute-start(bf16[12,32,128]{2,1,0:T(8,128)(2,1)S(1)} %get-tuple-element.56), channel_id=1, source_target_pairs={{0,1},{1,0},{2,3},{3,2},{4,5},{5,4},{6,7},{7,6},{8,9},{9,8},{10,11... | collective-permute-start | bytes 294920 | tf_op jit(solution)/shard_map/ppermute | solution.py:312
  26.8 0.5 collective-permute-start.11
  27.3 3.4 %own_terms.2.acc_ref = f32[28,32,128]{2,1,0:T(8,128)S(1)} custom-call(s32[12,1,28]{2,1,0:T(1,128)S(1)} %bitcast.35, bf16[28,12,128,128]{3,2,1,0:T(8,128)(2,1)S(1)} %bitcast.23, bf16[28,12,128,128]{3,2,1,0:T(8,128)(2,1)S(1)} %get-tuple-element.46.turned_ref, bf16[28,32,128]{2,1,0:T(8,128)(2,1)S(1)} %get-tuple-element.53.u_ref), custom_call_target="tpu_custom_call" | custom-call | flops 704643072 | bytes 8388608 | tf_op jit(solution)/shard_map/own_terms/pallas_call | solution.py:270
  30.7 0.0 collective-permute-done.8.refs_0_
  30.8 0.0 collective-permute-done.9.refs_1_
  30.8 0.0 collective-permute-done.10.refs_2_
  30.8 0.0 collective-permute-done.11.refs_3_
  30.8 1.9 %advance.3 = (f32[32,3584]{1,0:T(8,128)S(1)}, bf16[28,32,128]{2,1,0:T(8,128)(2,1)S(1)}, bf16[12,32,128]{2,1,0:T(8,128)(2,1)S(1)}, bf16[12,32,128]{2,1,0:T(8,128)...) custom-call(s32[12,1,28]{2,1,0:T(1,128)S(1)} %bitcast.36, s32[12]{0:T(128)S(1)} %stack.91.meta_ref, ...), custom_call_target="tpu_custom_call" | custom-call | flops 150994944 | bytes 1048576 | tf_op jit(solution)/shard_map/advance/pallas_call | solution.py:270
  32.7 0.1 collective-permute-start.12
  32.8 0.6 %collective-permute-start.13 = (bf16[12,32,128]{2,1,0:T(8,128)(2,1)S(1)}, bf16[12,32,128]{2,1,0:T(8,128)(2,1)S(1)}, u32[]{:S(2)}, u32[]{:S(2)}) collective-permute-start(bf16[12,32,128]{2,1,0:T(8,128)(2,1)S(1)} %get-tuple-element.61), channel_id=1, source_target_pairs={{8,16},{16,8},{9,17},{17,9},{10,18},{18,10},{11,19},{19,11},{12,20... | collective-permute-start | bytes 294920 | tf_op jit(solution)/shard_map/ppermute | solution.py:312
  33.4 3.1 %collective-permute-start.14 = (bf16[12,32,128]{2,1,0:T(8,128)(2,1)S(1)}, bf16[12,32,128]{2,1,0:T(8,128)(2,1)S(1)}, u32[]{:S(2)}, u32[]{:S(2)}) collective-permute-start(bf16[12,32,128]{2,1,0:T(8,128)(2,1)S(1)} %get-tuple-element.62), channel_id=1, source_target_pairs={{0,1},{1,0},{2,3},{3,2},{4,5},{5,4},{6,7},{7,6},{8,9},{9,8},{10,11... | collective-permute-start | bytes 294920 | tf_op jit(solution)/shard_map/ppermute | solution.py:312
  36.6 0.4 collective-permute-start.15
  37.0 3.4 %own_terms.3.acc_ref = f32[28,32,128]{2,1,0:T(8,128)S(1)} custom-call(s32[12,1,28]{2,1,0:T(1,128)S(1)} %bitcast.37, bf16[28,12,128,128]{3,2,1,0:T(8,128)(2,1)S(1)} %bitcast.25, bf16[28,12,128,128]{3,2,1,0:T(8,128)(2,1)S(1)} %get-tuple-element.46.turned_ref, bf16[28,32,128]{2,1,0:T(8,128)(2,1)S(1)} %get-tuple-element.59.u_ref), custom_call_target="tpu_custom_call" | custom-call | flops 704643072 | bytes 8388608 | tf_op jit(solution)/shard_map/own_terms/pallas_call | solution.py:270
  40.4 0.0 collective-permute-done.12.refs_0_
  40.5 0.0 collective-permute-done.13.refs_1_
  40.5 0.0 collective-permute-done.14.refs_2_
  40.5 0.0 collective-permute-done.15.refs_3_
  40.5 2.0 %finish.1 = (f32[32,3584]{1,0:T(8,128)S(1)}, f32[32,8,128]{2,1,0:T(8,128)S(1)}) custom-call(s32[12,1,28]{2,1,0:T(1,128)S(1)} %bitcast.38, s32[12]{0:T(128)S(1)} %stack.91.meta_ref, bf16[28,12,128,128]{3,2,1,0:T(8,128)(2,1)S(1)} %get-tuple-element.46.turned_ref, f32[28,128]{1,0:T(8,128)S(1)} %get-tuple-element.47.inv_ref, ...), custom_call_target="tpu_custom_call" | custom-call | flops 75497472 | bytes 1048576 | tf_op jit(solution)/shard_map/finish/pallas_call | solution.py:270
  42.4 10.7 %all_to_all.5.grams_ref = f32[32,8,128]{2,1,0:T(8,128)S(1)} all-to-all(f32[32,8,128]{2,1,0:T(8,128)S(1)} %get-tuple-element.65), channel_id=1, replica_groups=mesh['narrow'=4,'wide'=8] {'narrow','wide'}, dimensions={0} | all-to-all | bytes 262144 | tf_op jit(solution)/shard_map/all_to_all | solution.py:392
  53.1 2.2 %orthonormal.1 = f32[32,3584]{1,0:T(8,128)} custom-call(f32[32,8,128]{2,1,0:T(8,128)S(1)} %all_to_all.5.grams_ref, f32[32,3584]{1,0:T(8,128)S(1)} %get-tuple-element.66.y_ref), custom_call_target="tpu_custom_call" | custom-call | tf_op jit(solution)/shard_map/orthonormal/pallas_call | solution.py:270
Async XLA Ops:
  0.0 8.8 %copy-start.2 = (s32[1,1,28,12]{2,1,3,0:T(1,128)S(1)}, s32[1,1,28,12]{2,1,3,0:T(1,128)}, u32[]{:S(2)}) copy-start(s32[1,1,28,12]{2,1,3,0:T(1,128)} %param.5) | copy-start | bytes 4036
  0.1 8.7 %copy-start = (bf16[1,1,28,12,128,128]{5,4,3,2,1,0:T(8,128)(2,1)S(1)}, bf16[1,1,28,12,128,128]{5,4,3,2,1,0:T(8,128)(2,1)}, u32[]{:S(2)}) copy-start(bf16[1,1,28,12,128,128]{5,4,3,2,1,0:T(8,128)(2,1)} %param.4) | copy-start | bytes 33030148
  0.1 11.9 %copy-start.1 = (bf16[1,1,32,3584]{3,2,1,0:T(8,128)(2,1)S(1)}, bf16[1,1,32,3584]{3,2,1,0:T(8,128)(2,1)}, u32[]{:S(2)}) copy-start(bf16[1,1,32,3584]{3,2,1,0:T(8,128)(2,1)} %param.3) | copy-start | bytes 688132
  2.9 9.0 %collective-permute-start = (f32[8,128]{1,0:T(8,128)S(1)}, f32[8,128]{1,0:T(8,128)S(1)}, u32[]{:S(2)}, u32[]{:S(2)}) collective-permute-start(f32[8,128]{1,0:T(8,128)S(1)} %get-tuple-element.41), channel_id=1, source_target_pairs={{1,2},{2,1},{3,4},{4,3},{5,6},{6,5},{9,10},{10,9},{11,12},{12,11},... | collective-permute-start | bytes 12296 | tf_op jit(solution)/shard_map/ppermute | solution.py:312
  3.4 8.5 %collective-permute-start.1 = (f32[8,128]{1,0:T(8,128)S(1)}, f32[8,128]{1,0:T(8,128)S(1)}, u32[]{:S(2)}, u32[]{:S(2)}) collective-permute-start(f32[8,128]{1,0:T(8,128)S(1)} %get-tuple-element.42), channel_id=1, source_target_pairs={{8,16},{16,8},{9,17},{17,9},{10,18},{18,10},{11,19},{19,11},{12,20... | collective-permute-start | bytes 12296 | tf_op jit(solution)/shard_map/ppermute | solution.py:312
  6.0 5.9 %collective-permute-start.2 = (f32[8,128]{1,0:T(8,128)S(1)}, f32[8,128]{1,0:T(8,128)S(1)}, u32[]{:S(2)}, u32[]{:S(2)}) collective-permute-start(f32[8,128]{1,0:T(8,128)S(1)} %get-tuple-element.43), channel_id=1, source_target_pairs={{0,1},{1,0},{2,3},{3,2},{4,5},{5,4},{6,7},{7,6},{8,9},{9,8},{10,11... | collective-permute-start | bytes 12296 | tf_op jit(solution)/shard_map/ppermute | solution.py:312
  8.1 3.8 %collective-permute-start.3 = (f32[8,128]{1,0:T(8,128)S(1)}, f32[8,128]{1,0:T(8,128)S(1)}, u32[]{:S(2)}, u32[]{:S(2)}) collective-permute-start(f32[8,128]{1,0:T(8,128)S(1)} %get-tuple-element.44), channel_id=1, source_target_pairs={{0,8},{8,0},{16,24},{24,16},{1,9},{9,1},{17,25},{25,17},{2,10},{10... | collective-permute-start | bytes 12296 | tf_op jit(solution)/shard_map/ppermute | solution.py:312
  13.2 7.9 %collective-permute-start.4 = (bf16[12,32,128]{2,1,0:T(8,128)(2,1)S(1)}, bf16[12,32,128]{2,1,0:T(8,128)(2,1)S(1)}, u32[]{:S(2)}, u32[]{:S(2)}) collective-permute-start(bf16[12,32,128]{2,1,0:T(8,128)(2,1)S(1)} %get-tuple-element.49), channel_id=1, source_target_pairs={{1,2},{2,1},{3,4},{4,3},{5,6},{6,5},{9,10},{10,9},{11,12},{12,11},... | collective-permute-start | bytes 294920 | tf_op jit(solution)/shard_map/ppermute | solution.py:312
  13.3 7.8 %collective-permute-start.5 = (bf16[12,32,128]{2,1,0:T(8,128)(2,1)S(1)}, bf16[12,32,128]{2,1,0:T(8,128)(2,1)S(1)}, u32[]{:S(2)}, u32[]{:S(2)}) collective-permute-start(bf16[12,32,128]{2,1,0:T(8,128)(2,1)S(1)} %get-tuple-element.50), channel_id=1, source_target_pairs={{8,16},{16,8},{9,17},{17,9},{10,18},{18,10},{11,19},{19,11},{12,20... | collective-permute-start | bytes 294920 | tf_op jit(solution)/shard_map/ppermute | solution.py:312
  14.0 7.2 %collective-permute-start.6 = (bf16[12,32,128]{2,1,0:T(8,128)(2,1)S(1)}, bf16[12,32,128]{2,1,0:T(8,128)(2,1)S(1)}, u32[]{:S(2)}, u32[]{:S(2)}) collective-permute-start(bf16[12,32,128]{2,1,0:T(8,128)(2,1)S(1)} %get-tuple-element.51), channel_id=1, source_target_pairs={{0,1},{1,0},{2,3},{3,2},{4,5},{5,4},{6,7},{7,6},{8,9},{9,8},{10,11... | collective-permute-start | bytes 294920 | tf_op jit(solution)/shard_map/ppermute | solution.py:312
  16.4 4.8 %collective-permute-start.7 = (bf16[12,32,128]{2,1,0:T(8,128)(2,1)S(1)}, bf16[12,32,128]{2,1,0:T(8,128)(2,1)S(1)}, u32[]{:S(2)}, u32[]{:S(2)}) collective-permute-start(bf16[12,32,128]{2,1,0:T(8,128)(2,1)S(1)} %get-tuple-element.52), channel_id=1, source_target_pairs={{0,8},{8,0},{16,24},{24,16},{1,9},{9,1},{17,25},{25,17},{2,10},{10... | collective-permute-start | bytes 294920 | tf_op jit(solution)/shard_map/ppermute | solution.py:312
  22.9 7.9 %collective-permute-start.8 = (bf16[12,32,128]{2,1,0:T(8,128)(2,1)S(1)}, bf16[12,32,128]{2,1,0:T(8,128)(2,1)S(1)}, u32[]{:S(2)}, u32[]{:S(2)}) collective-permute-start(bf16[12,32,128]{2,1,0:T(8,128)(2,1)S(1)} %get-tuple-element.54), channel_id=1, source_target_pairs={{1,2},{2,1},{3,4},{4,3},{5,6},{6,5},{9,10},{10,9},{11,12},{12,11},... | collective-permute-start | bytes 294920 | tf_op jit(solution)/shard_map/ppermute | solution.py:312
  23.1 7.7 %collective-permute-start.9 = (bf16[12,32,128]{2,1,0:T(8,128)(2,1)S(1)}, bf16[12,32,128]{2,1,0:T(8,128)(2,1)S(1)}, u32[]{:S(2)}, u32[]{:S(2)}) collective-permute-start(bf16[12,32,128]{2,1,0:T(8,128)(2,1)S(1)} %get-tuple-element.55), channel_id=1, source_target_pairs={{8,16},{16,8},{9,17},{17,9},{10,18},{18,10},{11,19},{19,11},{12,20... | collective-permute-start | bytes 294920 | tf_op jit(solution)/shard_map/ppermute | solution.py:312
  24.5 6.2 %collective-permute-start.10 = (bf16[12,32,128]{2,1,0:T(8,128)(2,1)S(1)}, bf16[12,32,128]{2,1,0:T(8,128)(2,1)S(1)}, u32[]{:S(2)}, u32[]{:S(2)}) collective-permute-start(bf16[12,32,128]{2,1,0:T(8,128)(2,1)S(1)} %get-tuple-element.56), channel_id=1, source_target_pairs={{0,1},{1,0},{2,3},{3,2},{4,5},{5,4},{6,7},{7,6},{8,9},{9,8},{10,11... | collective-permute-start | bytes 294920 | tf_op jit(solution)/shard_map/ppermute | solution.py:312
  26.8 4.0 %collective-permute-start.11 = (bf16[12,32,128]{2,1,0:T(8,128)(2,1)S(1)}, bf16[12,32,128]{2,1,0:T(8,128)(2,1)S(1)}, u32[]{:S(2)}, u32[]{:S(2)}) collective-permute-start(bf16[12,32,128]{2,1,0:T(8,128)(2,1)S(1)} %get-tuple-element.57), channel_id=1, source_target_pairs={{0,8},{8,0},{16,24},{24,16},{1,9},{9,1},{17,25},{25,17},{2,10},{10... | collective-permute-start | bytes 294920 | tf_op jit(solution)/shard_map/ppermute | solution.py:312
  32.7 7.7 %collective-permute-start.12 = (bf16[12,32,128]{2,1,0:T(8,128)(2,1)S(1)}, bf16[12,32,128]{2,1,0:T(8,128)(2,1)S(1)}, u32[]{:S(2)}, u32[]{:S(2)}) collective-permute-start(bf16[12,32,128]{2,1,0:T(8,128)(2,1)S(1)} %get-tuple-element.60), channel_id=1, source_target_pairs={{1,2},{2,1},{3,4},{4,3},{5,6},{6,5},{9,10},{10,9},{11,12},{12,11},... | collective-permute-start | bytes 294920 | tf_op jit(solution)/shard_map/ppermute | solution.py:312
  32.8 7.7 %collective-permute-start.13 = (bf16[12,32,128]{2,1,0:T(8,128)(2,1)S(1)}, bf16[12,32,128]{2,1,0:T(8,128)(2,1)S(1)}, u32[]{:S(2)}, u32[]{:S(2)}) collective-permute-start(bf16[12,32,128]{2,1,0:T(8,128)(2,1)S(1)} %get-tuple-element.61), channel_id=1, source_target_pairs={{8,16},{16,8},{9,17},{17,9},{10,18},{18,10},{11,19},{19,11},{12,20... | collective-permute-start | bytes 294920 | tf_op jit(solution)/shard_map/ppermute | solution.py:312
  33.4 7.0 %collective-permute-start.14 = (bf16[12,32,128]{2,1,0:T(8,128)(2,1)S(1)}, bf16[12,32,128]{2,1,0:T(8,128)(2,1)S(1)}, u32[]{:S(2)}, u32[]{:S(2)}) collective-permute-start(bf16[12,32,128]{2,1,0:T(8,128)(2,1)S(1)} %get-tuple-element.62), channel_id=1, source_target_pairs={{0,1},{1,0},{2,3},{3,2},{4,5},{5,4},{6,7},{7,6},{8,9},{9,8},{10,11... | collective-permute-start | bytes 294920 | tf_op jit(solution)/shard_map/ppermute | solution.py:312
  36.6 3.9 %collective-permute-start.15 = (bf16[12,32,128]{2,1,0:T(8,128)(2,1)S(1)}, bf16[12,32,128]{2,1,0:T(8,128)(2,1)S(1)}, u32[]{:S(2)}, u32[]{:S(2)}) collective-permute-start(bf16[12,32,128]{2,1,0:T(8,128)(2,1)S(1)} %get-tuple-element.63), channel_id=1, source_target_pairs={{0,8},{8,0},{16,24},{24,16},{1,9},{9,1},{17,25},{25,17},{2,10},{10... | collective-permute-start | bytes 294920 | tf_op jit(solution)/shard_map/ppermute | solution.py:312

commit v3 on v2

--- a/solution.py
+++ b/solution.py
@@ -46,38 +46,62 @@
 ORDER = (3, 1, 2, 0)
 
 
-def outgoing_ones(meta_ref, pattern_hbm, w_hbm, *refs):
-    pay_refs, (w_ref, pattern_ref, sums, sems) = refs[:4], refs[4:]
+def places(shape):
+    rim_of, live_of, by_rim = [], [], []
+    for a, axis in enumerate(("narrow", "wide")):
+        place = lax.axis_index(axis)
+        behind = (place > 0).astype(jnp.int32)
+        ahead = (place < shape[a] - 1).astype(jnp.int32)
+        odd = lax.rem(place, 2)
+        for m in (0, 1):
+            after = odd if m else 1 - odd
+            rim_of.append(2 * a + after)
+            live_of.append(after * ahead + (1 - after) * behind)
+        by_rim += [behind, ahead]
+    return [rim_of[m] for m in ORDER], [live_of[m] for m in ORDER], by_rim
+
+
+def fetch(source, target, sem):
+    copy = pltpu.make_async_copy(source, target, sem)
+    copy.start()
+    return copy
+
+
+def outgoing_ones(shape, pattern_hbm, w_hbm, *refs):
+    pay_refs, (pattern_ref, w_ref, sums, sems) = refs[:4], refs[4:]
+    named = fetch(pattern_hbm, pattern_ref, sems.at[RIMS])
     copies = []
     for r in range(RIMS):
         rows = pl.ds(r * RIM, RIM)
-        copies.append(pltpu.make_async_copy(w_hbm.at[rows, INNER:], w_ref.at[rows], sems.at[r]))
-        copies[-1].start()
-    copies.append(pltpu.make_async_copy(pattern_hbm, pattern_ref, sems.at[RIMS]))
-    copies[-1].start()
-    copies[-1].wait()
+        copies.append(fetch(w_hbm.at[rows, INNER:], w_ref.at[rows], sems.at[r]))
+    blocks = pattern_ref.shape[2]
     slots = w_ref.shape[1]
     sums[...] = jnp.zeros_like(sums)
     ones = jnp.ones((8, LANES), BF16)
+    named.wait()
     for r in range(RIMS):
         copies[r].wait()
         for b in range(r * RIM, (r + 1) * RIM):
             part = mm(ones, beside([w_ref[b, s] for s in range(slots)]), ROWS_BY_COLS)
             for s in range(slots):
-                q = pattern_ref[INNER + s, 0, b] - pattern_ref.shape[2]
-                sums[r, pl.ds(q, 1)] += part[0:1, s * LANES : (s + 1) * LANES]
+                sums[r * RIM - blocks + pattern_ref[INNER + s, 0, b]] += part[:, s * LANES : (s + 1) * LANES]
+    rim_of, _, _ = places(shape)
     for m in range(4):
-        pay_refs[m][...] = sums[meta_ref[m]].astype(BF16).astype(F32)
-
-
-def local_degree(pattern_ref, meta_ref, w_ref, deg_ref, acc):
+        for q in range(RIM):
+            pay_refs[m][q : q + 1] = sums[rim_of[m] * RIM + q][0:1].astype(BF16).astype(F32)
+
+
+def local_degree(shape, pattern_ref, w_ref, deg_ref, acc):
     blocks, slots = w_ref.shape[:2]
-    acc[...] = jnp.zeros_like(acc)
+    by_rim = places(shape)[2]
     ones = jnp.ones((8, LANES), BF16)
-    wide_ones = jnp.ones((8, 3 * LANES), BF16)
+    for b in range(0, blocks, 2):
+        part = mm(ones, beside([w_ref[b, 0], w_ref[b + 1, 0]]), ROWS_BY_COLS)
+        acc[b] = part[:, :LANES]
+        acc[b + 1] = part[:, LANES:]
     for b in range(blocks):
         own = INNER if b < RIMS * RIM else slots
-        for group in slot_pairs(0, own):
+        for group in slot_pairs(1, own):
             part = mm(ones, beside([w_ref[b, s] for s in group]), ROWS_BY_COLS)
             for i, s in enumerate(group):
                 acc[pattern_ref[s, 0, b]] += part[:, i * LANES : (i + 1) * LANES]
@@ -88,18 +112,13 @@
             outer = w_ref[b, own].astype(F32)
             for s in range(own + 1, slots):
                 outer = outer + w_ref[b, s].astype(F32)
-            rows = rows + meta_ref[8 + b // RIM].astype(F32) * outer
-        high = rows.astype(BF16)
-        rest = rows - high.astype(F32)
-        mid = rest.astype(BF16)
-        low = (rest - mid.astype(F32)).astype(BF16)
-        total = mm(wide_ones, beside([high, mid, low]), ROWS_BY_ROWS)
-        deg_ref[b : b + 1] = total[0:1]
+            rows = rows + by_rim[b // RIM].astype(F32) * outer
+        deg_ref[b : b + 1] = jnp.sum(rows, axis=1, keepdims=True).T
     for b in range(blocks):
         deg_ref[b : b + 1] += acc[b, 0:1]
 
 
-def send_out(u_ref, w_ref, pattern_ref, meta_ref, terms, pay_refs):
+def send_out(shape, u_ref, w_ref, pattern_ref, terms, pay_refs):
     blocks, slots = w_ref.shape[:2]
     terms[...] = jnp.zeros_like(terms)
     for b in range(RIMS * RIM):
@@ -108,17 +127,19 @@
         for s in range(INNER, slots):
             i = s - INNER
             terms[base + pattern_ref[s, 0, b]] += part[:, i * LANES : (i + 1) * LANES]
+    rim_of, _, _ = places(shape)
     for m in range(4):
-        first = meta_ref[m] * RIM
+        first = rim_of[m] * RIM
         pay_refs[m][0:RIM] = u_ref[pl.ds(first, RIM)]
         pay_refs[m][RIM:] = terms[pl.ds(first, RIM)].astype(BF16)
 
 
-def first_scaled(pattern_ref, meta_ref, w_ref, deg_ref, x_ref, *refs):
+def first_scaled(shape, pattern_ref, w_ref, deg_ref, x_ref, *refs):
     in_refs, (inv_ref, u_ref), pay_refs, (rims, terms) = refs[:4], refs[4:6], refs[6:10], refs[10:]
     blocks = w_ref.shape[0]
+    rim_of, live_of, _ = places(shape)
     for m in range(4):
-        rims[meta_ref[m]] = in_refs[m][...] * meta_ref[4 + m].astype(F32)
+        rims[rim_of[m]] = in_refs[m][...] * live_of[m].astype(F32)
     for b in range(blocks):
         degree = deg_ref[b : b + 1]
         if b < RIMS * RIM:
@@ -126,16 +147,18 @@
         inv = 1.0 / jnp.sqrt(0.5 * degree)
         inv_ref[b : b + 1] = inv
         u_ref[b] = (inv * x_ref[:, column(b)].astype(F32)).astype(BF16)
-    send_out(u_ref, w_ref, pattern_ref, meta_ref, terms, pay_refs)
+    send_out(shape, u_ref, w_ref, pattern_ref, terms, pay_refs)
 
 
 def own_products(pattern_ref, w_ref, turned, u_ref, acc_ref):
     blocks, slots = w_ref.shape[:2]
-    acc_ref[...] = jnp.zeros_like(acc_ref)
+    for b in range(blocks):
+        both = mm(u_ref[b], beside([w_ref[b, 0], turned(b, 0)]), ROWS_BY_COLS)
+        acc_ref[b] = both[:, :LANES] + both[:, LANES:]
     for b in range(blocks):
         total = None
         own = INNER if b < RIMS * RIM else slots
-        for group in slot_pairs(0, own):
+        for group in slot_pairs(1, own):
             part = mm(u_ref[b], beside([w_ref[b, s] for s in group]), ROWS_BY_COLS)
             for i, s in enumerate(group):
                 acc_ref[pattern_ref[s, 0, b]] += part[:, i * LANES : (i + 1) * LANES]
@@ -163,19 +186,15 @@
             turned(b, s)
 
 
-def combine(step, pattern_ref, meta_ref, turned_ref, inv_ref, acc_ref, in_refs, y_ref, before_ref, next_ref, ext, u_ref):
+def combine(
+    shape, step, pattern_ref, turned_ref, inv_ref, acc_ref, in_refs, y_ref, before_ref, next_ref, ext, u_ref
+):
     blocks, slots = turned_ref.shape[:2]
+    rim_of, live_of, _ = places(shape)
     for m in range(4):
-        live = meta_ref[4 + m].astype(BF16)
-        first = meta_ref[m] * 2 * RIM
-        ext[pl.ds(first, 2 * RIM)] = in_refs[m][...] * live
-    for b in range(blocks):
-        total = acc_ref[b]
-        if b < RIMS * RIM:
-            base = (b // RIM) * 2 * RIM
-            ahead = beside([ext[base + pattern_ref[s, 0, b] - blocks] for s in range(INNER, slots)])
-            total = total + mm(ahead, over([turned_ref[b, s] for s in range(INNER, slots)]), ROWS_BY_COLS)
-            total = total + ext[base + RIM + b % RIM].astype(F32)
+        ext[pl.ds(rim_of[m] * 2 * RIM, 2 * RIM)] = in_refs[m][...] * live_of[m].astype(BF16)
+
+    def update(b, total):
         inv = inv_ref[b : b + 1]
         y = y_ref[:, column(b)].astype(F32)
         lap = y - inv * (0.5 * total)
@@ -186,17 +205,27 @@
         if u_ref is not None:
             u_ref[b] = (inv * new).astype(BF16)
 
-
-def advance(step, pattern_ref, meta_ref, w_ref, turned_ref, inv_ref, acc_ref, *refs):
+    for b in range(RIMS * RIM, blocks):
+        update(b, acc_ref[b])
+    for b in range(RIMS * RIM):
+        base = (b // RIM) * 2 * RIM
+        ahead = beside([ext[base + pattern_ref[s, 0, b] - blocks] for s in range(INNER, slots)])
+        ahead = mm(ahead, over([turned_ref[b, s] for s in range(INNER, slots)]), ROWS_BY_COLS)
+        update(b, acc_ref[b] + ahead + ext[base + RIM + b % RIM].astype(F32))
+
+
+def advance(shape, step, pattern_ref, w_ref, turned_ref, inv_ref, acc_ref, *refs):
     in_refs, (y_ref, before_ref, next_ref, u_ref) = refs[:4], refs[4:8]
     pay_refs, (ext, terms) = refs[8:12], refs[12:]
-    combine(step, pattern_ref, meta_ref, turned_ref, inv_ref, acc_ref, in_refs, y_ref, before_ref, next_ref, ext, u_ref)
-    send_out(u_ref, w_ref, pattern_ref, meta_ref, terms, pay_refs)
-
-
-def finish(pattern_ref, meta_ref, turned_ref, inv_ref, acc_ref, *refs):
+    combine(
+        shape, step, pattern_ref, turned_ref, inv_ref, acc_ref, in_refs, y_ref, before_ref, next_ref, ext, u_ref
+    )
+    send_out(shape, u_ref, w_ref, pattern_ref, terms, pay_refs)
+
+
+def finish(shape, pattern_ref, turned_ref, inv_ref, acc_ref, *refs):
     in_refs, (y_ref, before_ref, next_ref, gram_ref, ext) = refs[:4], refs[4:]
-    combine(2, pattern_ref, meta_ref, turned_ref, inv_ref, acc_ref, in_refs, y_ref, before_ref, next_ref, ext, None)
+    combine(shape, 2, pattern_ref, turned_ref, inv_ref, acc_ref, in_refs, y_ref, before_ref, next_ref, ext, None)
     y = next_ref[...]
     gram = mm(y, y, ROWS_BY_ROWS, lax.Precision.HIGHEST)
     packed = beside([gram[8 * i : 8 * i + 8] for i in range(gram.shape[0] // 8)])
@@ -270,9 +299,12 @@
     return pl.pallas_call(
         body,
         name=name,
-        out_shape=[pltpu.VMEM(s, d) if len(s) == 4 else jax.ShapeDtypeStruct(s, d) for s, d in outs],
+        out_shape=[
+            pltpu.SMEM(s, d) if d == jnp.int32 else pltpu.VMEM(s, d) if len(s) == 4 else jax.ShapeDtypeStruct(s, d)
+            for s, d in outs
+        ],
         in_specs=specs,
-        out_specs=[pl.BlockSpec(memory_space=pltpu.VMEM)] * len(outs),
+        out_specs=[pl.BlockSpec(memory_space=pltpu.SMEM if d == jnp.int32 else pltpu.VMEM) for _, d in outs],
         scratch_shapes=list(scratch),
         compiler_params=pltpu.CompilerParams(vmem_limit_bytes=16 << 20),
         cost_estimate=pl.CostEstimate(flops=flops, bytes_accessed=moved, transcendentals=0),
@@ -312,50 +344,38 @@
     return [lax.ppermute(payload, ("narrow", "wide"), pairs[m]) for payload, m in zip(payloads, ORDER)]
 
 
-def placement():
-    sends, live, by_rim = [], [], []
-    for a, axis in enumerate(("narrow", "wide")):
-        place = lax.axis_index(axis)
-        last = lax.axis_size(axis) - 1
-        for m in (0, 1):
-            after = (place + m) % 2 == 0
-            sends.append(2 * a + after.astype(jnp.int32))
-            live.append(jnp.where(after, place < last, place > 0).astype(jnp.int32))
-        by_rim += [(place > 0).astype(jnp.int32), (place < last).astype(jnp.int32)]
-    return jnp.stack([sends[m] for m in ORDER] + [live[m] for m in ORDER] + by_rim)
-
-
 def body(start_block, weights, pattern):
     x = start_block[0, 0]
     w = weights[0, 0]
     slots_of = jnp.transpose(pattern, (0, 3, 1, 2))[0]
-    meta = placement()
+    shape = (lax.axis_size("narrow"), lax.axis_size("wide"))
     vecs, docs = x.shape
     blocks, slots = w.shape[:2]
     rows = RIMS * RIM
-    ids = [("smem", slots_of), ("smem", meta)]
     tile = ((blocks, vecs, LANES), F32)
     scaled = ((blocks, vecs, LANES), BF16)
     full = ((vecs, docs), F32)
     payload = [((2 * RIM, vecs, LANES), BF16)] * 4
     per_block = 2 * LANES * LANES
 
-    pays = kernel_call(
-        outgoing_ones, "outgoing_ones", ids[1:] + [("hbm", slots_of), ("hbm", w)], [((8, LANES), F32)] * 4,
-        [pltpu.VMEM((rows, slots - INNER, LANES, LANES), BF16), pltpu.SMEM(slots_of.shape, jnp.int32),
-         pltpu.VMEM((RIMS, 8, LANES), F32), pltpu.SemaphoreType.DMA((RIMS + 1,))],
+    *pays, slots_of = kernel_call(
+        functools.partial(outgoing_ones, shape), "outgoing_ones", [("hbm", slots_of), ("hbm", w)],
+        [((8, LANES), F32)] * 4 + [(slots_of.shape, jnp.int32)],
+        [pltpu.VMEM((rows, slots - INNER, LANES, LANES), BF16),
+         pltpu.VMEM((rows, 8, LANES), F32), pltpu.SemaphoreType.DMA((RIMS + 1,))],
         flops=rows * 3 * per_block * 32, moved=1 << 20,
     )
     w, *pays = lax.optimization_barrier((w, *pays))
-    held = ids + [("held", w)]
+    names = [("smem", slots_of)]
+    held = names + [("held", w)]
     (degree,) = kernel_call(
-        local_degree, "local_degree", held, [((blocks, LANES), F32)],
+        functools.partial(local_degree, shape), "local_degree", held, [((blocks, LANES), F32)],
         [pltpu.VMEM((blocks, 8, LANES), F32)],
         flops=blocks * slots * per_block * 32, moved=8 << 20,
     )
     got = exchange(pays)
     inv, u, *pays = kernel_call(
-        first_scaled, "first_scaled",
+        functools.partial(first_scaled, shape), "first_scaled",
         held + [("vmem", degree), ("vmem", x)] + [("vmem", g) for g in got],
         [((blocks, LANES), F32), scaled] + payload,
         [pltpu.VMEM((RIMS, 8, LANES), F32), pltpu.VMEM((rows, vecs, LANES), F32)],
@@ -366,11 +386,12 @@
         cost = dict(flops=2 * blocks * slots * per_block * vecs, moved=8 << 20)
         if step == 0:
             acc, turned = kernel_call(
-                own_terms_turning, "own_terms_turning", ids[:1] + [("held", w), ("vmem", u)], [tile, (w.shape, BF16)], **cost
+                own_terms_turning, "own_terms_turning", held + [("vmem", u)], [tile, (w.shape, BF16)],
+                **cost
             )
         else:
             (acc,) = kernel_call(
-                own_terms, "own_terms", ids[:1] + [("held", w), ("held", turned), ("vmem", u)], [tile], **cost
+                own_terms, "own_terms", held + [("held", turned), ("vmem", u)], [tile], **cost
             )
         got = exchange(pays)
         common = [("held", turned), ("vmem", inv), ("vmem", acc)] + [("vmem", g) for g in got]
@@ -378,14 +399,15 @@
         ext = pltpu.VMEM((2 * rows, vecs, LANES), BF16)
         if step < 2:
             new, u, *pays = kernel_call(
-                functools.partial(advance, step), "advance", held + common, [full, scaled] + payload,
+                functools.partial(advance, shape, step), "advance", held + common, [full, scaled] + payload,
                 [ext, pltpu.VMEM((rows, vecs, LANES), F32)],
                 flops=2 * rows * 3 * per_block * 32, moved=1 << 20,
             )
         else:
-            peers = lax.axis_size("narrow") * lax.axis_size("wide")
+            peers = shape[0] * shape[1]
             new, grams = kernel_call(
-                finish, "finish", ids + common, [full, ((peers, 8, LANES), F32)], [ext],
+                functools.partial(finish, shape), "finish", names + common, [full, ((peers, 8, LANES), F32)],
+                [ext],
                 flops=rows * 3 * per_block * 32, moved=1 << 20,
             )
         before, y = y, new

time: 55.5 us -> 51.4 us (0.926)
  Pallas kernels: 26.2 us -> 19.7 us
  blocking collectives: 10.7 us -> 12 us
  waiting for transfers between devices: 0.04 us -> 0.83 us
    pallas_call x10, Pallas kernels: 26.2 us -> 19.7 us  [kernel_call(): pl.pallas_call(body, name=name, out_shape=[pltpu.SMEM(s, d) if d == jnp.i...]
    all_to_all x1, blocking collectives: 10.7 us -> 12 us  [body(): grams = lax.all_to_all(grams, ('narrow', 'wide'), 0, 0)]
    ppermute x16, waiting for transfers between devices: 0.04 us -> 0.83 us  [exchange(): lax.ppermute(payload, ('narrow', 'wide'), pairs[m])]
  transfers between devices with their start and end apart: 16 -> 16, of which waited for: 0 -> 2; matrix products, arithmetic and copies ran while one was open for 0% -> 0% of each run, Pallas kernels for 26% -> 22%
where the time goes in v3:
time: 51.4 us; the launch traced here: 51.2 us
  Pallas kernels  19.7 us (38%)
  starting transfers between devices  18.5 us (36%)
  blocking collectives  12 us (23%)
  waiting for transfers between devices  0.83 us (2%)
    pallas_call x10, Pallas kernels, kernel_call(): pl.pallas_call(body, name=name, out_shape=[pltpu.SMEM(s, d) if d == jnp.i...  19.7 us
    ppermute x16, starting transfers between devices, exchange(): lax.ppermute(payload, ('narrow', 'wide'), pairs[m])  18.5 us
    all_to_all x1, blocking collectives, body(): grams = lax.all_to_all(grams, ('narrow', 'wide'), 0, 0)  12 us
  transfers between devices with their start and end apart: 16, of which 2 were waited for; matrix products, arithmetic and copies ran while one was open for 0% of the time, Pallas kernels for 22%

profile of v3, /device:TPU:0, one launch (start us, length us, event | category | flops | bytes accessed | tf_op | source)
XLA Modules:
  0.0 51.2 jit_solution(9741715007235292493)
XLA Ops:
  0.0 0.0 copy-start
  0.0 0.0 copy-start.1
  0.0 2.2 %outgoing_ones.1 = (f32[8,128]{1,0:T(8,128)S(1)}, f32[8,128]{1,0:T(8,128)S(1)}, f32[8,128]{1,0:T(8,128)S(1)}, f32[8,128]{1,0:T(8,128)S(1)}, s32[12,1,28]{2,1,0:T(1,128)S(4)}) custom-call(s32[12,1,28]{2,1,0:T(1,128)} %bitcast.18, bf16[28,12,128,128]{3,2,1,0:T(8,128)(2,1)} %bitcast.6), custom_call_target="tpu_custom_call" | custom-call | flops 75497472 | bytes 1048576 | tf_op jit(solution)/shard_map/outgoing_ones/pallas_call | solution.py:299
  2.2 0.5 collective-permute-start
  2.7 2.6 %collective-permute-start.1 = (f32[8,128]{1,0:T(8,128)S(1)}, f32[8,128]{1,0:T(8,128)S(1)}, u32[]{:S(2)}, u32[]{:S(2)}) collective-permute-start(f32[8,128]{1,0:T(8,128)S(1)} %get-tuple-element.44), channel_id=1, source_target_pairs={{8,16},{16,8},{9,17},{17,9},{10,18},{18,10},{11,19},{19,11},{12,20... | collective-permute-start | bytes 12296 | tf_op jit(solution)/shard_map/ppermute | solution.py:344
  5.3 2.1 %collective-permute-start.2 = (f32[8,128]{1,0:T(8,128)S(1)}, f32[8,128]{1,0:T(8,128)S(1)}, u32[]{:S(2)}, u32[]{:S(2)}) collective-permute-start(f32[8,128]{1,0:T(8,128)S(1)} %get-tuple-element.45), channel_id=1, source_target_pairs={{0,1},{1,0},{2,3},{3,2},{4,5},{5,4},{6,7},{7,6},{8,9},{9,8},{10,11... | collective-permute-start | bytes 12296 | tf_op jit(solution)/shard_map/ppermute | solution.py:344
  7.4 0.7 %collective-permute-start.3 = (f32[8,128]{1,0:T(8,128)S(1)}, f32[8,128]{1,0:T(8,128)S(1)}, u32[]{:S(2)}, u32[]{:S(2)}) collective-permute-start(f32[8,128]{1,0:T(8,128)S(1)} %get-tuple-element.46), channel_id=1, source_target_pairs={{0,8},{8,0},{16,24},{24,16},{1,9},{9,1},{17,25},{25,17},{2,10},{10... | collective-permute-start | bytes 12296 | tf_op jit(solution)/shard_map/ppermute | solution.py:344
  8.1 0.0 copy-done
  8.1 2.0 %local_degree.1.deg_ref = f32[28,128]{1,0:T(8,128)S(1)} custom-call(s32[12,1,28]{2,1,0:T(1,128)S(4)} %get-tuple-element.37.pattern_ref, bf16[28,12,128,128]{3,2,1,0:T(8,128)(2,1)S(1)} %bitcast.7), custom_call_target="tpu_custom_call" | custom-call | flops 352321536 | bytes 8388608 | tf_op jit(solution)/shard_map/local_degree/pallas_call | solution.py:299
  10.1 0.0 collective-permute-done.refs_0_
  10.1 0.0 collective-permute-done.1.refs_1_
  10.1 0.0 collective-permute-done.2.refs_2_
  10.1 0.0 collective-permute-done.3.refs_3_
  10.1 0.0 copy-done.1
  10.1 0.6 %first_scaled.1 = (f32[28,128]{1,0:T(8,128)S(1)}, bf16[28,32,128]{2,1,0:T(8,128)(2,1)S(1)}, bf16[12,32,128]{2,1,0:T(8,128)(2,1)S(1)}, bf16[12,32,128]{2,1,0:T(8,...) custom-call(s32[12,1,28]{2,1,0:T(1,128)S(4)} %get-tuple-element.37.pattern_ref, ...), custom_call_target="tpu_custom_call" | custom-call | flops 75497472 | bytes 1048576 | tf_op jit(solution)/shard_map/first_scaled/pallas_call | solution.py:299
  10.8 0.1 collective-permute-start.4
  10.9 0.6 %collective-permute-start.5 = (bf16[12,32,128]{2,1,0:T(8,128)(2,1)S(1)}, bf16[12,32,128]{2,1,0:T(8,128)(2,1)S(1)}, u32[]{:S(2)}, u32[]{:S(2)}) collective-permute-start(bf16[12,32,128]{2,1,0:T(8,128)(2,1)S(1)} %get-tuple-element.52), channel_id=1, source_target_pairs={{8,16},{16,8},{9,17},{17,9},{10,18},{18,10},{11,19},{19,11},{12,20... | collective-permute-start | bytes 294920 | tf_op jit(solution)/shard_map/ppermute | solution.py:344
  11.5 2.4 %collective-permute-start.6 = (bf16[12,32,128]{2,1,0:T(8,128)(2,1)S(1)}, bf16[12,32,128]{2,1,0:T(8,128)(2,1)S(1)}, u32[]{:S(2)}, u32[]{:S(2)}) collective-permute-start(bf16[12,32,128]{2,1,0:T(8,128)(2,1)S(1)} %get-tuple-element.53), channel_id=1, source_target_pairs={{0,1},{1,0},{2,3},{3,2},{4,5},{5,4},{6,7},{7,6},{8,9},{9,8},{10,11... | collective-permute-start | bytes 294920 | tf_op jit(solution)/shard_map/ppermute | solution.py:344
  13.9 0.3 collective-permute-start.7
  14.2 3.3 %own_terms_turning.1 = (f32[28,32,128]{2,1,0:T(8,128)S(1)}, bf16[28,12,128,128]{3,2,1,0:T(8,128)(2,1)S(1)}) custom-call(s32[12,1,28]{2,1,0:T(1,128)S(4)} %get-tuple-element.37.pattern_ref, bf16[28,12,128,128]{3,2,1,0:T(8,128)(2,1)S(1)} %bitcast.9, bf16[28,32,128]{2,1,0:T(8,128)(2,1)S(1)} %get-tuple-element.47.u_ref), custom_call_target="tpu_custom_call" | custom-call | flops 704643072 | bytes 8388608 | tf_op jit(solution)/shard_map/own_terms_turning/pallas_call | solution.py:299
  17.6 0.0 collective-permute-done.4.refs_0_
  17.6 0.0 collective-permute-done.5.refs_1_
  17.6 0.0 collective-permute-done.6.refs_2_
  17.6 0.0 collective-permute-done.7.refs_3_
  17.6 1.1 %advance.2 = (f32[32,3584]{1,0:T(8,128)S(1)}, bf16[28,32,128]{2,1,0:T(8,128)(2,1)S(1)}, bf16[12,32,128]{2,1,0:T(8,128)(2,1)S(1)}, bf16[12,32,128]{2,1,0:T(8,128)...) custom-call(s32[12,1,28]{2,1,0:T(1,128)S(4)} %get-tuple-element.37.pattern_ref, ...), custom_call_target="tpu_custom_call" | custom-call | flops 150994944 | bytes 1048576 | tf_op jit(solution)/shard_map/advance/pallas_call | solution.py:299
  18.7 0.3 collective-permute-start.8
  19.0 1.4 %collective-permute-start.9 = (bf16[12,32,128]{2,1,0:T(8,128)(2,1)S(1)}, bf16[12,32,128]{2,1,0:T(8,128)(2,1)S(1)}, u32[]{:S(2)}, u32[]{:S(2)}) collective-permute-start(bf16[12,32,128]{2,1,0:T(8,128)(2,1)S(1)} %get-tuple-element.57), channel_id=1, source_target_pairs={{8,16},{16,8},{9,17},{17,9},{10,18},{18,10},{11,19},{19,11},{12,20... | collective-permute-start | bytes 294920 | tf_op jit(solution)/shard_map/ppermute | solution.py:344
  20.4 2.5 %collective-permute-start.10 = (bf16[12,32,128]{2,1,0:T(8,128)(2,1)S(1)}, bf16[12,32,128]{2,1,0:T(8,128)(2,1)S(1)}, u32[]{:S(2)}, u32[]{:S(2)}) collective-permute-start(bf16[12,32,128]{2,1,0:T(8,128)(2,1)S(1)} %get-tuple-element.58), channel_id=1, source_target_pairs={{0,1},{1,0},{2,3},{3,2},{4,5},{5,4},{6,7},{7,6},{8,9},{9,8},{10,11... | collective-permute-start | bytes 294920 | tf_op jit(solution)/shard_map/ppermute | solution.py:344
  22.9 0.4 collective-permute-start.11
  23.2 2.8 %own_terms.2.acc_ref = f32[28,32,128]{2,1,0:T(8,128)S(1)} custom-call(s32[12,1,28]{2,1,0:T(1,128)S(4)} %get-tuple-element.37.pattern_ref, bf16[28,12,128,128]{3,2,1,0:T(8,128)(2,1)S(1)} %bitcast.11, bf16[28,12,128,128]{3,2,1,0:T(8,128)(2,1)S(1)} %get-tuple-element.48.turned_ref, bf16[28,32,128]{2,1,0:T(8,128)(2,1)S(1)} %get-tuple-element.55.u_ref), custom_call_target="tpu_custom_call" | custom-call | flops 704643072 | bytes 8388608 | tf_op jit(solution)/shard_map/own_terms/pallas_call | solution.py:299
  26.1 0.0 collective-permute-done.8.refs_0_
  26.1 0.0 collective-permute-done.9.refs_1_
  26.1 0.4 collective-permute-done.10.refs_2_
  26.5 0.0 collective-permute-done.11.refs_3_
  26.5 1.3 %advance.3 = (f32[32,3584]{1,0:T(8,128)S(1)}, bf16[28,32,128]{2,1,0:T(8,128)(2,1)S(1)}, bf16[12,32,128]{2,1,0:T(8,128)(2,1)S(1)}, bf16[12,32,128]{2,1,0:T(8,128)...) custom-call(s32[12,1,28]{2,1,0:T(1,128)S(4)} %get-tuple-element.37.pattern_ref, ...), custom_call_target="tpu_custom_call" | custom-call | flops 150994944 | bytes 1048576 | tf_op jit(solution)/shard_map/advance/pallas_call | solution.py:299
  27.8 0.2 collective-permute-start.12
  27.9 1.4 %collective-permute-start.13 = (bf16[12,32,128]{2,1,0:T(8,128)(2,1)S(1)}, bf16[12,32,128]{2,1,0:T(8,128)(2,1)S(1)}, u32[]{:S(2)}, u32[]{:S(2)}) collective-permute-start(bf16[12,32,128]{2,1,0:T(8,128)(2,1)S(1)} %get-tuple-element.63), channel_id=1, source_target_pairs={{8,16},{16,8},{9,17},{17,9},{10,18},{18,10},{11,19},{19,11},{12,20... | collective-permute-start | bytes 294920 | tf_op jit(solution)/shard_map/ppermute | solution.py:344
  29.3 2.7 %collective-permute-start.14 = (bf16[12,32,128]{2,1,0:T(8,128)(2,1)S(1)}, bf16[12,32,128]{2,1,0:T(8,128)(2,1)S(1)}, u32[]{:S(2)}, u32[]{:S(2)}) collective-permute-start(bf16[12,32,128]{2,1,0:T(8,128)(2,1)S(1)} %get-tuple-element.64), channel_id=1, source_target_pairs={{0,1},{1,0},{2,3},{3,2},{4,5},{5,4},{6,7},{7,6},{8,9},{9,8},{10,11... | collective-permute-start | bytes 294920 | tf_op jit(solution)/shard_map/ppermute | solution.py:344
  32.0 0.4 collective-permute-start.15
  32.4 2.8 %own_terms.3.acc_ref = f32[28,32,128]{2,1,0:T(8,128)S(1)} custom-call(s32[12,1,28]{2,1,0:T(1,128)S(4)} %get-tuple-element.37.pattern_ref, bf16[28,12,128,128]{3,2,1,0:T(8,128)(2,1)S(1)} %bitcast.13, bf16[28,12,128,128]{3,2,1,0:T(8,128)(2,1)S(1)} %get-tuple-element.48.turned_ref, bf16[28,32,128]{2,1,0:T(8,128)(2,1)S(1)} %get-tuple-element.61.u_ref), custom_call_target="tpu_custom_call" | custom-call | flops 704643072 | bytes 8388608 | tf_op jit(solution)/shard_map/own_terms/pallas_call | solution.py:299
  35.2 0.0 collective-permute-done.12.refs_0_
  35.2 0.0 collective-permute-done.13.refs_1_
  35.3 0.4 collective-permute-done.14.refs_2_
  35.7 0.0 collective-permute-done.15.refs_3_
  35.7 1.3 %finish.1 = (f32[32,3584]{1,0:T(8,128)S(1)}, f32[32,8,128]{2,1,0:T(8,128)S(1)}) custom-call(s32[12,1,28]{2,1,0:T(1,128)S(4)} %get-tuple-element.37.pattern_ref, bf16[28,12,128,128]{3,2,1,0:T(8,128)(2,1)S(1)} %get-tuple-element.48.turned_ref, f32[28,128]{1,0:T(8,128)S(1)} %get-tuple-element.49.inv_ref, f32[28,32,128]{2,1,0:T(8,128)S(1)} %own_terms.3.acc_ref, ...), custom_call_target="tpu_custom_call" | custom-call | flops 75497472 | bytes 1048576 | tf_op jit(solution)/shard_map/finish/pallas_call | solution.py:299
  37.0 12.0 %all_to_all.5.grams_ref = f32[32,8,128]{2,1,0:T(8,128)S(1)} all-to-all(f32[32,8,128]{2,1,0:T(8,128)S(1)} %get-tuple-element.67), channel_id=1, replica_groups=mesh['narrow'=4,'wide'=8] {'narrow','wide'}, dimensions={0} | all-to-all | bytes 262144 | tf_op jit(solution)/shard_map/all_to_all | solution.py:414
  49.0 2.2 %orthonormal.1 = f32[32,3584]{1,0:T(8,128)} custom-call(f32[32,8,128]{2,1,0:T(8,128)S(1)} %all_to_all.5.grams_ref, f32[32,3584]{1,0:T(8,128)S(1)} %get-tuple-element.68.y_ref), custom_call_target="tpu_custom_call" | custom-call | tf_op jit(solution)/shard_map/orthonormal/pallas_call | solution.py:299
Async XLA Ops:
  0.0 8.1 %copy-start = (bf16[1,1,28,12,128,128]{5,4,3,2,1,0:T(8,128)(2,1)S(1)}, bf16[1,1,28,12,128,128]{5,4,3,2,1,0:T(8,128)(2,1)}, u32[]{:S(2)}) copy-start(bf16[1,1,28,12,128,128]{5,4,3,2,1,0:T(8,128)(2,1)} %param.4) | copy-start | bytes 33030148
  0.0 10.1 %copy-start.1 = (bf16[1,1,32,3584]{3,2,1,0:T(8,128)(2,1)S(1)}, bf16[1,1,32,3584]{3,2,1,0:T(8,128)(2,1)}, u32[]{:S(2)}) copy-start(bf16[1,1,32,3584]{3,2,1,0:T(8,128)(2,1)} %param.3) | copy-start | bytes 688132
  2.2 7.9 %collective-permute-start = (f32[8,128]{1,0:T(8,128)S(1)}, f32[8,128]{1,0:T(8,128)S(1)}, u32[]{:S(2)}, u32[]{:S(2)}) collective-permute-start(f32[8,128]{1,0:T(8,128)S(1)} %get-tuple-element.43), channel_id=1, source_target_pairs={{1,2},{2,1},{3,4},{4,3},{5,6},{6,5},{9,10},{10,9},{11,12},{12,11},... | collective-permute-start | bytes 12296 | tf_op jit(solution)/shard_map/ppermute | solution.py:344
  2.7 7.4 %collective-permute-start.1 = (f32[8,128]{1,0:T(8,128)S(1)}, f32[8,128]{1,0:T(8,128)S(1)}, u32[]{:S(2)}, u32[]{:S(2)}) collective-permute-start(f32[8,128]{1,0:T(8,128)S(1)} %get-tuple-element.44), channel_id=1, source_target_pairs={{8,16},{16,8},{9,17},{17,9},{10,18},{18,10},{11,19},{19,11},{12,20... | collective-permute-start | bytes 12296 | tf_op jit(solution)/shard_map/ppermute | solution.py:344
  5.3 4.8 %collective-permute-start.2 = (f32[8,128]{1,0:T(8,128)S(1)}, f32[8,128]{1,0:T(8,128)S(1)}, u32[]{:S(2)}, u32[]{:S(2)}) collective-permute-start(f32[8,128]{1,0:T(8,128)S(1)} %get-tuple-element.45), channel_id=1, source_target_pairs={{0,1},{1,0},{2,3},{3,2},{4,5},{5,4},{6,7},{7,6},{8,9},{9,8},{10,11... | collective-permute-start | bytes 12296 | tf_op jit(solution)/shard_map/ppermute | solution.py:344
  7.4 2.7 %collective-permute-start.3 = (f32[8,128]{1,0:T(8,128)S(1)}, f32[8,128]{1,0:T(8,128)S(1)}, u32[]{:S(2)}, u32[]{:S(2)}) collective-permute-start(f32[8,128]{1,0:T(8,128)S(1)} %get-tuple-element.46), channel_id=1, source_target_pairs={{0,8},{8,0},{16,24},{24,16},{1,9},{9,1},{17,25},{25,17},{2,10},{10... | collective-permute-start | bytes 12296 | tf_op jit(solution)/shard_map/ppermute | solution.py:344
  10.8 6.8 %collective-permute-start.4 = (bf16[12,32,128]{2,1,0:T(8,128)(2,1)S(1)}, bf16[12,32,128]{2,1,0:T(8,128)(2,1)S(1)}, u32[]{:S(2)}, u32[]{:S(2)}) collective-permute-start(bf16[12,32,128]{2,1,0:T(8,128)(2,1)S(1)} %get-tuple-element.51), channel_id=1, source_target_pairs={{1,2},{2,1},{3,4},{4,3},{5,6},{6,5},{9,10},{10,9},{11,12},{12,11},... | collective-permute-start | bytes 294920 | tf_op jit(solution)/shard_map/ppermute | solution.py:344
  10.9 6.7 %collective-permute-start.5 = (bf16[12,32,128]{2,1,0:T(8,128)(2,1)S(1)}, bf16[12,32,128]{2,1,0:T(8,128)(2,1)S(1)}, u32[]{:S(2)}, u32[]{:S(2)}) collective-permute-start(bf16[12,32,128]{2,1,0:T(8,128)(2,1)S(1)} %get-tuple-element.52), channel_id=1, source_target_pairs={{8,16},{16,8},{9,17},{17,9},{10,18},{18,10},{11,19},{19,11},{12,20... | collective-permute-start | bytes 294920 | tf_op jit(solution)/shard_map/ppermute | solution.py:344
  11.5 6.1 %collective-permute-start.6 = (bf16[12,32,128]{2,1,0:T(8,128)(2,1)S(1)}, bf16[12,32,128]{2,1,0:T(8,128)(2,1)S(1)}, u32[]{:S(2)}, u32[]{:S(2)}) collective-permute-start(bf16[12,32,128]{2,1,0:T(8,128)(2,1)S(1)} %get-tuple-element.53), channel_id=1, source_target_pairs={{0,1},{1,0},{2,3},{3,2},{4,5},{5,4},{6,7},{7,6},{8,9},{9,8},{10,11... | collective-permute-start | bytes 294920 | tf_op jit(solution)/shard_map/ppermute | solution.py:344
  13.9 3.7 %collective-permute-start.7 = (bf16[12,32,128]{2,1,0:T(8,128)(2,1)S(1)}, bf16[12,32,128]{2,1,0:T(8,128)(2,1)S(1)}, u32[]{:S(2)}, u32[]{:S(2)}) collective-permute-start(bf16[12,32,128]{2,1,0:T(8,128)(2,1)S(1)} %get-tuple-element.54), channel_id=1, source_target_pairs={{0,8},{8,0},{16,24},{24,16},{1,9},{9,1},{17,25},{25,17},{2,10},{10... | collective-permute-start | bytes 294920 | tf_op jit(solution)/shard_map/ppermute | solution.py:344
  18.7 7.3 %collective-permute-start.8 = (bf16[12,32,128]{2,1,0:T(8,128)(2,1)S(1)}, bf16[12,32,128]{2,1,0:T(8,128)(2,1)S(1)}, u32[]{:S(2)}, u32[]{:S(2)}) collective-permute-start(bf16[12,32,128]{2,1,0:T(8,128)(2,1)S(1)} %get-tuple-element.56), channel_id=1, source_target_pairs={{1,2},{2,1},{3,4},{4,3},{5,6},{6,5},{9,10},{10,9},{11,12},{12,11},... | collective-permute-start | bytes 294920 | tf_op jit(solution)/shard_map/ppermute | solution.py:344
  19.0 7.1 %collective-permute-start.9 = (bf16[12,32,128]{2,1,0:T(8,128)(2,1)S(1)}, bf16[12,32,128]{2,1,0:T(8,128)(2,1)S(1)}, u32[]{:S(2)}, u32[]{:S(2)}) collective-permute-start(bf16[12,32,128]{2,1,0:T(8,128)(2,1)S(1)} %get-tuple-element.57), channel_id=1, source_target_pairs={{8,16},{16,8},{9,17},{17,9},{10,18},{18,10},{11,19},{19,11},{12,20... | collective-permute-start | bytes 294920 | tf_op jit(solution)/shard_map/ppermute | solution.py:344
  20.4 6.1 %collective-permute-start.10 = (bf16[12,32,128]{2,1,0:T(8,128)(2,1)S(1)}, bf16[12,32,128]{2,1,0:T(8,128)(2,1)S(1)}, u32[]{:S(2)}, u32[]{:S(2)}) collective-permute-start(bf16[12,32,128]{2,1,0:T(8,128)(2,1)S(1)} %get-tuple-element.58), channel_id=1, source_target_pairs={{0,1},{1,0},{2,3},{3,2},{4,5},{5,4},{6,7},{7,6},{8,9},{9,8},{10,11... | collective-permute-start | bytes 294920 | tf_op jit(solution)/shard_map/ppermute | solution.py:344
  22.9 3.6 %collective-permute-start.11 = (bf16[12,32,128]{2,1,0:T(8,128)(2,1)S(1)}, bf16[12,32,128]{2,1,0:T(8,128)(2,1)S(1)}, u32[]{:S(2)}, u32[]{:S(2)}) collective-permute-start(bf16[12,32,128]{2,1,0:T(8,128)(2,1)S(1)} %get-tuple-element.59), channel_id=1, source_target_pairs={{0,8},{8,0},{16,24},{24,16},{1,9},{9,1},{17,25},{25,17},{2,10},{10... | collective-permute-start | bytes 294920 | tf_op jit(solution)/shard_map/ppermute | solution.py:344
  27.8 7.5 %collective-permute-start.12 = (bf16[12,32,128]{2,1,0:T(8,128)(2,1)S(1)}, bf16[12,32,128]{2,1,0:T(8,128)(2,1)S(1)}, u32[]{:S(2)}, u32[]{:S(2)}) collective-permute-start(bf16[12,32,128]{2,1,0:T(8,128)(2,1)S(1)} %get-tuple-element.62), channel_id=1, source_target_pairs={{1,2},{2,1},{3,4},{4,3},{5,6},{6,5},{9,10},{10,9},{11,12},{12,11},... | collective-permute-start | bytes 294920 | tf_op jit(solution)/shard_map/ppermute | solution.py:344
  27.9 7.3 %collective-permute-start.13 = (bf16[12,32,128]{2,1,0:T(8,128)(2,1)S(1)}, bf16[12,32,128]{2,1,0:T(8,128)(2,1)S(1)}, u32[]{:S(2)}, u32[]{:S(2)}) collective-permute-start(bf16[12,32,128]{2,1,0:T(8,128)(2,1)S(1)} %get-tuple-element.63), channel_id=1, source_target_pairs={{8,16},{16,8},{9,17},{17,9},{10,18},{18,10},{11,19},{19,11},{12,20... | collective-permute-start | bytes 294920 | tf_op jit(solution)/shard_map/ppermute | solution.py:344
  29.3 6.4 %collective-permute-start.14 = (bf16[12,32,128]{2,1,0:T(8,128)(2,1)S(1)}, bf16[12,32,128]{2,1,0:T(8,128)(2,1)S(1)}, u32[]{:S(2)}, u32[]{:S(2)}) collective-permute-start(bf16[12,32,128]{2,1,0:T(8,128)(2,1)S(1)} %get-tuple-element.64), channel_id=1, source_target_pairs={{0,1},{1,0},{2,3},{3,2},{4,5},{5,4},{6,7},{7,6},{8,9},{9,8},{10,11... | collective-permute-start | bytes 294920 | tf_op jit(solution)/shard_map/ppermute | solution.py:344
  32.0 3.6 %collective-permute-start.15 = (bf16[12,32,128]{2,1,0:T(8,128)(2,1)S(1)}, bf16[12,32,128]{2,1,0:T(8,128)(2,1)S(1)}, u32[]{:S(2)}, u32[]{:S(2)}) collective-permute-start(bf16[12,32,128]{2,1,0:T(8,128)(2,1)S(1)} %get-tuple-element.65), channel_id=1, source_target_pairs={{0,8},{8,0},{16,24},{24,16},{1,9},{9,1},{17,25},{25,17},{2,10},{10... | collective-permute-start | bytes 294920 | tf_op jit(solution)/shard_map/ppermute | solution.py:344

commit v4 on v3

--- a/solution.py
+++ b/solution.py
@@ -11,6 +11,7 @@
 RIM = 6
 RIMS = 4
 INNER = 9
+PARTS = 3
 LANES = 128
 F32 = jnp.float32
 BF16 = jnp.bfloat16
@@ -23,8 +24,15 @@
 ROWS_BY_COLS = (((1,), (0,)), ((), ()))
 
 
-def mm(left, right, dims, precision=None):
-    return lax.dot_general(left, right, dims, precision=precision, preferred_element_type=F32)
+def mm(left, right, dims):
+    return lax.dot_general(left, right, dims, preferred_element_type=F32)
+
+
+def three(x):
+    high = x.astype(BF16)
+    rest = x - high.astype(F32)
+    mid = rest.astype(BF16)
+    return high, mid, (rest - mid.astype(F32)).astype(BF16)
 
 
 def beside(parts):
@@ -43,7 +51,7 @@
     return pl.ds(b * LANES, LANES)
 
 
-ORDER = (3, 1, 2, 0)
+ORDER = (2, 3, 1, 0)
 
 
 def places(shape):
@@ -69,22 +77,22 @@
 
 def outgoing_ones(shape, pattern_hbm, w_hbm, *refs):
     pay_refs, (pattern_ref, w_ref, sums, sems) = refs[:4], refs[4:]
-    named = fetch(pattern_hbm, pattern_ref, sems.at[RIMS])
+    named = fetch(pattern_hbm, pattern_ref, sems.at[PARTS])
     copies = []
-    for r in range(RIMS):
-        rows = pl.ds(r * RIM, RIM)
-        copies.append(fetch(w_hbm.at[rows, INNER:], w_ref.at[rows], sems.at[r]))
+    for part in range(PARTS):
+        rows = pl.ds(part * RIMS * RIM // PARTS, RIMS * RIM // PARTS)
+        copies.append(fetch(w_hbm.at[rows, INNER:], w_ref.at[rows], sems.at[part]))
     blocks = pattern_ref.shape[2]
     slots = w_ref.shape[1]
     sums[...] = jnp.zeros_like(sums)
     ones = jnp.ones((8, LANES), BF16)
     named.wait()
-    for r in range(RIMS):
-        copies[r].wait()
-        for b in range(r * RIM, (r + 1) * RIM):
+    for p in range(PARTS):
+        copies[p].wait()
+        for b in range(p * RIMS * RIM // PARTS, (p + 1) * RIMS * RIM // PARTS):
             part = mm(ones, beside([w_ref[b, s] for s in range(slots)]), ROWS_BY_COLS)
             for s in range(slots):
-                sums[r * RIM - blocks + pattern_ref[INNER + s, 0, b]] += part[:, s * LANES : (s + 1) * LANES]
+                sums[b // RIM * RIM - blocks + pattern_ref[INNER + s, 0, b]] += part[:, s * LANES : (s + 1) * LANES]
     rim_of, _, _ = places(shape)
     for m in range(4):
         for q in range(RIM):
@@ -226,8 +234,10 @@
 def finish(shape, pattern_ref, turned_ref, inv_ref, acc_ref, *refs):
     in_refs, (y_ref, before_ref, next_ref, gram_ref, ext) = refs[:4], refs[4:]
     combine(shape, 2, pattern_ref, turned_ref, inv_ref, acc_ref, in_refs, y_ref, before_ref, next_ref, ext, None)
-    y = next_ref[...]
-    gram = mm(y, y, ROWS_BY_ROWS, lax.Precision.HIGHEST)
+    n = next_ref.shape[0]
+    terms = over(three(next_ref[...]))
+    every = mm(terms, terms, ROWS_BY_ROWS)
+    gram = sum(every[n * i : n * (i + 1), n * j : n * (j + 1)] for i, j in ((0, 2), (2, 0), (1, 1), (0, 1), (1, 0), (0, 0)))
     packed = beside([gram[8 * i : 8 * i + 8] for i in range(gram.shape[0] // 8)])
     gram_ref[...] = jnp.broadcast_to(packed[None], gram_ref.shape)
 
@@ -275,7 +285,13 @@
     packed = jnp.sum(grams_ref[...], axis=0)
     n = y_ref.shape[0]
     gram = over([packed[:, n * i : n * (i + 1)] for i in range(n // 8)])
-    out_ref[...] = mm(inverse_factor(gram, scale), y_ref[...], ROWS_BY_COLS, lax.Precision.HIGHEST)
+    a = three(inverse_factor(gram, scale))
+    pairs = ((0, 0), (0, 1), (1, 0), (0, 2), (1, 1), (2, 0))
+    left = beside([a[i] for i, _ in pairs])
+    width = 4 * LANES
+    for at in range(0, y_ref.shape[1], width):
+        y = three(y_ref[:, at : at + width])
+        out_ref[:, at : at + width] = mm(left, over([y[j] for _, j in pairs]), ROWS_BY_COLS)
 
 
 def in_vmem(x):
@@ -362,7 +378,7 @@
         functools.partial(outgoing_ones, shape), "outgoing_ones", [("hbm", slots_of), ("hbm", w)],
         [((8, LANES), F32)] * 4 + [(slots_of.shape, jnp.int32)],
         [pltpu.VMEM((rows, slots - INNER, LANES, LANES), BF16),
-         pltpu.VMEM((rows, 8, LANES), F32), pltpu.SemaphoreType.DMA((RIMS + 1,))],
+         pltpu.VMEM((rows, 8, LANES), F32), pltpu.SemaphoreType.DMA((PARTS + 1,))],
         flops=rows * 3 * per_block * 32, moved=1 << 20,
     )
     w, *pays = lax.optimization_barrier((w, *pays))

time: 51.4 us -> 49.4 us (0.961)
  starting transfers between devices: 18.5 us -> 17.6 us
  blocking collectives: 12 us -> 11.3 us
    ppermute x16, starting transfers between devices: 18.5 us -> 17.6 us  [exchange(): lax.ppermute(payload, ('narrow', 'wide'), pairs[m])]
    all_to_all x1, blocking collectives: 12 us -> 11.3 us  [body(): grams = lax.all_to_all(grams, ('narrow', 'wide'), 0, 0)]
    pallas_call x10, Pallas kernels: 19.7 us -> 19.2 us  [kernel_call(): pl.pallas_call(body, name=name, out_shape=[pltpu.SMEM(s, d) if d == jnp.i...]
  transfers between devices with their start and end apart: 16 -> 16, of which waited for: 2 -> 4; matrix products, arithmetic and copies ran while one was open for 0% -> 0% of each run, Pallas kernels for 22% -> 22%
where the time goes in v4:
time: 49.4 us; the launch traced here: 49.2 us
  Pallas kernels  19.2 us (39%)
  starting transfers between devices  17.6 us (36%)
  blocking collectives  11.3 us (23%)
  waiting for transfers between devices  1.12 us (2%)
    pallas_call x10, Pallas kernels, kernel_call(): pl.pallas_call(body, name=name, out_shape=[pltpu.SMEM(s, d) if d == jnp.i...  19.2 us
    ppermute x16, starting transfers between devices, exchange(): lax.ppermute(payload, ('narrow', 'wide'), pairs[m])  17.6 us
    all_to_all x1, blocking collectives, body(): grams = lax.all_to_all(grams, ('narrow', 'wide'), 0, 0)  11.3 us
    ppermute x16, waiting for transfers between devices, exchange(): lax.ppermute(payload, ('narrow', 'wide'), pairs[m])  1.12 us
  transfers between devices with their start and end apart: 16, of which 4 were waited for; matrix products, arithmetic and copies ran while one was open for 0% of the time, Pallas kernels for 22%

profile of v4, /device:TPU:0, one launch (start us, length us, event | category | flops | bytes accessed | tf_op | source)
XLA Modules:
  0.0 49.2 jit_solution(8776293861822799303)
XLA Ops:
  0.0 0.0 copy-start
  0.0 0.0 copy-start.1
  0.0 2.1 %outgoing_ones.1 = (f32[8,128]{1,0:T(8,128)S(1)}, f32[8,128]{1,0:T(8,128)S(1)}, f32[8,128]{1,0:T(8,128)S(1)}, f32[8,128]{1,0:T(8,128)S(1)}, s32[12,1,28]{2,1,0:T(1,128)S(4)}) custom-call(s32[12,1,28]{2,1,0:T(1,128)} %bitcast.18, bf16[28,12,128,128]{3,2,1,0:T(8,128)(2,1)} %bitcast.6), custom_call_target="tpu_custom_call" | custom-call | flops 75497472 | bytes 1048576 | tf_op jit(solution)/shard_map/outgoing_ones/pallas_call | solution.py:315
  2.1 3.0 %collective-permute-start = (f32[8,128]{1,0:T(8,128)S(1)}, f32[8,128]{1,0:T(8,128)S(1)}, u32[]{:S(2)}, u32[]{:S(2)}) collective-permute-start(f32[8,128]{1,0:T(8,128)S(1)} %get-tuple-element.43), channel_id=1, source_target_pairs={{0,1},{1,0},{2,3},{3,2},{4,5},{5,4},{6,7},{7,6},{8,9},{9,8},{10,11... | collective-permute-start | bytes 12296 | tf_op jit(solution)/shard_map/ppermute | solution.py:360
  5.2 0.0 collective-permute-start.1
  5.2 1.6 %collective-permute-start.2 = (f32[8,128]{1,0:T(8,128)S(1)}, f32[8,128]{1,0:T(8,128)S(1)}, u32[]{:S(2)}, u32[]{:S(2)}) collective-permute-start(f32[8,128]{1,0:T(8,128)S(1)} %get-tuple-element.45), channel_id=1, source_target_pairs={{8,16},{16,8},{9,17},{17,9},{10,18},{18,10},{11,19},{19,11},{12,20... | collective-permute-start | bytes 12296 | tf_op jit(solution)/shard_map/ppermute | solution.py:360
  6.8 0.0 collective-permute-start.3
  6.8 0.0 copy-done
  6.8 2.0 %local_degree.1.deg_ref = f32[28,128]{1,0:T(8,128)S(1)} custom-call(s32[12,1,28]{2,1,0:T(1,128)S(4)} %get-tuple-element.37.pattern_ref, bf16[28,12,128,128]{3,2,1,0:T(8,128)(2,1)S(1)} %bitcast.7), custom_call_target="tpu_custom_call" | custom-call | flops 352321536 | bytes 8388608 | tf_op jit(solution)/shard_map/local_degree/pallas_call | solution.py:315
  8.8 0.0 collective-permute-done.refs_0_
  8.8 0.0 collective-permute-done.1.refs_1_
  8.8 0.0 collective-permute-done.2.refs_2_
  8.8 0.0 collective-permute-done.3.refs_3_
  8.8 0.0 copy-done.1
  8.8 0.6 %first_scaled.1 = (f32[28,128]{1,0:T(8,128)S(1)}, bf16[28,32,128]{2,1,0:T(8,128)(2,1)S(1)}, bf16[12,32,128]{2,1,0:T(8,128)(2,1)S(1)}, bf16[12,32,128]{2,1,0:T(8,...) custom-call(s32[12,1,28]{2,1,0:T(1,128)S(4)} %get-tuple-element.37.pattern_ref, ...), custom_call_target="tpu_custom_call" | custom-call | flops 75497472 | bytes 1048576 | tf_op jit(solution)/shard_map/first_scaled/pallas_call | solution.py:315
  9.5 3.1 %collective-permute-start.4 = (bf16[12,32,128]{2,1,0:T(8,128)(2,1)S(1)}, bf16[12,32,128]{2,1,0:T(8,128)(2,1)S(1)}, u32[]{:S(2)}, u32[]{:S(2)}) collective-permute-start(bf16[12,32,128]{2,1,0:T(8,128)(2,1)S(1)} %get-tuple-element.51), channel_id=1, source_target_pairs={{0,1},{1,0},{2,3},{3,2},{4,5},{5,4},{6,7},{7,6},{8,9},{9,8},{10,11... | collective-permute-start | bytes 294920 | tf_op jit(solution)/shard_map/ppermute | solution.py:360
  12.6 0.0 collective-permute-start.5
  12.6 1.0 %collective-permute-start.6 = (bf16[12,32,128]{2,1,0:T(8,128)(2,1)S(1)}, bf16[12,32,128]{2,1,0:T(8,128)(2,1)S(1)}, u32[]{:S(2)}, u32[]{:S(2)}) collective-permute-start(bf16[12,32,128]{2,1,0:T(8,128)(2,1)S(1)} %get-tuple-element.53), channel_id=1, source_target_pairs={{8,16},{16,8},{9,17},{17,9},{10,18},{18,10},{11,19},{19,11},{12,20... | collective-permute-start | bytes 294920 | tf_op jit(solution)/shard_map/ppermute | solution.py:360
  13.5 0.0 collective-permute-start.7
  13.5 3.3 %own_terms_turning.1 = (f32[28,32,128]{2,1,0:T(8,128)S(1)}, bf16[28,12,128,128]{3,2,1,0:T(8,128)(2,1)S(1)}) custom-call(s32[12,1,28]{2,1,0:T(1,128)S(4)} %get-tuple-element.37.pattern_ref, bf16[28,12,128,128]{3,2,1,0:T(8,128)(2,1)S(1)} %bitcast.9, bf16[28,32,128]{2,1,0:T(8,128)(2,1)S(1)} %get-tuple-element.47.u_ref), custom_call_target="tpu_custom_call" | custom-call | flops 704643072 | bytes 8388608 | tf_op jit(solution)/shard_map/own_terms_turning/pallas_call | solution.py:315
  16.9 0.0 collective-permute-done.4.refs_0_
  16.9 0.0 collective-permute-done.5.refs_1_
  16.9 0.1 collective-permute-done.6.refs_2_
  17.0 0.0 collective-permute-done.7.refs_3_
  17.0 1.1 %advance.2 = (f32[32,3584]{1,0:T(8,128)S(1)}, bf16[28,32,128]{2,1,0:T(8,128)(2,1)S(1)}, bf16[12,32,128]{2,1,0:T(8,128)(2,1)S(1)}, bf16[12,32,128]{2,1,0:T(8,128)...) custom-call(s32[12,1,28]{2,1,0:T(1,128)S(4)} %get-tuple-element.37.pattern_ref, ...), custom_call_target="tpu_custom_call" | custom-call | flops 150994944 | bytes 1048576 | tf_op jit(solution)/shard_map/advance/pallas_call | solution.py:315
  18.1 3.4 %collective-permute-start.8 = (bf16[12,32,128]{2,1,0:T(8,128)(2,1)S(1)}, bf16[12,32,128]{2,1,0:T(8,128)(2,1)S(1)}, u32[]{:S(2)}, u32[]{:S(2)}) collective-permute-start(bf16[12,32,128]{2,1,0:T(8,128)(2,1)S(1)} %get-tuple-element.56), channel_id=1, source_target_pairs={{0,1},{1,0},{2,3},{3,2},{4,5},{5,4},{6,7},{7,6},{8,9},{9,8},{10,11... | collective-permute-start | bytes 294920 | tf_op jit(solution)/shard_map/ppermute | solution.py:360
  21.5 0.0 collective-permute-start.9
  21.5 1.1 %collective-permute-start.10 = (bf16[12,32,128]{2,1,0:T(8,128)(2,1)S(1)}, bf16[12,32,128]{2,1,0:T(8,128)(2,1)S(1)}, u32[]{:S(2)}, u32[]{:S(2)}) collective-permute-start(bf16[12,32,128]{2,1,0:T(8,128)(2,1)S(1)} %get-tuple-element.58), channel_id=1, source_target_pairs={{8,16},{16,8},{9,17},{17,9},{10,18},{18,10},{11,19},{19,11},{12,20... | collective-permute-start | bytes 294920 | tf_op jit(solution)/shard_map/ppermute | solution.py:360
  22.6 0.0 collective-permute-start.11
  22.6 2.8 %own_terms.2.acc_ref = f32[28,32,128]{2,1,0:T(8,128)S(1)} custom-call(s32[12,1,28]{2,1,0:T(1,128)S(4)} %get-tuple-element.37.pattern_ref, bf16[28,12,128,128]{3,2,1,0:T(8,128)(2,1)S(1)} %bitcast.11, bf16[28,12,128,128]{3,2,1,0:T(8,128)(2,1)S(1)} %get-tuple-element.48.turned_ref, bf16[28,32,128]{2,1,0:T(8,128)(2,1)S(1)} %get-tuple-element.55.u_ref), custom_call_target="tpu_custom_call" | custom-call | flops 704643072 | bytes 8388608 | tf_op jit(solution)/shard_map/own_terms/pallas_call | solution.py:315
  25.4 0.3 collective-permute-done.8.refs_0_
  25.7 0.0 collective-permute-done.9.refs_1_
  25.7 0.3 collective-permute-done.10.refs_2_
  25.9 0.0 collective-permute-done.11.refs_3_
  25.9 1.3 %advance.3 = (f32[32,3584]{1,0:T(8,128)S(1)}, bf16[28,32,128]{2,1,0:T(8,128)(2,1)S(1)}, bf16[12,32,128]{2,1,0:T(8,128)(2,1)S(1)}, bf16[12,32,128]{2,1,0:T(8,128)...) custom-call(s32[12,1,28]{2,1,0:T(1,128)S(4)} %get-tuple-element.37.pattern_ref, ...), custom_call_target="tpu_custom_call" | custom-call | flops 150994944 | bytes 1048576 | tf_op jit(solution)/shard_map/advance/pallas_call | solution.py:315
  27.2 3.2 %collective-permute-start.12 = (bf16[12,32,128]{2,1,0:T(8,128)(2,1)S(1)}, bf16[12,32,128]{2,1,0:T(8,128)(2,1)S(1)}, u32[]{:S(2)}, u32[]{:S(2)}) collective-permute-start(bf16[12,32,128]{2,1,0:T(8,128)(2,1)S(1)} %get-tuple-element.62), channel_id=1, source_target_pairs={{0,1},{1,0},{2,3},{3,2},{4,5},{5,4},{6,7},{7,6},{8,9},{9,8},{10,11... | collective-permute-start | bytes 294920 | tf_op jit(solution)/shard_map/ppermute | solution.py:360
  30.5 0.0 collective-permute-start.13
  30.5 1.2 %collective-permute-start.14 = (bf16[12,32,128]{2,1,0:T(8,128)(2,1)S(1)}, bf16[12,32,128]{2,1,0:T(8,128)(2,1)S(1)}, u32[]{:S(2)}, u32[]{:S(2)}) collective-permute-start(bf16[12,32,128]{2,1,0:T(8,128)(2,1)S(1)} %get-tuple-element.64), channel_id=1, source_target_pairs={{8,16},{16,8},{9,17},{17,9},{10,18},{18,10},{11,19},{19,11},{12,20... | collective-permute-start | bytes 294920 | tf_op jit(solution)/shard_map/ppermute | solution.py:360
  31.7 0.0 collective-permute-start.15
  31.7 2.8 %own_terms.3.acc_ref = f32[28,32,128]{2,1,0:T(8,128)S(1)} custom-call(s32[12,1,28]{2,1,0:T(1,128)S(4)} %get-tuple-element.37.pattern_ref, bf16[28,12,128,128]{3,2,1,0:T(8,128)(2,1)S(1)} %bitcast.13, bf16[28,12,128,128]{3,2,1,0:T(8,128)(2,1)S(1)} %get-tuple-element.48.turned_ref, bf16[28,32,128]{2,1,0:T(8,128)(2,1)S(1)} %get-tuple-element.61.u_ref), custom_call_target="tpu_custom_call" | custom-call | flops 704643072 | bytes 8388608 | tf_op jit(solution)/shard_map/own_terms/pallas_call | solution.py:315
  34.5 0.0 collective-permute-done.12.refs_0_
  34.5 0.0 collective-permute-done.13.refs_1_
  34.5 0.4 collective-permute-done.14.refs_2_
  34.9 0.0 collective-permute-done.15.refs_3_
  34.9 1.0 %finish.1 = (f32[32,3584]{1,0:T(8,128)S(1)}, f32[32,8,128]{2,1,0:T(8,128)S(1)}) custom-call(s32[12,1,28]{2,1,0:T(1,128)S(4)} %get-tuple-element.37.pattern_ref, bf16[28,12,128,128]{3,2,1,0:T(8,128)(2,1)S(1)} %get-tuple-element.48.turned_ref, f32[28,128]{1,0:T(8,128)S(1)} %get-tuple-element.49.inv_ref, f32[28,32,128]{2,1,0:T(8,128)S(1)} %own_terms.3.acc_ref, ...), custom_call_target="tpu_custom_call" | custom-call | flops 75497472 | bytes 1048576 | tf_op jit(solution)/shard_map/finish/pallas_call | solution.py:315
  35.9 11.3 %all_to_all.5.grams_ref = f32[32,8,128]{2,1,0:T(8,128)S(1)} all-to-all(f32[32,8,128]{2,1,0:T(8,128)S(1)} %get-tuple-element.67), channel_id=1, replica_groups=mesh['narrow'=4,'wide'=8] {'narrow','wide'}, dimensions={0} | all-to-all | bytes 262144 | tf_op jit(solution)/shard_map/all_to_all | solution.py:430
  47.2 2.1 %orthonormal.1 = f32[32,3584]{1,0:T(8,128)} custom-call(f32[32,8,128]{2,1,0:T(8,128)S(1)} %all_to_all.5.grams_ref, f32[32,3584]{1,0:T(8,128)S(1)} %get-tuple-element.68.y_ref), custom_call_target="tpu_custom_call" | custom-call | tf_op jit(solution)/shard_map/orthonormal/pallas_call | solution.py:315
Async XLA Ops:
  0.0 6.8 %copy-start = (bf16[1,1,28,12,128,128]{5,4,3,2,1,0:T(8,128)(2,1)S(1)}, bf16[1,1,28,12,128,128]{5,4,3,2,1,0:T(8,128)(2,1)}, u32[]{:S(2)}) copy-start(bf16[1,1,28,12,128,128]{5,4,3,2,1,0:T(8,128)(2,1)} %param.4) | copy-start | bytes 33030148
  0.0 8.8 %copy-start.1 = (bf16[1,1,32,3584]{3,2,1,0:T(8,128)(2,1)S(1)}, bf16[1,1,32,3584]{3,2,1,0:T(8,128)(2,1)}, u32[]{:S(2)}) copy-start(bf16[1,1,32,3584]{3,2,1,0:T(8,128)(2,1)} %param.3) | copy-start | bytes 688132
  2.1 6.7 %collective-permute-start = (f32[8,128]{1,0:T(8,128)S(1)}, f32[8,128]{1,0:T(8,128)S(1)}, u32[]{:S(2)}, u32[]{:S(2)}) collective-permute-start(f32[8,128]{1,0:T(8,128)S(1)} %get-tuple-element.43), channel_id=1, source_target_pairs={{0,1},{1,0},{2,3},{3,2},{4,5},{5,4},{6,7},{7,6},{8,9},{9,8},{10,11... | collective-permute-start | bytes 12296 | tf_op jit(solution)/shard_map/ppermute | solution.py:360
  5.2 3.7 %collective-permute-start.1 = (f32[8,128]{1,0:T(8,128)S(1)}, f32[8,128]{1,0:T(8,128)S(1)}, u32[]{:S(2)}, u32[]{:S(2)}) collective-permute-start(f32[8,128]{1,0:T(8,128)S(1)} %get-tuple-element.44), channel_id=1, source_target_pairs={{1,2},{2,1},{3,4},{4,3},{5,6},{6,5},{9,10},{10,9},{11,12},{12,11},... | collective-permute-start | bytes 12296 | tf_op jit(solution)/shard_map/ppermute | solution.py:360
  5.2 3.7 %collective-permute-start.2 = (f32[8,128]{1,0:T(8,128)S(1)}, f32[8,128]{1,0:T(8,128)S(1)}, u32[]{:S(2)}, u32[]{:S(2)}) collective-permute-start(f32[8,128]{1,0:T(8,128)S(1)} %get-tuple-element.45), channel_id=1, source_target_pairs={{8,16},{16,8},{9,17},{17,9},{10,18},{18,10},{11,19},{19,11},{12,20... | collective-permute-start | bytes 12296 | tf_op jit(solution)/shard_map/ppermute | solution.py:360
  6.8 2.1 %collective-permute-start.3 = (f32[8,128]{1,0:T(8,128)S(1)}, f32[8,128]{1,0:T(8,128)S(1)}, u32[]{:S(2)}, u32[]{:S(2)}) collective-permute-start(f32[8,128]{1,0:T(8,128)S(1)} %get-tuple-element.46), channel_id=1, source_target_pairs={{0,8},{8,0},{16,24},{24,16},{1,9},{9,1},{17,25},{25,17},{2,10},{10... | collective-permute-start | bytes 12296 | tf_op jit(solution)/shard_map/ppermute | solution.py:360
  9.5 7.4 %collective-permute-start.4 = (bf16[12,32,128]{2,1,0:T(8,128)(2,1)S(1)}, bf16[12,32,128]{2,1,0:T(8,128)(2,1)S(1)}, u32[]{:S(2)}, u32[]{:S(2)}) collective-permute-start(bf16[12,32,128]{2,1,0:T(8,128)(2,1)S(1)} %get-tuple-element.51), channel_id=1, source_target_pairs={{0,1},{1,0},{2,3},{3,2},{4,5},{5,4},{6,7},{7,6},{8,9},{9,8},{10,11... | collective-permute-start | bytes 294920 | tf_op jit(solution)/shard_map/ppermute | solution.py:360
  12.6 4.3 %collective-permute-start.5 = (bf16[12,32,128]{2,1,0:T(8,128)(2,1)S(1)}, bf16[12,32,128]{2,1,0:T(8,128)(2,1)S(1)}, u32[]{:S(2)}, u32[]{:S(2)}) collective-permute-start(bf16[12,32,128]{2,1,0:T(8,128)(2,1)S(1)} %get-tuple-element.52), channel_id=1, source_target_pairs={{1,2},{2,1},{3,4},{4,3},{5,6},{6,5},{9,10},{10,9},{11,12},{12,11},... | collective-permute-start | bytes 294920 | tf_op jit(solution)/shard_map/ppermute | solution.py:360
  12.6 4.4 %collective-permute-start.6 = (bf16[12,32,128]{2,1,0:T(8,128)(2,1)S(1)}, bf16[12,32,128]{2,1,0:T(8,128)(2,1)S(1)}, u32[]{:S(2)}, u32[]{:S(2)}) collective-permute-start(bf16[12,32,128]{2,1,0:T(8,128)(2,1)S(1)} %get-tuple-element.53), channel_id=1, source_target_pairs={{8,16},{16,8},{9,17},{17,9},{10,18},{18,10},{11,19},{19,11},{12,20... | collective-permute-start | bytes 294920 | tf_op jit(solution)/shard_map/ppermute | solution.py:360
  13.5 3.5 %collective-permute-start.7 = (bf16[12,32,128]{2,1,0:T(8,128)(2,1)S(1)}, bf16[12,32,128]{2,1,0:T(8,128)(2,1)S(1)}, u32[]{:S(2)}, u32[]{:S(2)}) collective-permute-start(bf16[12,32,128]{2,1,0:T(8,128)(2,1)S(1)} %get-tuple-element.54), channel_id=1, source_target_pairs={{0,8},{8,0},{16,24},{24,16},{1,9},{9,1},{17,25},{25,17},{2,10},{10... | collective-permute-start | bytes 294920 | tf_op jit(solution)/shard_map/ppermute | solution.py:360
  18.1 7.5 %collective-permute-start.8 = (bf16[12,32,128]{2,1,0:T(8,128)(2,1)S(1)}, bf16[12,32,128]{2,1,0:T(8,128)(2,1)S(1)}, u32[]{:S(2)}, u32[]{:S(2)}) collective-permute-start(bf16[12,32,128]{2,1,0:T(8,128)(2,1)S(1)} %get-tuple-element.56), channel_id=1, source_target_pairs={{0,1},{1,0},{2,3},{3,2},{4,5},{5,4},{6,7},{7,6},{8,9},{9,8},{10,11... | collective-permute-start | bytes 294920 | tf_op jit(solution)/shard_map/ppermute | solution.py:360
  21.5 4.2 %collective-permute-start.9 = (bf16[12,32,128]{2,1,0:T(8,128)(2,1)S(1)}, bf16[12,32,128]{2,1,0:T(8,128)(2,1)S(1)}, u32[]{:S(2)}, u32[]{:S(2)}) collective-permute-start(bf16[12,32,128]{2,1,0:T(8,128)(2,1)S(1)} %get-tuple-element.57), channel_id=1, source_target_pairs={{1,2},{2,1},{3,4},{4,3},{5,6},{6,5},{9,10},{10,9},{11,12},{12,11},... | collective-permute-start | bytes 294920 | tf_op jit(solution)/shard_map/ppermute | solution.py:360
  21.5 4.4 %collective-permute-start.10 = (bf16[12,32,128]{2,1,0:T(8,128)(2,1)S(1)}, bf16[12,32,128]{2,1,0:T(8,128)(2,1)S(1)}, u32[]{:S(2)}, u32[]{:S(2)}) collective-permute-start(bf16[12,32,128]{2,1,0:T(8,128)(2,1)S(1)} %get-tuple-element.58), channel_id=1, source_target_pairs={{8,16},{16,8},{9,17},{17,9},{10,18},{18,10},{11,19},{19,11},{12,20... | collective-permute-start | bytes 294920 | tf_op jit(solution)/shard_map/ppermute | solution.py:360
  22.6 3.4 %collective-permute-start.11 = (bf16[12,32,128]{2,1,0:T(8,128)(2,1)S(1)}, bf16[12,32,128]{2,1,0:T(8,128)(2,1)S(1)}, u32[]{:S(2)}, u32[]{:S(2)}) collective-permute-start(bf16[12,32,128]{2,1,0:T(8,128)(2,1)S(1)} %get-tuple-element.59), channel_id=1, source_target_pairs={{0,8},{8,0},{16,24},{24,16},{1,9},{9,1},{17,25},{25,17},{2,10},{10... | collective-permute-start | bytes 294920 | tf_op jit(solution)/shard_map/ppermute | solution.py:360
  27.2 7.3 %collective-permute-start.12 = (bf16[12,32,128]{2,1,0:T(8,128)(2,1)S(1)}, bf16[12,32,128]{2,1,0:T(8,128)(2,1)S(1)}, u32[]{:S(2)}, u32[]{:S(2)}) collective-permute-start(bf16[12,32,128]{2,1,0:T(8,128)(2,1)S(1)} %get-tuple-element.62), channel_id=1, source_target_pairs={{0,1},{1,0},{2,3},{3,2},{4,5},{5,4},{6,7},{7,6},{8,9},{9,8},{10,11... | collective-permute-start | bytes 294920 | tf_op jit(solution)/shard_map/ppermute | solution.py:360
  30.5 4.0 %collective-permute-start.13 = (bf16[12,32,128]{2,1,0:T(8,128)(2,1)S(1)}, bf16[12,32,128]{2,1,0:T(8,128)(2,1)S(1)}, u32[]{:S(2)}, u32[]{:S(2)}) collective-permute-start(bf16[12,32,128]{2,1,0:T(8,128)(2,1)S(1)} %get-tuple-element.63), channel_id=1, source_target_pairs={{1,2},{2,1},{3,4},{4,3},{5,6},{6,5},{9,10},{10,9},{11,12},{12,11},... | collective-permute-start | bytes 294920 | tf_op jit(solution)/shard_map/ppermute | solution.py:360
  30.5 4.4 %collective-permute-start.14 = (bf16[12,32,128]{2,1,0:T(8,128)(2,1)S(1)}, bf16[12,32,128]{2,1,0:T(8,128)(2,1)S(1)}, u32[]{:S(2)}, u32[]{:S(2)}) collective-permute-start(bf16[12,32,128]{2,1,0:T(8,128)(2,1)S(1)} %get-tuple-element.64), channel_id=1, source_target_pairs={{8,16},{16,8},{9,17},{17,9},{10,18},{18,10},{11,19},{19,11},{12,20... | collective-permute-start | bytes 294920 | tf_op jit(solution)/shard_map/ppermute | solution.py:360
  31.7 3.3 %collective-permute-start.15 = (bf16[12,32,128]{2,1,0:T(8,128)(2,1)S(1)}, bf16[12,32,128]{2,1,0:T(8,128)(2,1)S(1)}, u32[]{:S(2)}, u32[]{:S(2)}) collective-permute-start(bf16[12,32,128]{2,1,0:T(8,128)(2,1)S(1)} %get-tuple-element.65), channel_id=1, source_target_pairs={{0,8},{8,0},{16,24},{24,16},{1,9},{9,1},{17,25},{25,17},{2,10},{10... | collective-permute-start | bytes 294920 | tf_op jit(solution)/shard_map/ppermute | solution.py:360

commit v5 on v4

--- a/solution.py
+++ b/solution.py
@@ -76,7 +76,7 @@
 
 
 def outgoing_ones(shape, pattern_hbm, w_hbm, *refs):
-    pay_refs, (pattern_ref, w_ref, sums, sems) = refs[:4], refs[4:]
+    pay_refs, (pattern_ref, w_ref, sems), sums = refs[:4], refs[4:7], refs[7:]
     named = fetch(pattern_hbm, pattern_ref, sems.at[PARTS])
     copies = []
     for part in range(PARTS):
@@ -84,7 +84,8 @@
         copies.append(fetch(w_hbm.at[rows, INNER:], w_ref.at[rows], sems.at[part]))
     blocks = pattern_ref.shape[2]
     slots = w_ref.shape[1]
-    sums[...] = jnp.zeros_like(sums)
+    for r in range(RIMS):
+        sums[r][...] = jnp.zeros_like(sums[r])
     ones = jnp.ones((8, LANES), BF16)
     named.wait()
     for p in range(PARTS):
@@ -92,27 +93,32 @@
         for b in range(p * RIMS * RIM // PARTS, (p + 1) * RIMS * RIM // PARTS):
             part = mm(ones, beside([w_ref[b, s] for s in range(slots)]), ROWS_BY_COLS)
             for s in range(slots):
-                sums[b // RIM * RIM - blocks + pattern_ref[INNER + s, 0, b]] += part[:, s * LANES : (s + 1) * LANES]
+                sums[b // RIM][pattern_ref[INNER + s, 0, b] - blocks] += part[:, s * LANES : (s + 1) * LANES]
     rim_of, _, _ = places(shape)
     for m in range(4):
+        low = ORDER[m] // 2 * 2
+        upper = (rim_of[m] - low).astype(F32)
         for q in range(RIM):
-            pay_refs[m][q : q + 1] = sums[rim_of[m] * RIM + q][0:1].astype(BF16).astype(F32)
-
-
-def local_degree(shape, pattern_ref, w_ref, deg_ref, acc):
+            total = sums[low][q, 0:1] * (1.0 - upper) + sums[low + 1][q, 0:1] * upper
+            pay_refs[m][q : q + 1] = total.astype(BF16).astype(F32)
+
+
+def local_degree(shape, pattern_ref, w_ref, deg_ref, *accs):
     blocks, slots = w_ref.shape[:2]
     by_rim = places(shape)[2]
     ones = jnp.ones((8, LANES), BF16)
     for b in range(0, blocks, 2):
         part = mm(ones, beside([w_ref[b, 0], w_ref[b + 1, 0]]), ROWS_BY_COLS)
-        acc[b] = part[:, :LANES]
-        acc[b + 1] = part[:, LANES:]
+        accs[0][b] = part[:, :LANES]
+        accs[0][b + 1] = part[:, LANES:]
+    for acc in accs[1:]:
+        acc[...] = jnp.zeros_like(acc)
     for b in range(blocks):
         own = INNER if b < RIMS * RIM else slots
         for group in slot_pairs(1, own):
             part = mm(ones, beside([w_ref[b, s] for s in group]), ROWS_BY_COLS)
             for i, s in enumerate(group):
-                acc[pattern_ref[s, 0, b]] += part[:, i * LANES : (i + 1) * LANES]
+                accs[s % len(accs)][pattern_ref[s, 0, b]] += part[:, i * LANES : (i + 1) * LANES]
         rows = w_ref[b, 0].astype(F32)
         for s in range(1, own):
             rows = rows + w_ref[b, s].astype(F32)
@@ -123,39 +129,55 @@
             rows = rows + by_rim[b // RIM].astype(F32) * outer
         deg_ref[b : b + 1] = jnp.sum(rows, axis=1, keepdims=True).T
     for b in range(blocks):
-        deg_ref[b : b + 1] += acc[b, 0:1]
-
-
-def send_out(shape, u_ref, w_ref, pattern_ref, terms, pay_refs):
+        deg_ref[b : b + 1] += sum(acc[b, 0:1] for acc in accs)
+
+
+def halves(blocks):
+    wide = tuple(range(2 * RIM, RIMS * RIM))
+    return wide, tuple(b for b in range(blocks) if b not in wide)
+
+
+def first_rim(half):
+    return 2 - 2 * half
+
+
+def send_out(shape, half, u_ref, w_ref, pattern_ref, terms, pay_refs):
     blocks, slots = w_ref.shape[:2]
     terms[...] = jnp.zeros_like(terms)
-    for b in range(RIMS * RIM):
-        part = mm(u_ref[b], beside([w_ref[b, s] for s in range(INNER, slots)]), ROWS_BY_COLS)
-        base = (b // RIM) * RIM - blocks
+    for i in range(2 * RIM):
+        b = first_rim(half) * RIM + i
+        part = mm(u_ref[i], beside([w_ref[b, s] for s in range(INNER, slots)]), ROWS_BY_COLS)
+        base = i // RIM * RIM - blocks
         for s in range(INNER, slots):
-            i = s - INNER
-            terms[base + pattern_ref[s, 0, b]] += part[:, i * LANES : (i + 1) * LANES]
+            at = s - INNER
+            terms[base + pattern_ref[s, 0, b]] += part[:, at * LANES : (at + 1) * LANES]
     rim_of, _, _ = places(shape)
-    for m in range(4):
-        first = rim_of[m] * RIM
-        pay_refs[m][0:RIM] = u_ref[pl.ds(first, RIM)]
-        pay_refs[m][RIM:] = terms[pl.ds(first, RIM)].astype(BF16)
-
-
-def first_scaled(shape, pattern_ref, w_ref, deg_ref, x_ref, *refs):
-    in_refs, (inv_ref, u_ref), pay_refs, (rims, terms) = refs[:4], refs[4:6], refs[6:10], refs[10:]
-    blocks = w_ref.shape[0]
+    for k in range(2):
+        first = (rim_of[2 * half + k] - first_rim(half)) * RIM
+        pay_refs[k][0:RIM] = u_ref[pl.ds(first, RIM)]
+        pay_refs[k][RIM:] = terms[pl.ds(first, RIM)].astype(BF16)
+
+
+def first_scaled(shape, half, pattern_ref, w_ref, deg_ref, x_ref, *refs):
+    in_refs, (inv_ref, u_ref), pay_refs, (rims, terms) = refs[:2], refs[2:4], refs[4:6], refs[6:]
     rim_of, live_of, _ = places(shape)
-    for m in range(4):
-        rims[rim_of[m]] = in_refs[m][...] * live_of[m].astype(F32)
-    for b in range(blocks):
+    for k in range(2):
+        m = 2 * half + k
+        rims[rim_of[m] - first_rim(half)] = in_refs[k][...] * live_of[m].astype(F32)
+    for i, b in enumerate(halves(w_ref.shape[0])[half]):
         degree = deg_ref[b : b + 1]
         if b < RIMS * RIM:
-            degree = degree + rims[b // RIM, b % RIM : b % RIM + 1]
+            degree = degree + rims[i // RIM, b % RIM : b % RIM + 1]
         inv = 1.0 / jnp.sqrt(0.5 * degree)
-        inv_ref[b : b + 1] = inv
-        u_ref[b] = (inv * x_ref[:, column(b)].astype(F32)).astype(BF16)
-    send_out(shape, u_ref, w_ref, pattern_ref, terms, pay_refs)
+        inv_ref[i : i + 1] = inv
+        u_ref[i] = (inv * x_ref[:, column(b)].astype(F32)).astype(BF16)
+    send_out(shape, half, u_ref, w_ref, pattern_ref, terms, pay_refs)
+
+
+def gather_halves(u_refs, u):
+    for part_ref, blocks in zip(u_refs, halves(u.shape[0])):
+        for i, b in enumerate(blocks):
+            u[b] = part_ref[i]
 
 
 def own_products(pattern_ref, w_ref, turned, u_ref, acc_ref):
@@ -176,11 +198,12 @@
         acc_ref[b] += total
 
 
-def own_terms(pattern_ref, w_ref, turned_ref, u_ref, acc_ref):
-    own_products(pattern_ref, w_ref, lambda b, s: turned_ref[b, s], u_ref, acc_ref)
-
-
-def own_terms_turning(pattern_ref, w_ref, u_ref, acc_ref, turned_ref):
+def own_terms(pattern_ref, w_ref, turned_ref, u_wide, u_rest, acc_ref, u):
+    gather_halves((u_wide, u_rest), u)
+    own_products(pattern_ref, w_ref, lambda b, s: turned_ref[b, s], u, acc_ref)
+
+
+def own_terms_turning(pattern_ref, w_ref, u_wide, u_rest, acc_ref, turned_ref, u):
     blocks, slots = w_ref.shape[:2]
 
     def turned(b, s):
@@ -188,58 +211,75 @@
         turned_ref[b, s] = block
         return block
 
-    own_products(pattern_ref, w_ref, turned, u_ref, acc_ref)
+    gather_halves((u_wide, u_rest), u)
+    own_products(pattern_ref, w_ref, turned, u, acc_ref)
     for b in range(RIMS * RIM):
         for s in range(INNER, slots):
             turned(b, s)
 
 
-def combine(
-    shape, step, pattern_ref, turned_ref, inv_ref, acc_ref, in_refs, y_ref, before_ref, next_ref, ext, u_ref
-):
+def combine(shape, step, half, pattern_ref, turned_ref, inv_ref, acc_ref, in_refs, y_ref, before_ref, ext, write):
     blocks, slots = turned_ref.shape[:2]
     rim_of, live_of, _ = places(shape)
-    for m in range(4):
-        ext[pl.ds(rim_of[m] * 2 * RIM, 2 * RIM)] = in_refs[m][...] * live_of[m].astype(BF16)
-
-    def update(b, total):
-        inv = inv_ref[b : b + 1]
-        y = y_ref[:, column(b)].astype(F32)
+    for k in range(2):
+        m = 2 * half + k
+        first = (rim_of[m] - first_rim(half)) * 2 * RIM
+        ext[pl.ds(first, 2 * RIM)] = in_refs[k][...] * live_of[m].astype(BF16)
+    mine = halves(blocks)[half]
+
+    def vectors(ref, b, i):
+        whole = ref.shape[1] == blocks * LANES
+        return ref[:, column(b if whole else i)].astype(F32)
+
+    def update(b, i, total):
+        inv = inv_ref[i : i + 1]
+        y = vectors(y_ref, b, i)
         lap = y - inv * (0.5 * total)
         new = (lap - center * y) / half_width
         if step > 0:
-            new = 2.0 * new - before_ref[:, column(b)].astype(F32)
-        next_ref[:, column(b)] = new
-        if u_ref is not None:
-            u_ref[b] = (inv * new).astype(BF16)
-
-    for b in range(RIMS * RIM, blocks):
-        update(b, acc_ref[b])
-    for b in range(RIMS * RIM):
-        base = (b // RIM) * 2 * RIM
+            new = 2.0 * new - vectors(before_ref, b, i)
+        write(b, i, new, inv)
+
+    for i in range(2 * RIM, len(mine)):
+        update(mine[i], i, acc_ref[mine[i]])
+    for i in range(2 * RIM):
+        b = mine[i]
+        base = i // RIM * 2 * RIM
         ahead = beside([ext[base + pattern_ref[s, 0, b] - blocks] for s in range(INNER, slots)])
         ahead = mm(ahead, over([turned_ref[b, s] for s in range(INNER, slots)]), ROWS_BY_COLS)
-        update(b, acc_ref[b] + ahead + ext[base + RIM + b % RIM].astype(F32))
-
-
-def advance(shape, step, pattern_ref, w_ref, turned_ref, inv_ref, acc_ref, *refs):
-    in_refs, (y_ref, before_ref, next_ref, u_ref) = refs[:4], refs[4:8]
-    pay_refs, (ext, terms) = refs[8:12], refs[12:]
+        update(b, i, acc_ref[b] + ahead + ext[base + RIM + b % RIM].astype(F32))
+
+
+def advance(shape, step, half, pattern_ref, w_ref, turned_ref, inv_ref, acc_ref, *refs):
+    in_refs, (y_ref, before_ref, next_ref, u_ref), pay_refs, (ext, terms) = refs[:2], refs[2:6], refs[6:8], refs[8:]
+
+    def write(b, i, new, inv):
+        next_ref[:, column(i)] = new
+        u_ref[i] = (inv * new).astype(BF16)
+
     combine(
-        shape, step, pattern_ref, turned_ref, inv_ref, acc_ref, in_refs, y_ref, before_ref, next_ref, ext, u_ref
+        shape, step, half, pattern_ref, turned_ref, inv_ref, acc_ref, in_refs, y_ref, before_ref, ext, write
     )
-    send_out(shape, u_ref, w_ref, pattern_ref, terms, pay_refs)
-
-
-def finish(shape, pattern_ref, turned_ref, inv_ref, acc_ref, *refs):
-    in_refs, (y_ref, before_ref, next_ref, gram_ref, ext) = refs[:4], refs[4:]
-    combine(shape, 2, pattern_ref, turned_ref, inv_ref, acc_ref, in_refs, y_ref, before_ref, next_ref, ext, None)
+    send_out(shape, half, u_ref, w_ref, pattern_ref, terms, pay_refs)
+
+
+def finish(shape, half, pattern_ref, turned_ref, inv_ref, acc_ref, *refs):
+    in_refs, (y_ref, before_ref), refs = refs[:2], refs[2:4], refs[4:]
+    next_ref, gram_ref, ext = refs[-3:]
+
+    def write(b, i, new, inv):
+        next_ref[:, column(i)] = new
+
+    combine(shape, 2, half, pattern_ref, turned_ref, inv_ref, acc_ref, in_refs, y_ref, before_ref, ext, write)
     n = next_ref.shape[0]
     terms = over(three(next_ref[...]))
     every = mm(terms, terms, ROWS_BY_ROWS)
     gram = sum(every[n * i : n * (i + 1), n * j : n * (j + 1)] for i, j in ((0, 2), (2, 0), (1, 1), (0, 1), (1, 0), (0, 0)))
-    packed = beside([gram[8 * i : 8 * i + 8] for i in range(gram.shape[0] // 8)])
-    gram_ref[...] = jnp.broadcast_to(packed[None], gram_ref.shape)
+    packed = beside([gram[8 * i : 8 * i + 8] for i in range(n // 8)])
+    if half == 0:
+        gram_ref[...] = packed
+    else:
+        gram_ref[...] = jnp.broadcast_to((packed + refs[0][...])[None], gram_ref.shape)
 
 
 def inverse_factor(gram, scale):
@@ -281,17 +321,21 @@
     return over(parts)
 
 
-def orthonormal(scale, grams_ref, y_ref, out_ref):
+def orthonormal(scale, grams_ref, wide_ref, rest_ref, out_ref):
     packed = jnp.sum(grams_ref[...], axis=0)
-    n = y_ref.shape[0]
+    n = wide_ref.shape[0]
     gram = over([packed[:, n * i : n * (i + 1)] for i in range(n // 8)])
     a = three(inverse_factor(gram, scale))
     pairs = ((0, 0), (0, 1), (1, 0), (0, 2), (1, 1), (2, 0))
     left = beside([a[i] for i, _ in pairs])
     width = 4 * LANES
-    for at in range(0, y_ref.shape[1], width):
-        y = three(y_ref[:, at : at + width])
-        out_ref[:, at : at + width] = mm(left, over([y[j] for _, j in pairs]), ROWS_BY_COLS)
+    at = 0
+    for ref, first in ((rest_ref, 0), (wide_ref, 0), (rest_ref, 2 * RIM * LANES)):
+        last = 2 * RIM * LANES if first == 0 else ref.shape[1]
+        for start in range(first, last, width):
+            y = three(ref[:, start : start + width])
+            out_ref[:, at : at + width] = mm(left, over([y[j] for _, j in pairs]), ROWS_BY_COLS)
+            at += width
 
 
 def in_vmem(x):
@@ -355,9 +399,10 @@
     return flat
 
 
-def exchange(payloads):
+def exchange(payloads, half):
     pairs = swaps()
-    return [lax.ppermute(payload, ("narrow", "wide"), pairs[m]) for payload, m in zip(payloads, ORDER)]
+    order = ORDER[2 * half : 2 * half + 2]
+    return [lax.ppermute(payload, ("narrow", "wide"), pairs[m]) for payload, m in zip(payloads, order)]
 
 
 def body(start_block, weights, pattern):
@@ -369,16 +414,15 @@
     blocks, slots = w.shape[:2]
     rows = RIMS * RIM
     tile = ((blocks, vecs, LANES), F32)
-    scaled = ((blocks, vecs, LANES), BF16)
     full = ((vecs, docs), F32)
-    payload = [((2 * RIM, vecs, LANES), BF16)] * 4
+    payload = [((2 * RIM, vecs, LANES), BF16)] * 2
     per_block = 2 * LANES * LANES
 
     *pays, slots_of = kernel_call(
         functools.partial(outgoing_ones, shape), "outgoing_ones", [("hbm", slots_of), ("hbm", w)],
         [((8, LANES), F32)] * 4 + [(slots_of.shape, jnp.int32)],
-        [pltpu.VMEM((rows, slots - INNER, LANES, LANES), BF16),
-         pltpu.VMEM((rows, 8, LANES), F32), pltpu.SemaphoreType.DMA((PARTS + 1,))],
+        [pltpu.VMEM((rows, slots - INNER, LANES, LANES), BF16), pltpu.SemaphoreType.DMA((PARTS + 1,))]
+        + [pltpu.VMEM((RIM, 8, LANES), F32)] * RIMS,
         flops=rows * 3 * per_block * 32, moved=1 << 20,
     )
     w, *pays = lax.optimization_barrier((w, *pays))
@@ -386,51 +430,66 @@
     held = names + [("held", w)]
     (degree,) = kernel_call(
         functools.partial(local_degree, shape), "local_degree", held, [((blocks, LANES), F32)],
-        [pltpu.VMEM((blocks, 8, LANES), F32)],
+        [pltpu.VMEM((blocks, 8, LANES), F32)] * 4,
         flops=blocks * slots * per_block * 32, moved=8 << 20,
     )
-    got = exchange(pays)
-    inv, u, *pays = kernel_call(
-        functools.partial(first_scaled, shape), "first_scaled",
-        held + [("vmem", degree), ("vmem", x)] + [("vmem", g) for g in got],
-        [((blocks, LANES), F32), scaled] + payload,
-        [pltpu.VMEM((RIMS, 8, LANES), F32), pltpu.VMEM((rows, vecs, LANES), F32)],
-        flops=rows * 3 * per_block * 32, moved=1 << 20,
-    )
-    before, y = x, x
+    got = [exchange(pays[:2], 0), exchange(pays[2:], 1)]
+    ext = pltpu.VMEM((4 * RIM, vecs, LANES), BF16)
+    terms = pltpu.VMEM((2 * RIM, vecs, LANES), F32)
+    count = [len(half) for half in halves(blocks)]
+    inv, u, pays = [None] * 2, [None] * 2, [None] * 2
+    for half in (0, 1):
+        inv[half], u[half], *pays[half] = kernel_call(
+            functools.partial(first_scaled, shape, half), "first_scaled",
+            held + [("vmem", degree), ("vmem", x)] + [("vmem", g) for g in got[half]],
+            [((count[half], LANES), F32), ((count[half], vecs, LANES), BF16)] + payload,
+            [pltpu.VMEM((2, 8, LANES), F32), terms],
+            flops=rows * 3 * per_block * 16, moved=1 << 19,
+        )
+    before, y = [x, x], [x, x]
     for step in range(3):
         cost = dict(flops=2 * blocks * slots * per_block * vecs, moved=8 << 20)
+        u_ins = [("vmem", part) for part in u]
+        u_whole = [pltpu.VMEM((blocks, vecs, LANES), BF16)]
         if step == 0:
             acc, turned = kernel_call(
-                own_terms_turning, "own_terms_turning", held + [("vmem", u)], [tile, (w.shape, BF16)],
-                **cost
+                own_terms_turning, "own_terms_turning", held + u_ins, [tile, (w.shape, BF16)], u_whole, **cost
             )
         else:
-            (acc,) = kernel_call(
-                own_terms, "own_terms", held + [("held", turned), ("vmem", u)], [tile], **cost
-            )
-        got = exchange(pays)
-        common = [("held", turned), ("vmem", inv), ("vmem", acc)] + [("vmem", g) for g in got]
-        common += [("vmem", y), ("vmem", before)]
-        ext = pltpu.VMEM((2 * rows, vecs, LANES), BF16)
+            (acc,) = kernel_call(own_terms, "own_terms", held + [("held", turned)] + u_ins, [tile], u_whole, **cost)
+        got = [exchange(pays[0], 0), exchange(pays[1], 1)]
+        ins = [
+            [("vmem", inv[half])] + [("vmem", g) for g in got[half]] + [("vmem", y[half]), ("vmem", before[half])]
+            for half in (0, 1)
+        ]
         if step < 2:
-            new, u, *pays = kernel_call(
-                functools.partial(advance, shape, step), "advance", held + common, [full, scaled] + payload,
-                [ext, pltpu.VMEM((rows, vecs, LANES), F32)],
-                flops=2 * rows * 3 * per_block * 32, moved=1 << 20,
-            )
+            new, u, pays = [None] * 2, [None] * 2, [None] * 2
+            for half in (0, 1):
+                new[half], u[half], *pays[half] = kernel_call(
+                    functools.partial(advance, shape, step, half), "advance",
+                    held + [("held", turned), ins[half][0], ("vmem", acc)] + ins[half][1:],
+                    [((vecs, count[half] * LANES), F32), ((count[half], vecs, LANES), BF16)] + payload,
+                    [ext, terms],
+                    flops=rows * 3 * per_block * 32, moved=1 << 19,
+                )
+            before, y = y, new
         else:
             peers = shape[0] * shape[1]
-            new, grams = kernel_call(
-                functools.partial(finish, shape), "finish", names + common, [full, ((peers, 8, LANES), F32)],
-                [ext],
-                flops=rows * 3 * per_block * 32, moved=1 << 20,
-            )
-        before, y = y, new
+            packed = ((8, LANES), F32)
+            new, more = [None] * 2, []
+            for half in (0, 1):
+                new[half], grams = kernel_call(
+                    functools.partial(finish, shape, half), "finish",
+                    names + [("held", turned), ins[half][0], ("vmem", acc)] + ins[half][1:] + more,
+                    [((vecs, count[half] * LANES), F32), packed if half == 0 else ((peers, 8, LANES), F32)], [ext],
+                    flops=rows * 3 * per_block * 16, moved=1 << 19,
+                )
+                more = [("vmem", grams)]
+            y = new
     grams = lax.all_to_all(grams, ("narrow", "wide"), 0, 0)
     (out,) = kernel_call(
         functools.partial(orthonormal, math.sqrt(peers * docs)), "orthonormal",
-        [("vmem", grams), ("vmem", y)], [full],
+        [("vmem", grams), ("vmem", y[0]), ("vmem", y[1])], [full],
     )
     return out[None, None]
 

time: 49.4 us -> 48.5 us (0.982)
  waiting for transfers between devices: 1.12 us -> 0.19 us
  Pallas kernels: 19.2 us -> 19.9 us
  starting transfers between devices: 17.6 us -> 17 us
    ppermute x16, waiting for transfers between devices: 1.12 us -> 0.19 us  [exchange(): lax.ppermute(payload, ('narrow', 'wide'), pairs[m])]
    pallas_call x10 -> x14, Pallas kernels: 19.2 us -> 19.9 us  [kernel_call(): pl.pallas_call(body, name=name, out_shape=[pltpu.SMEM(s, d) if d == jnp.i...]
    ppermute x16, starting transfers between devices: 17.6 us -> 17 us  [exchange(): lax.ppermute(payload, ('narrow', 'wide'), pairs[m])]
  transfers between devices with their start and end apart: 16 -> 16, of which waited for: 4 -> 1; matrix products, arithmetic and copies ran while one was open for 0% -> 0% of each run, Pallas kernels for 22% -> 31%
where the time goes in v5:
time: 48.5 us; the launch traced here: 48.4 us
  Pallas kernels  19.9 us (41%)
  starting transfers between devices  17 us (35%)
  blocking collectives  11.1 us (23%)
    pallas_call x14, Pallas kernels, kernel_call(): pl.pallas_call(body, name=name, out_shape=[pltpu.SMEM(s, d) if d == jnp.i...  19.9 us
    ppermute x16, starting transfers between devices, exchange(): lax.ppermute(payload, ('narrow', 'wide'), pairs[m])  17 us
    all_to_all x1, blocking collectives, body(): grams = lax.all_to_all(grams, ('narrow', 'wide'), 0, 0)  11.1 us
  transfers between devices with their start and end apart: 16, of which 1 were waited for; matrix products, arithmetic and copies ran while one was open for 0% of the time, Pallas kernels for 31%

profile of v5, /device:TPU:0, one launch (start us, length us, event | category | flops | bytes accessed | tf_op | source)
XLA Modules:
  0.0 48.4 jit_solution(17764339967010886114)
XLA Ops:
  0.0 0.0 copy-start
  0.0 0.0 copy-start.1
  0.0 2.1 %outgoing_ones.1 = (f32[8,128]{1,0:T(8,128)S(1)}, f32[8,128]{1,0:T(8,128)S(1)}, f32[8,128]{1,0:T(8,128)S(1)}, f32[8,128]{1,0:T(8,128)S(1)}, s32[12,1,28]{2,1,0:T(1,128)S(4)}) custom-call(s32[12,1,28]{2,1,0:T(1,128)} %bitcast.25, bf16[28,12,128,128]{3,2,1,0:T(8,128)(2,1)} %bitcast.6), custom_call_target="tpu_custom_call" | custom-call | flops 75497472 | bytes 1048576 | tf_op jit(solution)/shard_map/outgoing_ones/pallas_call | solution.py:359
  2.1 3.0 %collective-permute-start = (f32[8,128]{1,0:T(8,128)S(1)}, f32[8,128]{1,0:T(8,128)S(1)}, u32[]{:S(2)}, u32[]{:S(2)}) collective-permute-start(f32[8,128]{1,0:T(8,128)S(1)} %get-tuple-element.51), channel_id=1, source_target_pairs={{0,1},{1,0},{2,3},{3,2},{4,5},{5,4},{6,7},{7,6},{8,9},{9,8},{10,11... | collective-permute-start | bytes 12296 | tf_op jit(solution)/shard_map/ppermute | solution.py:405
  5.2 0.0 collective-permute-start.1
  5.2 1.6 %collective-permute-start.2 = (f32[8,128]{1,0:T(8,128)S(1)}, f32[8,128]{1,0:T(8,128)S(1)}, u32[]{:S(2)}, u32[]{:S(2)}) collective-permute-start(f32[8,128]{1,0:T(8,128)S(1)} %get-tuple-element.54), channel_id=1, source_target_pairs={{8,16},{16,8},{9,17},{17,9},{10,18},{18,10},{11,19},{19,11},{12,20... | collective-permute-start | bytes 12296 | tf_op jit(solution)/shard_map/ppermute | solution.py:405
  6.8 0.0 collective-permute-start.3
  6.8 0.0 copy-done
  6.8 1.8 %local_degree.1.deg_ref = f32[28,128]{1,0:T(8,128)S(1)} custom-call(s32[12,1,28]{2,1,0:T(1,128)S(4)} %get-tuple-element.45.pattern_ref, bf16[28,12,128,128]{3,2,1,0:T(8,128)(2,1)S(1)} %bitcast.7), custom_call_target="tpu_custom_call" | custom-call | flops 352321536 | bytes 8388608 | tf_op jit(solution)/shard_map/local_degree/pallas_call | solution.py:359
  8.6 0.0 collective-permute-done.refs_0_
  8.6 0.0 collective-permute-done.1.refs_1_
  8.6 0.0 copy-done.1
  8.6 0.4 first_scaled.2
  9.0 3.1 %collective-permute-start.4 = (bf16[12,32,128]{2,1,0:T(8,128)(2,1)S(1)}, bf16[12,32,128]{2,1,0:T(8,128)(2,1)S(1)}, u32[]{:S(2)}, u32[]{:S(2)}) collective-permute-start(bf16[12,32,128]{2,1,0:T(8,128)(2,1)S(1)} %get-tuple-element.61), channel_id=1, source_target_pairs={{0,1},{1,0},{2,3},{3,2},{4,5},{5,4},{6,7},{7,6},{8,9},{9,8},{10,11... | collective-permute-start | bytes 294920 | tf_op jit(solution)/shard_map/ppermute | solution.py:405
  12.1 0.0 collective-permute-start.5
  12.1 0.0 collective-permute-done.2.refs_0_
  12.1 0.0 collective-permute-done.3.refs_1_
  12.2 0.4 first_scaled.3
  12.6 0.7 %collective-permute-start.6 = (bf16[12,32,128]{2,1,0:T(8,128)(2,1)S(1)}, bf16[12,32,128]{2,1,0:T(8,128)(2,1)S(1)}, u32[]{:S(2)}, u32[]{:S(2)}) collective-permute-start(bf16[12,32,128]{2,1,0:T(8,128)(2,1)S(1)} %get-tuple-element.64), channel_id=1, source_target_pairs={{8,16},{16,8},{9,17},{17,9},{10,18},{18,10},{11,19},{19,11},{12,20... | collective-permute-start | bytes 294920 | tf_op jit(solution)/shard_map/ppermute | solution.py:405
  13.3 0.0 collective-permute-start.7
  13.3 3.4 %own_terms_turning.1 = (f32[28,32,128]{2,1,0:T(8,128)S(1)}, bf16[28,12,128,128]{3,2,1,0:T(8,128)(2,1)S(1)}) custom-call(s32[12,1,28]{2,1,0:T(1,128)S(4)} %get-tuple-element.45.pattern_ref, bf16[28,12,128,128]{3,2,1,0:T(8,128)(2,1)S(1)} %bitcast.10, bf16[12,32,128]{2,1,0:T(8,128)(2,1)S(1)} %get-tuple-element.53.u_wide, ...), custom_call_target="tpu_custom_call" | custom-call | flops 704643072 | bytes 8388608 | tf_op jit(solution)/shard_map/own_terms_turning/pallas_call | solution.py:359
  16.6 0.0 collective-permute-done.4.refs_0_
  16.7 0.0 collective-permute-done.5.refs_1_
  16.7 0.6 %advance.4 = (f32[32,1536]{1,0:T(8,128)S(1)}, bf16[12,32,128]{2,1,0:T(8,128)(2,1)S(1)}, bf16[12,32,128]{2,1,0:T(8,128)(2,1)S(1)}, bf16[12,32,128]{2,1,0:T(8,128)(2,1)S(1)}) custom-call(s32[12,1,28]{2,1,0:T(1,128)S(4)} %get-tuple-element.45.pattern_ref, bf16[28,12,128,128]{3,2,1,0:T(8,128)(2,1)S(1)} %bitcast.11, ...), custom_call_target="tpu_custom_call" | custom-call | flops 75497472 | bytes 524288 | tf_op jit(solution)/shard_map/advance/pallas_call | solution.py:359
  17.3 3.1 %collective-permute-start.8 = (bf16[12,32,128]{2,1,0:T(8,128)(2,1)S(1)}, bf16[12,32,128]{2,1,0:T(8,128)(2,1)S(1)}, u32[]{:S(2)}, u32[]{:S(2)}) collective-permute-start(bf16[12,32,128]{2,1,0:T(8,128)(2,1)S(1)} %get-tuple-element.67), channel_id=1, source_target_pairs={{0,1},{1,0},{2,3},{3,2},{4,5},{5,4},{6,7},{7,6},{8,9},{9,8},{10,11... | collective-permute-start | bytes 294920 | tf_op jit(solution)/shard_map/ppermute | solution.py:405
  20.4 0.0 collective-permute-start.9
  20.4 0.0 collective-permute-done.6.refs_0_
  20.4 0.0 collective-permute-done.7.refs_1_
  20.4 0.6 %advance.5 = (f32[32,2048]{1,0:T(8,128)S(1)}, bf16[16,32,128]{2,1,0:T(8,128)(2,1)S(1)}, bf16[12,32,128]{2,1,0:T(8,128)(2,1)S(1)}, bf16[12,32,128]{2,1,0:T(8,128)(2,1)S(1)}) custom-call(s32[12,1,28]{2,1,0:T(1,128)S(4)} %get-tuple-element.45.pattern_ref, bf16[28,12,128,128]{3,2,1,0:T(8,128)(2,1)S(1)} %bitcast.12, ...), custom_call_target="tpu_custom_call" | custom-call | flops 75497472 | bytes 524288 | tf_op jit(solution)/shard_map/advance/pallas_call | solution.py:359
  21.0 1.7 %collective-permute-start.10 = (bf16[12,32,128]{2,1,0:T(8,128)(2,1)S(1)}, bf16[12,32,128]{2,1,0:T(8,128)(2,1)S(1)}, u32[]{:S(2)}, u32[]{:S(2)}) collective-permute-start(bf16[12,32,128]{2,1,0:T(8,128)(2,1)S(1)} %get-tuple-element.71), channel_id=1, source_target_pairs={{8,16},{16,8},{9,17},{17,9},{10,18},{18,10},{11,19},{19,11},{12,20... | collective-permute-start | bytes 294920 | tf_op jit(solution)/shard_map/ppermute | solution.py:405
  22.7 0.0 collective-permute-start.11
  22.7 2.9 %own_terms.2.acc_ref = f32[28,32,128]{2,1,0:T(8,128)S(1)} custom-call(s32[12,1,28]{2,1,0:T(1,128)S(4)} %get-tuple-element.45.pattern_ref, bf16[28,12,128,128]{3,2,1,0:T(8,128)(2,1)S(1)} %bitcast.13, bf16[28,12,128,128]{3,2,1,0:T(8,128)(2,1)S(1)} %get-tuple-element.57.turned_ref, bf16[12,32,128]{2,1,0:T(8,128)(2,1)S(1)} %get-tuple-element.63.u_wide, ...), custom_call_target="tpu_custom_call" | custom-call | flops 704643072 | bytes 8388608 | tf_op jit(solution)/shard_map/own_terms/pallas_call | solution.py:359
  25.6 0.0 collective-permute-done.8.refs_0_
  25.6 0.0 collective-permute-done.9.refs_1_
  25.6 0.6 %advance.6 = (f32[32,1536]{1,0:T(8,128)S(1)}, bf16[12,32,128]{2,1,0:T(8,128)(2,1)S(1)}, bf16[12,32,128]{2,1,0:T(8,128)(2,1)S(1)}, bf16[12,32,128]{2,1,0:T(8,128)(2,1)S(1)}) custom-call(s32[12,1,28]{2,1,0:T(1,128)S(4)} %get-tuple-element.45.pattern_ref, bf16[28,12,128,128]{3,2,1,0:T(8,128)(2,1)S(1)} %bitcast.14, ...), custom_call_target="tpu_custom_call" | custom-call | flops 75497472 | bytes 524288 | tf_op jit(solution)/shard_map/advance/pallas_call | solution.py:359
  26.2 3.1 %collective-permute-start.14 = (bf16[12,32,128]{2,1,0:T(8,128)(2,1)S(1)}, bf16[12,32,128]{2,1,0:T(8,128)(2,1)S(1)}, u32[]{:S(2)}, u32[]{:S(2)}) collective-permute-start(bf16[12,32,128]{2,1,0:T(8,128)(2,1)S(1)} %get-tuple-element.78), channel_id=1, source_target_pairs={{0,1},{1,0},{2,3},{3,2},{4,5},{5,4},{6,7},{7,6},{8,9},{9,8},{10,11... | collective-permute-start | bytes 294920 | tf_op jit(solution)/shard_map/ppermute | solution.py:405
  29.3 0.0 collective-permute-start.15
  29.3 0.0 collective-permute-done.10.refs_0_
  29.3 0.0 collective-permute-done.11.refs_1_
  29.3 0.6 %advance.7 = (f32[32,2048]{1,0:T(8,128)S(1)}, bf16[16,32,128]{2,1,0:T(8,128)(2,1)S(1)}, bf16[12,32,128]{2,1,0:T(8,128)(2,1)S(1)}, bf16[12,32,128]{2,1,0:T(8,128)(2,1)S(1)}) custom-call(s32[12,1,28]{2,1,0:T(1,128)S(4)} %get-tuple-element.45.pattern_ref, bf16[28,12,128,128]{3,2,1,0:T(8,128)(2,1)S(1)} %bitcast.15, ...), custom_call_target="tpu_custom_call" | custom-call | flops 75497472 | bytes 524288 | tf_op jit(solution)/shard_map/advance/pallas_call | solution.py:359
  29.9 0.7 %collective-permute-start.12 = (bf16[12,32,128]{2,1,0:T(8,128)(2,1)S(1)}, bf16[12,32,128]{2,1,0:T(8,128)(2,1)S(1)}, u32[]{:S(2)}, u32[]{:S(2)}) collective-permute-start(bf16[12,32,128]{2,1,0:T(8,128)(2,1)S(1)} %get-tuple-element.75), channel_id=1, source_target_pairs={{8,16},{16,8},{9,17},{17,9},{10,18},{18,10},{11,19},{19,11},{12,20... | collective-permute-start | bytes 294920 | tf_op jit(solution)/shard_map/ppermute | solution.py:405
  30.6 0.0 collective-permute-start.13
  30.6 3.0 %own_terms.3.acc_ref = f32[28,32,128]{2,1,0:T(8,128)S(1)} custom-call(s32[12,1,28]{2,1,0:T(1,128)S(4)} %get-tuple-element.45.pattern_ref, bf16[28,12,128,128]{3,2,1,0:T(8,128)(2,1)S(1)} %bitcast.16, bf16[28,12,128,128]{3,2,1,0:T(8,128)(2,1)S(1)} %get-tuple-element.57.turned_ref, bf16[12,32,128]{2,1,0:T(8,128)(2,1)S(1)} %get-tuple-element.70.u_wide, ...), custom_call_target="tpu_custom_call" | custom-call | flops 704643072 | bytes 8388608 | tf_op jit(solution)/shard_map/own_terms/pallas_call | solution.py:359
  33.6 0.0 collective-permute-done.14.refs_0_
  33.6 0.0 collective-permute-done.15.refs_1_
  33.6 0.7 %finish.2 = (f32[32,1536]{1,0:T(8,128)S(1)}, f32[8,128]{1,0:T(8,128)S(1)}) custom-call(s32[12,1,28]{2,1,0:T(1,128)S(4)} %get-tuple-element.45.pattern_ref, bf16[28,12,128,128]{3,2,1,0:T(8,128)(2,1)S(1)} %get-tuple-element.57.turned_ref, f32[12,128]{1,0:T(8,128)S(1)} %get-tuple-element.59.inv_ref, f32[28,32,128]{2,1,0:T(8,128)S(1)} %own_terms.3.acc_ref, ...), custom_call_target="tpu_custom_call" | custom-call | flops 37748736 | bytes 524288 | tf_op jit(solution)/shard_map/finish/pallas_call | solution.py:359
  34.3 0.1 collective-permute-done.12.refs_0_
  34.4 0.0 collective-permute-done.13.refs_1_
  34.4 0.7 %finish.3 = (f32[32,2048]{1,0:T(8,128)S(1)}, f32[32,8,128]{2,1,0:T(8,128)S(1)}) custom-call(s32[12,1,28]{2,1,0:T(1,128)S(4)} %get-tuple-element.45.pattern_ref, bf16[28,12,128,128]{3,2,1,0:T(8,128)(2,1)S(1)} %get-tuple-element.57.turned_ref, f32[16,128]{1,0:T(8,128)S(1)} %get-tuple-element.58.inv_ref, f32[28,32,128]{2,1,0:T(8,128)S(1)} %own_terms.3.acc_ref, ...), custom_call_target="tpu_custom_call" | custom-call | flops 37748736 | bytes 524288 | tf_op jit(solution)/shard_map/finish/pallas_call | solution.py:359
  35.2 11.1 %all_to_all.5.grams_ref = f32[32,8,128]{2,1,0:T(8,128)S(1)} all-to-all(f32[32,8,128]{2,1,0:T(8,128)S(1)} %get-tuple-element.82), channel_id=1, replica_groups=mesh['narrow'=4,'wide'=8] {'narrow','wide'}, dimensions={0} | all-to-all | bytes 262144 | tf_op jit(solution)/shard_map/all_to_all | solution.py:489
  46.3 2.1 %orthonormal.1 = f32[32,3584]{1,0:T(8,128)} custom-call(f32[32,8,128]{2,1,0:T(8,128)S(1)} %all_to_all.5.grams_ref, f32[32,1536]{1,0:T(8,128)S(1)} %get-tuple-element.83.wide_ref, f32[32,2048]{1,0:T(8,128)S(1)} %get-tuple-element.84.rest_ref), custom_call_target="tpu_custom_call" | custom-call | tf_op jit(solution)/shard_map/orthonormal/pallas_call | solution.py:359
Async XLA Ops:
  0.0 6.8 %copy-start = (bf16[1,1,28,12,128,128]{5,4,3,2,1,0:T(8,128)(2,1)S(1)}, bf16[1,1,28,12,128,128]{5,4,3,2,1,0:T(8,128)(2,1)}, u32[]{:S(2)}) copy-start(bf16[1,1,28,12,128,128]{5,4,3,2,1,0:T(8,128)(2,1)} %param.4) | copy-start | bytes 33030148
  0.0 8.6 %copy-start.1 = (bf16[1,1,32,3584]{3,2,1,0:T(8,128)(2,1)S(1)}, bf16[1,1,32,3584]{3,2,1,0:T(8,128)(2,1)}, u32[]{:S(2)}) copy-start(bf16[1,1,32,3584]{3,2,1,0:T(8,128)(2,1)} %param.3) | copy-start | bytes 688132
  2.1 6.5 %collective-permute-start = (f32[8,128]{1,0:T(8,128)S(1)}, f32[8,128]{1,0:T(8,128)S(1)}, u32[]{:S(2)}, u32[]{:S(2)}) collective-permute-start(f32[8,128]{1,0:T(8,128)S(1)} %get-tuple-element.51), channel_id=1, source_target_pairs={{0,1},{1,0},{2,3},{3,2},{4,5},{5,4},{6,7},{7,6},{8,9},{9,8},{10,11... | collective-permute-start | bytes 12296 | tf_op jit(solution)/shard_map/ppermute | solution.py:405
  5.2 3.5 %collective-permute-start.1 = (f32[8,128]{1,0:T(8,128)S(1)}, f32[8,128]{1,0:T(8,128)S(1)}, u32[]{:S(2)}, u32[]{:S(2)}) collective-permute-start(f32[8,128]{1,0:T(8,128)S(1)} %get-tuple-element.52), channel_id=1, source_target_pairs={{1,2},{2,1},{3,4},{4,3},{5,6},{6,5},{9,10},{10,9},{11,12},{12,11},... | collective-permute-start | bytes 12296 | tf_op jit(solution)/shard_map/ppermute | solution.py:405
  5.2 7.0 %collective-permute-start.2 = (f32[8,128]{1,0:T(8,128)S(1)}, f32[8,128]{1,0:T(8,128)S(1)}, u32[]{:S(2)}, u32[]{:S(2)}) collective-permute-start(f32[8,128]{1,0:T(8,128)S(1)} %get-tuple-element.54), channel_id=1, source_target_pairs={{8,16},{16,8},{9,17},{17,9},{10,18},{18,10},{11,19},{19,11},{12,20... | collective-permute-start | bytes 12296 | tf_op jit(solution)/shard_map/ppermute | solution.py:405
  6.8 5.4 %collective-permute-start.3 = (f32[8,128]{1,0:T(8,128)S(1)}, f32[8,128]{1,0:T(8,128)S(1)}, u32[]{:S(2)}, u32[]{:S(2)}) collective-permute-start(f32[8,128]{1,0:T(8,128)S(1)} %get-tuple-element.55), channel_id=1, source_target_pairs={{0,8},{8,0},{16,24},{24,16},{1,9},{9,1},{17,25},{25,17},{2,10},{10... | collective-permute-start | bytes 12296 | tf_op jit(solution)/shard_map/ppermute | solution.py:405
  9.0 7.6 %collective-permute-start.4 = (bf16[12,32,128]{2,1,0:T(8,128)(2,1)S(1)}, bf16[12,32,128]{2,1,0:T(8,128)(2,1)S(1)}, u32[]{:S(2)}, u32[]{:S(2)}) collective-permute-start(bf16[12,32,128]{2,1,0:T(8,128)(2,1)S(1)} %get-tuple-element.61), channel_id=1, source_target_pairs={{0,1},{1,0},{2,3},{3,2},{4,5},{5,4},{6,7},{7,6},{8,9},{9,8},{10,11... | collective-permute-start | bytes 294920 | tf_op jit(solution)/shard_map/ppermute | solution.py:405
  12.1 4.5 %collective-permute-start.5 = (bf16[12,32,128]{2,1,0:T(8,128)(2,1)S(1)}, bf16[12,32,128]{2,1,0:T(8,128)(2,1)S(1)}, u32[]{:S(2)}, u32[]{:S(2)}) collective-permute-start(bf16[12,32,128]{2,1,0:T(8,128)(2,1)S(1)} %get-tuple-element.62), channel_id=1, source_target_pairs={{1,2},{2,1},{3,4},{4,3},{5,6},{6,5},{9,10},{10,9},{11,12},{12,11},... | collective-permute-start | bytes 294920 | tf_op jit(solution)/shard_map/ppermute | solution.py:405
  12.6 7.8 %collective-permute-start.6 = (bf16[12,32,128]{2,1,0:T(8,128)(2,1)S(1)}, bf16[12,32,128]{2,1,0:T(8,128)(2,1)S(1)}, u32[]{:S(2)}, u32[]{:S(2)}) collective-permute-start(bf16[12,32,128]{2,1,0:T(8,128)(2,1)S(1)} %get-tuple-element.64), channel_id=1, source_target_pairs={{8,16},{16,8},{9,17},{17,9},{10,18},{18,10},{11,19},{19,11},{12,20... | collective-permute-start | bytes 294920 | tf_op jit(solution)/shard_map/ppermute | solution.py:405
  13.3 7.1 %collective-permute-start.7 = (bf16[12,32,128]{2,1,0:T(8,128)(2,1)S(1)}, bf16[12,32,128]{2,1,0:T(8,128)(2,1)S(1)}, u32[]{:S(2)}, u32[]{:S(2)}) collective-permute-start(bf16[12,32,128]{2,1,0:T(8,128)(2,1)S(1)} %get-tuple-element.65), channel_id=1, source_target_pairs={{0,8},{8,0},{16,24},{24,16},{1,9},{9,1},{17,25},{25,17},{2,10},{10... | collective-permute-start | bytes 294920 | tf_op jit(solution)/shard_map/ppermute | solution.py:405
  17.3 8.3 %collective-permute-start.8 = (bf16[12,32,128]{2,1,0:T(8,128)(2,1)S(1)}, bf16[12,32,128]{2,1,0:T(8,128)(2,1)S(1)}, u32[]{:S(2)}, u32[]{:S(2)}) collective-permute-start(bf16[12,32,128]{2,1,0:T(8,128)(2,1)S(1)} %get-tuple-element.67), channel_id=1, source_target_pairs={{0,1},{1,0},{2,3},{3,2},{4,5},{5,4},{6,7},{7,6},{8,9},{9,8},{10,11... | collective-permute-start | bytes 294920 | tf_op jit(solution)/shard_map/ppermute | solution.py:405
  20.4 5.2 %collective-permute-start.9 = (bf16[12,32,128]{2,1,0:T(8,128)(2,1)S(1)}, bf16[12,32,128]{2,1,0:T(8,128)(2,1)S(1)}, u32[]{:S(2)}, u32[]{:S(2)}) collective-permute-start(bf16[12,32,128]{2,1,0:T(8,128)(2,1)S(1)} %get-tuple-element.68), channel_id=1, source_target_pairs={{1,2},{2,1},{3,4},{4,3},{5,6},{6,5},{9,10},{10,9},{11,12},{12,11},... | collective-permute-start | bytes 294920 | tf_op jit(solution)/shard_map/ppermute | solution.py:405
  21.0 8.3 %collective-permute-start.10 = (bf16[12,32,128]{2,1,0:T(8,128)(2,1)S(1)}, bf16[12,32,128]{2,1,0:T(8,128)(2,1)S(1)}, u32[]{:S(2)}, u32[]{:S(2)}) collective-permute-start(bf16[12,32,128]{2,1,0:T(8,128)(2,1)S(1)} %get-tuple-element.71), channel_id=1, source_target_pairs={{8,16},{16,8},{9,17},{17,9},{10,18},{18,10},{11,19},{19,11},{12,20... | collective-permute-start | bytes 294920 | tf_op jit(solution)/shard_map/ppermute | solution.py:405
  22.7 6.6 %collective-permute-start.11 = (bf16[12,32,128]{2,1,0:T(8,128)(2,1)S(1)}, bf16[12,32,128]{2,1,0:T(8,128)(2,1)S(1)}, u32[]{:S(2)}, u32[]{:S(2)}) collective-permute-start(bf16[12,32,128]{2,1,0:T(8,128)(2,1)S(1)} %get-tuple-element.72), channel_id=1, source_target_pairs={{0,8},{8,0},{16,24},{24,16},{1,9},{9,1},{17,25},{25,17},{2,10},{10... | collective-permute-start | bytes 294920 | tf_op jit(solution)/shard_map/ppermute | solution.py:405
  26.2 7.4 %collective-permute-start.14 = (bf16[12,32,128]{2,1,0:T(8,128)(2,1)S(1)}, bf16[12,32,128]{2,1,0:T(8,128)(2,1)S(1)}, u32[]{:S(2)}, u32[]{:S(2)}) collective-permute-start(bf16[12,32,128]{2,1,0:T(8,128)(2,1)S(1)} %get-tuple-element.78), channel_id=1, source_target_pairs={{0,1},{1,0},{2,3},{3,2},{4,5},{5,4},{6,7},{7,6},{8,9},{9,8},{10,11... | collective-permute-start | bytes 294920 | tf_op jit(solution)/shard_map/ppermute | solution.py:405
  29.3 4.3 %collective-permute-start.15 = (bf16[12,32,128]{2,1,0:T(8,128)(2,1)S(1)}, bf16[12,32,128]{2,1,0:T(8,128)(2,1)S(1)}, u32[]{:S(2)}, u32[]{:S(2)}) collective-permute-start(bf16[12,32,128]{2,1,0:T(8,128)(2,1)S(1)} %get-tuple-element.79), channel_id=1, source_target_pairs={{1,2},{2,1},{3,4},{4,3},{5,6},{6,5},{9,10},{10,9},{11,12},{12,11},... | collective-permute-start | bytes 294920 | tf_op jit(solution)/shard_map/ppermute | solution.py:405
  29.9 4.5 %collective-permute-start.12 = (bf16[12,32,128]{2,1,0:T(8,128)(2,1)S(1)}, bf16[12,32,128]{2,1,0:T(8,128)(2,1)S(1)}, u32[]{:S(2)}, u32[]{:S(2)}) collective-permute-start(bf16[12,32,128]{2,1,0:T(8,128)(2,1)S(1)} %get-tuple-element.75), channel_id=1, source_target_pairs={{8,16},{16,8},{9,17},{17,9},{10,18},{18,10},{11,19},{19,11},{12,20... | collective-permute-start | bytes 294920 | tf_op jit(solution)/shard_map/ppermute | solution.py:405
  30.6 3.8 %collective-permute-start.13 = (bf16[12,32,128]{2,1,0:T(8,128)(2,1)S(1)}, bf16[12,32,128]{2,1,0:T(8,128)(2,1)S(1)}, u32[]{:S(2)}, u32[]{:S(2)}) collective-permute-start(bf16[12,32,128]{2,1,0:T(8,128)(2,1)S(1)} %get-tuple-element.76), channel_id=1, source_target_pairs={{0,8},{8,0},{16,24},{24,16},{1,9},{9,1},{17,25},{25,17},{2,10},{10... | collective-permute-start | bytes 294920 | tf_op jit(solution)/shard_map/ppermute | solution.py:405

commit v6 on v5

--- a/solution.py
+++ b/solution.py
@@ -183,19 +183,14 @@
 def own_products(pattern_ref, w_ref, turned, u_ref, acc_ref):
     blocks, slots = w_ref.shape[:2]
     for b in range(blocks):
-        both = mm(u_ref[b], beside([w_ref[b, 0], turned(b, 0)]), ROWS_BY_COLS)
-        acc_ref[b] = both[:, :LANES] + both[:, LANES:]
+        acc_ref[b] = mm(u_ref[b], turned(b, 0), ROWS_BY_COLS)
     for b in range(blocks):
-        total = None
-        own = INNER if b < RIMS * RIM else slots
-        for group in slot_pairs(1, own):
-            part = mm(u_ref[b], beside([w_ref[b, s] for s in group]), ROWS_BY_COLS)
-            for i, s in enumerate(group):
-                acc_ref[pattern_ref[s, 0, b]] += part[:, i * LANES : (i + 1) * LANES]
-            ahead = beside([u_ref[pattern_ref[s, 0, b]] for s in group])
-            ahead = mm(ahead, over([turned(b, s) for s in group]), ROWS_BY_COLS)
-            total = ahead if total is None else total + ahead
-        acc_ref[b] += total
+        group = range(1, INNER if b < RIMS * RIM else slots)
+        part = mm(u_ref[b], beside([w_ref[b, s] for s in group]), ROWS_BY_COLS)
+        for i, s in enumerate(group):
+            acc_ref[pattern_ref[s, 0, b]] += part[:, i * LANES : (i + 1) * LANES]
+        ahead = beside([u_ref[pattern_ref[s, 0, b]] for s in group])
+        acc_ref[b] += mm(ahead, over([turned(b, s) for s in group]), ROWS_BY_COLS)
 
 
 def own_terms(pattern_ref, w_ref, turned_ref, u_wide, u_rest, acc_ref, u):
@@ -208,6 +203,8 @@
 
     def turned(b, s):
         block = w_ref[b, s].T
+        if s == 0:
+            block = (block.astype(F32) + w_ref[b, s].astype(F32)).astype(BF16)
         turned_ref[b, s] = block
         return block
 

time: 48.5 us -> 48.2 us (level)
  Pallas kernels: 19.9 us -> 19.4 us
  transfers between devices with their start and end apart: 16 -> 16, of which waited for: 1 -> 2; matrix products, arithmetic and copies ran while one was open for 0% -> 0% of each run, Pallas kernels for 31% -> 30%
where the time goes in v6:
time: 48.2 us; the launch traced here: 48 us
  Pallas kernels  19.4 us (40%)
  starting transfers between devices  17 us (35%)
  blocking collectives  11 us (23%)
    pallas_call x14, Pallas kernels, kernel_call(): pl.pallas_call(body, name=name, out_shape=[pltpu.SMEM(s, d) if d == jnp.i...  19.4 us
    ppermute x16, starting transfers between devices, exchange(): lax.ppermute(payload, ('narrow', 'wide'), pairs[m])  17 us
    all_to_all x1, blocking collectives, body(): grams = lax.all_to_all(grams, ('narrow', 'wide'), 0, 0)  11 us
  transfers between devices with their start and end apart: 16, of which 2 were waited for; matrix products, arithmetic and copies ran while one was open for 0% of the time, Pallas kernels for 30%

profile of v6, /device:TPU:0, one launch (start us, length us, event | category | flops | bytes accessed | tf_op | source)
XLA Modules:
  0.0 48.0 jit_solution(16585800178474244735)
XLA Ops:
  0.0 0.0 copy-start
  0.0 0.0 copy-start.1
  0.0 2.1 %outgoing_ones.1 = (f32[8,128]{1,0:T(8,128)S(1)}, f32[8,128]{1,0:T(8,128)S(1)}, f32[8,128]{1,0:T(8,128)S(1)}, f32[8,128]{1,0:T(8,128)S(1)}, s32[12,1,28]{2,1,0:T(1,128)S(4)}) custom-call(s32[12,1,28]{2,1,0:T(1,128)} %bitcast.25, bf16[28,12,128,128]{3,2,1,0:T(8,128)(2,1)} %bitcast.6), custom_call_target="tpu_custom_call" | custom-call | flops 75497472 | bytes 1048576 | tf_op jit(solution)/shard_map/outgoing_ones/pallas_call | solution.py:356
  2.1 3.0 %collective-permute-start = (f32[8,128]{1,0:T(8,128)S(1)}, f32[8,128]{1,0:T(8,128)S(1)}, u32[]{:S(2)}, u32[]{:S(2)}) collective-permute-start(f32[8,128]{1,0:T(8,128)S(1)} %get-tuple-element.51), channel_id=1, source_target_pairs={{0,1},{1,0},{2,3},{3,2},{4,5},{5,4},{6,7},{7,6},{8,9},{9,8},{10,11... | collective-permute-start | bytes 12296 | tf_op jit(solution)/shard_map/ppermute | solution.py:402
  5.2 0.0 collective-permute-start.1
  5.2 1.6 %collective-permute-start.2 = (f32[8,128]{1,0:T(8,128)S(1)}, f32[8,128]{1,0:T(8,128)S(1)}, u32[]{:S(2)}, u32[]{:S(2)}) collective-permute-start(f32[8,128]{1,0:T(8,128)S(1)} %get-tuple-element.54), channel_id=1, source_target_pairs={{8,16},{16,8},{9,17},{17,9},{10,18},{18,10},{11,19},{19,11},{12,20... | collective-permute-start | bytes 12296 | tf_op jit(solution)/shard_map/ppermute | solution.py:402
  6.8 0.0 collective-permute-start.3
  6.8 0.0 copy-done
  6.8 1.8 %local_degree.1.deg_ref = f32[28,128]{1,0:T(8,128)S(1)} custom-call(s32[12,1,28]{2,1,0:T(1,128)S(4)} %get-tuple-element.45.pattern_ref, bf16[28,12,128,128]{3,2,1,0:T(8,128)(2,1)S(1)} %bitcast.7), custom_call_target="tpu_custom_call" | custom-call | flops 352321536 | bytes 8388608 | tf_op jit(solution)/shard_map/local_degree/pallas_call | solution.py:356
  8.6 0.0 collective-permute-done.refs_0_
  8.6 0.0 collective-permute-done.1.refs_1_
  8.6 0.0 copy-done.1
  8.6 0.4 first_scaled.2
  9.1 3.1 %collective-permute-start.4 = (bf16[12,32,128]{2,1,0:T(8,128)(2,1)S(1)}, bf16[12,32,128]{2,1,0:T(8,128)(2,1)S(1)}, u32[]{:S(2)}, u32[]{:S(2)}) collective-permute-start(bf16[12,32,128]{2,1,0:T(8,128)(2,1)S(1)} %get-tuple-element.61), channel_id=1, source_target_pairs={{0,1},{1,0},{2,3},{3,2},{4,5},{5,4},{6,7},{7,6},{8,9},{9,8},{10,11... | collective-permute-start | bytes 294920 | tf_op jit(solution)/shard_map/ppermute | solution.py:402
  12.1 0.0 collective-permute-start.5
  12.1 0.0 collective-permute-done.2.refs_0_
  12.1 0.0 collective-permute-done.3.refs_1_
  12.1 0.4 first_scaled.3
  12.6 0.7 %collective-permute-start.6 = (bf16[12,32,128]{2,1,0:T(8,128)(2,1)S(1)}, bf16[12,32,128]{2,1,0:T(8,128)(2,1)S(1)}, u32[]{:S(2)}, u32[]{:S(2)}) collective-permute-start(bf16[12,32,128]{2,1,0:T(8,128)(2,1)S(1)} %get-tuple-element.64), channel_id=1, source_target_pairs={{8,16},{16,8},{9,17},{17,9},{10,18},{18,10},{11,19},{19,11},{12,20... | collective-permute-start | bytes 294920 | tf_op jit(solution)/shard_map/ppermute | solution.py:402
  13.3 0.0 collective-permute-start.7
  13.3 3.2 %own_terms_turning.1 = (f32[28,32,128]{2,1,0:T(8,128)S(1)}, bf16[28,12,128,128]{3,2,1,0:T(8,128)(2,1)S(1)}) custom-call(s32[12,1,28]{2,1,0:T(1,128)S(4)} %get-tuple-element.45.pattern_ref, bf16[28,12,128,128]{3,2,1,0:T(8,128)(2,1)S(1)} %bitcast.10, bf16[12,32,128]{2,1,0:T(8,128)(2,1)S(1)} %get-tuple-element.53.u_wide, ...), custom_call_target="tpu_custom_call" | custom-call | flops 704643072 | bytes 8388608 | tf_op jit(solution)/shard_map/own_terms_turning/pallas_call | solution.py:356
  16.4 0.0 collective-permute-done.4.refs_0_
  16.5 0.0 collective-permute-done.5.refs_1_
  16.5 0.6 %advance.4 = (f32[32,1536]{1,0:T(8,128)S(1)}, bf16[12,32,128]{2,1,0:T(8,128)(2,1)S(1)}, bf16[12,32,128]{2,1,0:T(8,128)(2,1)S(1)}, bf16[12,32,128]{2,1,0:T(8,128)(2,1)S(1)}) custom-call(s32[12,1,28]{2,1,0:T(1,128)S(4)} %get-tuple-element.45.pattern_ref, bf16[28,12,128,128]{3,2,1,0:T(8,128)(2,1)S(1)} %bitcast.11, ...), custom_call_target="tpu_custom_call" | custom-call | flops 75497472 | bytes 524288 | tf_op jit(solution)/shard_map/advance/pallas_call | solution.py:356
  17.1 3.1 %collective-permute-start.8 = (bf16[12,32,128]{2,1,0:T(8,128)(2,1)S(1)}, bf16[12,32,128]{2,1,0:T(8,128)(2,1)S(1)}, u32[]{:S(2)}, u32[]{:S(2)}) collective-permute-start(bf16[12,32,128]{2,1,0:T(8,128)(2,1)S(1)} %get-tuple-element.67), channel_id=1, source_target_pairs={{0,1},{1,0},{2,3},{3,2},{4,5},{5,4},{6,7},{7,6},{8,9},{9,8},{10,11... | collective-permute-start | bytes 294920 | tf_op jit(solution)/shard_map/ppermute | solution.py:402
  20.2 0.0 collective-permute-start.9
  20.2 0.0 collective-permute-done.6.refs_0_
  20.2 0.0 collective-permute-done.7.refs_1_
  20.2 0.6 %advance.5 = (f32[32,2048]{1,0:T(8,128)S(1)}, bf16[16,32,128]{2,1,0:T(8,128)(2,1)S(1)}, bf16[12,32,128]{2,1,0:T(8,128)(2,1)S(1)}, bf16[12,32,128]{2,1,0:T(8,128)(2,1)S(1)}) custom-call(s32[12,1,28]{2,1,0:T(1,128)S(4)} %get-tuple-element.45.pattern_ref, bf16[28,12,128,128]{3,2,1,0:T(8,128)(2,1)S(1)} %bitcast.12, ...), custom_call_target="tpu_custom_call" | custom-call | flops 75497472 | bytes 524288 | tf_op jit(solution)/shard_map/advance/pallas_call | solution.py:356
  20.8 1.7 %collective-permute-start.10 = (bf16[12,32,128]{2,1,0:T(8,128)(2,1)S(1)}, bf16[12,32,128]{2,1,0:T(8,128)(2,1)S(1)}, u32[]{:S(2)}, u32[]{:S(2)}) collective-permute-start(bf16[12,32,128]{2,1,0:T(8,128)(2,1)S(1)} %get-tuple-element.71), channel_id=1, source_target_pairs={{8,16},{16,8},{9,17},{17,9},{10,18},{18,10},{11,19},{19,11},{12,20... | collective-permute-start | bytes 294920 | tf_op jit(solution)/shard_map/ppermute | solution.py:402
  22.5 0.0 collective-permute-start.11
  22.5 2.7 %own_terms.2.acc_ref = f32[28,32,128]{2,1,0:T(8,128)S(1)} custom-call(s32[12,1,28]{2,1,0:T(1,128)S(4)} %get-tuple-element.45.pattern_ref, bf16[28,12,128,128]{3,2,1,0:T(8,128)(2,1)S(1)} %bitcast.13, bf16[28,12,128,128]{3,2,1,0:T(8,128)(2,1)S(1)} %get-tuple-element.57.turned_ref, bf16[12,32,128]{2,1,0:T(8,128)(2,1)S(1)} %get-tuple-element.63.u_wide, ...), custom_call_target="tpu_custom_call" | custom-call | flops 704643072 | bytes 8388608 | tf_op jit(solution)/shard_map/own_terms/pallas_call | solution.py:356
  25.2 0.0 collective-permute-done.8.refs_0_
  25.2 0.0 collective-permute-done.9.refs_1_
  25.2 0.6 %advance.6 = (f32[32,1536]{1,0:T(8,128)S(1)}, bf16[12,32,128]{2,1,0:T(8,128)(2,1)S(1)}, bf16[12,32,128]{2,1,0:T(8,128)(2,1)S(1)}, bf16[12,32,128]{2,1,0:T(8,128)(2,1)S(1)}) custom-call(s32[12,1,28]{2,1,0:T(1,128)S(4)} %get-tuple-element.45.pattern_ref, bf16[28,12,128,128]{3,2,1,0:T(8,128)(2,1)S(1)} %bitcast.14, ...), custom_call_target="tpu_custom_call" | custom-call | flops 75497472 | bytes 524288 | tf_op jit(solution)/shard_map/advance/pallas_call | solution.py:356
  25.8 3.1 %collective-permute-start.14 = (bf16[12,32,128]{2,1,0:T(8,128)(2,1)S(1)}, bf16[12,32,128]{2,1,0:T(8,128)(2,1)S(1)}, u32[]{:S(2)}, u32[]{:S(2)}) collective-permute-start(bf16[12,32,128]{2,1,0:T(8,128)(2,1)S(1)} %get-tuple-element.78), channel_id=1, source_target_pairs={{0,1},{1,0},{2,3},{3,2},{4,5},{5,4},{6,7},{7,6},{8,9},{9,8},{10,11... | collective-permute-start | bytes 294920 | tf_op jit(solution)/shard_map/ppermute | solution.py:402
  28.9 0.0 collective-permute-start.15
  28.9 0.0 collective-permute-done.10.refs_0_
  28.9 0.0 collective-permute-done.11.refs_1_
  28.9 0.8 %advance.7 = (f32[32,2048]{1,0:T(8,128)S(1)}, bf16[16,32,128]{2,1,0:T(8,128)(2,1)S(1)}, bf16[12,32,128]{2,1,0:T(8,128)(2,1)S(1)}, bf16[12,32,128]{2,1,0:T(8,128)(2,1)S(1)}) custom-call(s32[12,1,28]{2,1,0:T(1,128)S(4)} %get-tuple-element.45.pattern_ref, bf16[28,12,128,128]{3,2,1,0:T(8,128)(2,1)S(1)} %bitcast.15, ...), custom_call_target="tpu_custom_call" | custom-call | flops 75497472 | bytes 524288 | tf_op jit(solution)/shard_map/advance/pallas_call | solution.py:356
  29.7 0.7 %collective-permute-start.12 = (bf16[12,32,128]{2,1,0:T(8,128)(2,1)S(1)}, bf16[12,32,128]{2,1,0:T(8,128)(2,1)S(1)}, u32[]{:S(2)}, u32[]{:S(2)}) collective-permute-start(bf16[12,32,128]{2,1,0:T(8,128)(2,1)S(1)} %get-tuple-element.75), channel_id=1, source_target_pairs={{8,16},{16,8},{9,17},{17,9},{10,18},{18,10},{11,19},{19,11},{12,20... | collective-permute-start | bytes 294920 | tf_op jit(solution)/shard_map/ppermute | solution.py:402
  30.4 0.0 collective-permute-start.13
  30.4 2.7 %own_terms.3.acc_ref = f32[28,32,128]{2,1,0:T(8,128)S(1)} custom-call(s32[12,1,28]{2,1,0:T(1,128)S(4)} %get-tuple-element.45.pattern_ref, bf16[28,12,128,128]{3,2,1,0:T(8,128)(2,1)S(1)} %bitcast.16, bf16[28,12,128,128]{3,2,1,0:T(8,128)(2,1)S(1)} %get-tuple-element.57.turned_ref, bf16[12,32,128]{2,1,0:T(8,128)(2,1)S(1)} %get-tuple-element.70.u_wide, ...), custom_call_target="tpu_custom_call" | custom-call | flops 704643072 | bytes 8388608 | tf_op jit(solution)/shard_map/own_terms/pallas_call | solution.py:356
  33.1 0.1 collective-permute-done.14.refs_0_
  33.2 0.0 collective-permute-done.15.refs_1_
  33.2 0.7 %finish.2 = (f32[32,1536]{1,0:T(8,128)S(1)}, f32[8,128]{1,0:T(8,128)S(1)}) custom-call(s32[12,1,28]{2,1,0:T(1,128)S(4)} %get-tuple-element.45.pattern_ref, bf16[28,12,128,128]{3,2,1,0:T(8,128)(2,1)S(1)} %get-tuple-element.57.turned_ref, f32[12,128]{1,0:T(8,128)S(1)} %get-tuple-element.59.inv_ref, f32[28,32,128]{2,1,0:T(8,128)S(1)} %own_terms.3.acc_ref, ...), custom_call_target="tpu_custom_call" | custom-call | flops 37748736 | bytes 524288 | tf_op jit(solution)/shard_map/finish/pallas_call | solution.py:356
  33.9 0.3 collective-permute-done.12.refs_0_
  34.2 0.0 collective-permute-done.13.refs_1_
  34.2 0.7 %finish.3 = (f32[32,2048]{1,0:T(8,128)S(1)}, f32[32,8,128]{2,1,0:T(8,128)S(1)}) custom-call(s32[12,1,28]{2,1,0:T(1,128)S(4)} %get-tuple-element.45.pattern_ref, bf16[28,12,128,128]{3,2,1,0:T(8,128)(2,1)S(1)} %get-tuple-element.57.turned_ref, f32[16,128]{1,0:T(8,128)S(1)} %get-tuple-element.58.inv_ref, f32[28,32,128]{2,1,0:T(8,128)S(1)} %own_terms.3.acc_ref, ...), custom_call_target="tpu_custom_call" | custom-call | flops 37748736 | bytes 524288 | tf_op jit(solution)/shard_map/finish/pallas_call | solution.py:356
  35.0 11.0 %all_to_all.5.grams_ref = f32[32,8,128]{2,1,0:T(8,128)S(1)} all-to-all(f32[32,8,128]{2,1,0:T(8,128)S(1)} %get-tuple-element.82), channel_id=1, replica_groups=mesh['narrow'=4,'wide'=8] {'narrow','wide'}, dimensions={0} | all-to-all | bytes 262144 | tf_op jit(solution)/shard_map/all_to_all | solution.py:486
  46.0 2.1 %orthonormal.1 = f32[32,3584]{1,0:T(8,128)} custom-call(f32[32,8,128]{2,1,0:T(8,128)S(1)} %all_to_all.5.grams_ref, f32[32,1536]{1,0:T(8,128)S(1)} %get-tuple-element.83.wide_ref, f32[32,2048]{1,0:T(8,128)S(1)} %get-tuple-element.84.rest_ref), custom_call_target="tpu_custom_call" | custom-call | tf_op jit(solution)/shard_map/orthonormal/pallas_call | solution.py:356
Async XLA Ops:
  0.0 6.8 %copy-start = (bf16[1,1,28,12,128,128]{5,4,3,2,1,0:T(8,128)(2,1)S(1)}, bf16[1,1,28,12,128,128]{5,4,3,2,1,0:T(8,128)(2,1)}, u32[]{:S(2)}) copy-start(bf16[1,1,28,12,128,128]{5,4,3,2,1,0:T(8,128)(2,1)} %param.4) | copy-start | bytes 33030148
  0.0 8.6 %copy-start.1 = (bf16[1,1,32,3584]{3,2,1,0:T(8,128)(2,1)S(1)}, bf16[1,1,32,3584]{3,2,1,0:T(8,128)(2,1)}, u32[]{:S(2)}) copy-start(bf16[1,1,32,3584]{3,2,1,0:T(8,128)(2,1)} %param.3) | copy-start | bytes 688132
  2.1 6.5 %collective-permute-start = (f32[8,128]{1,0:T(8,128)S(1)}, f32[8,128]{1,0:T(8,128)S(1)}, u32[]{:S(2)}, u32[]{:S(2)}) collective-permute-start(f32[8,128]{1,0:T(8,128)S(1)} %get-tuple-element.51), channel_id=1, source_target_pairs={{0,1},{1,0},{2,3},{3,2},{4,5},{5,4},{6,7},{7,6},{8,9},{9,8},{10,11... | collective-permute-start | bytes 12296 | tf_op jit(solution)/shard_map/ppermute | solution.py:402
  5.2 3.5 %collective-permute-start.1 = (f32[8,128]{1,0:T(8,128)S(1)}, f32[8,128]{1,0:T(8,128)S(1)}, u32[]{:S(2)}, u32[]{:S(2)}) collective-permute-start(f32[8,128]{1,0:T(8,128)S(1)} %get-tuple-element.52), channel_id=1, source_target_pairs={{1,2},{2,1},{3,4},{4,3},{5,6},{6,5},{9,10},{10,9},{11,12},{12,11},... | collective-permute-start | bytes 12296 | tf_op jit(solution)/shard_map/ppermute | solution.py:402
  5.2 7.0 %collective-permute-start.2 = (f32[8,128]{1,0:T(8,128)S(1)}, f32[8,128]{1,0:T(8,128)S(1)}, u32[]{:S(2)}, u32[]{:S(2)}) collective-permute-start(f32[8,128]{1,0:T(8,128)S(1)} %get-tuple-element.54), channel_id=1, source_target_pairs={{8,16},{16,8},{9,17},{17,9},{10,18},{18,10},{11,19},{19,11},{12,20... | collective-permute-start | bytes 12296 | tf_op jit(solution)/shard_map/ppermute | solution.py:402
  6.8 5.4 %collective-permute-start.3 = (f32[8,128]{1,0:T(8,128)S(1)}, f32[8,128]{1,0:T(8,128)S(1)}, u32[]{:S(2)}, u32[]{:S(2)}) collective-permute-start(f32[8,128]{1,0:T(8,128)S(1)} %get-tuple-element.55), channel_id=1, source_target_pairs={{0,8},{8,0},{16,24},{24,16},{1,9},{9,1},{17,25},{25,17},{2,10},{10... | collective-permute-start | bytes 12296 | tf_op jit(solution)/shard_map/ppermute | solution.py:402
  9.1 7.4 %collective-permute-start.4 = (bf16[12,32,128]{2,1,0:T(8,128)(2,1)S(1)}, bf16[12,32,128]{2,1,0:T(8,128)(2,1)S(1)}, u32[]{:S(2)}, u32[]{:S(2)}) collective-permute-start(bf16[12,32,128]{2,1,0:T(8,128)(2,1)S(1)} %get-tuple-element.61), channel_id=1, source_target_pairs={{0,1},{1,0},{2,3},{3,2},{4,5},{5,4},{6,7},{7,6},{8,9},{9,8},{10,11... | collective-permute-start | bytes 294920 | tf_op jit(solution)/shard_map/ppermute | solution.py:402
  12.1 4.3 %collective-permute-start.5 = (bf16[12,32,128]{2,1,0:T(8,128)(2,1)S(1)}, bf16[12,32,128]{2,1,0:T(8,128)(2,1)S(1)}, u32[]{:S(2)}, u32[]{:S(2)}) collective-permute-start(bf16[12,32,128]{2,1,0:T(8,128)(2,1)S(1)} %get-tuple-element.62), channel_id=1, source_target_pairs={{1,2},{2,1},{3,4},{4,3},{5,6},{6,5},{9,10},{10,9},{11,12},{12,11},... | collective-permute-start | bytes 294920 | tf_op jit(solution)/shard_map/ppermute | solution.py:402
  12.6 7.6 %collective-permute-start.6 = (bf16[12,32,128]{2,1,0:T(8,128)(2,1)S(1)}, bf16[12,32,128]{2,1,0:T(8,128)(2,1)S(1)}, u32[]{:S(2)}, u32[]{:S(2)}) collective-permute-start(bf16[12,32,128]{2,1,0:T(8,128)(2,1)S(1)} %get-tuple-element.64), channel_id=1, source_target_pairs={{8,16},{16,8},{9,17},{17,9},{10,18},{18,10},{11,19},{19,11},{12,20... | collective-permute-start | bytes 294920 | tf_op jit(solution)/shard_map/ppermute | solution.py:402
  13.3 6.9 %collective-permute-start.7 = (bf16[12,32,128]{2,1,0:T(8,128)(2,1)S(1)}, bf16[12,32,128]{2,1,0:T(8,128)(2,1)S(1)}, u32[]{:S(2)}, u32[]{:S(2)}) collective-permute-start(bf16[12,32,128]{2,1,0:T(8,128)(2,1)S(1)} %get-tuple-element.65), channel_id=1, source_target_pairs={{0,8},{8,0},{16,24},{24,16},{1,9},{9,1},{17,25},{25,17},{2,10},{10... | collective-permute-start | bytes 294920 | tf_op jit(solution)/shard_map/ppermute | solution.py:402
  17.1 8.1 %collective-permute-start.8 = (bf16[12,32,128]{2,1,0:T(8,128)(2,1)S(1)}, bf16[12,32,128]{2,1,0:T(8,128)(2,1)S(1)}, u32[]{:S(2)}, u32[]{:S(2)}) collective-permute-start(bf16[12,32,128]{2,1,0:T(8,128)(2,1)S(1)} %get-tuple-element.67), channel_id=1, source_target_pairs={{0,1},{1,0},{2,3},{3,2},{4,5},{5,4},{6,7},{7,6},{8,9},{9,8},{10,11... | collective-permute-start | bytes 294920 | tf_op jit(solution)/shard_map/ppermute | solution.py:402
  20.2 5.0 %collective-permute-start.9 = (bf16[12,32,128]{2,1,0:T(8,128)(2,1)S(1)}, bf16[12,32,128]{2,1,0:T(8,128)(2,1)S(1)}, u32[]{:S(2)}, u32[]{:S(2)}) collective-permute-start(bf16[12,32,128]{2,1,0:T(8,128)(2,1)S(1)} %get-tuple-element.68), channel_id=1, source_target_pairs={{1,2},{2,1},{3,4},{4,3},{5,6},{6,5},{9,10},{10,9},{11,12},{12,11},... | collective-permute-start | bytes 294920 | tf_op jit(solution)/shard_map/ppermute | solution.py:402
  20.8 8.1 %collective-permute-start.10 = (bf16[12,32,128]{2,1,0:T(8,128)(2,1)S(1)}, bf16[12,32,128]{2,1,0:T(8,128)(2,1)S(1)}, u32[]{:S(2)}, u32[]{:S(2)}) collective-permute-start(bf16[12,32,128]{2,1,0:T(8,128)(2,1)S(1)} %get-tuple-element.71), channel_id=1, source_target_pairs={{8,16},{16,8},{9,17},{17,9},{10,18},{18,10},{11,19},{19,11},{12,20... | collective-permute-start | bytes 294920 | tf_op jit(solution)/shard_map/ppermute | solution.py:402
  22.5 6.4 %collective-permute-start.11 = (bf16[12,32,128]{2,1,0:T(8,128)(2,1)S(1)}, bf16[12,32,128]{2,1,0:T(8,128)(2,1)S(1)}, u32[]{:S(2)}, u32[]{:S(2)}) collective-permute-start(bf16[12,32,128]{2,1,0:T(8,128)(2,1)S(1)} %get-tuple-element.72), channel_id=1, source_target_pairs={{0,8},{8,0},{16,24},{24,16},{1,9},{9,1},{17,25},{25,17},{2,10},{10... | collective-permute-start | bytes 294920 | tf_op jit(solution)/shard_map/ppermute | solution.py:402
  25.8 7.4 %collective-permute-start.14 = (bf16[12,32,128]{2,1,0:T(8,128)(2,1)S(1)}, bf16[12,32,128]{2,1,0:T(8,128)(2,1)S(1)}, u32[]{:S(2)}, u32[]{:S(2)}) collective-permute-start(bf16[12,32,128]{2,1,0:T(8,128)(2,1)S(1)} %get-tuple-element.78), channel_id=1, source_target_pairs={{0,1},{1,0},{2,3},{3,2},{4,5},{5,4},{6,7},{7,6},{8,9},{9,8},{10,11... | collective-permute-start | bytes 294920 | tf_op jit(solution)/shard_map/ppermute | solution.py:402
  28.9 4.3 %collective-permute-start.15 = (bf16[12,32,128]{2,1,0:T(8,128)(2,1)S(1)}, bf16[12,32,128]{2,1,0:T(8,128)(2,1)S(1)}, u32[]{:S(2)}, u32[]{:S(2)}) collective-permute-start(bf16[12,32,128]{2,1,0:T(8,128)(2,1)S(1)} %get-tuple-element.79), channel_id=1, source_target_pairs={{1,2},{2,1},{3,4},{4,3},{5,6},{6,5},{9,10},{10,9},{11,12},{12,11},... | collective-permute-start | bytes 294920 | tf_op jit(solution)/shard_map/ppermute | solution.py:402
  29.7 4.5 %collective-permute-start.12 = (bf16[12,32,128]{2,1,0:T(8,128)(2,1)S(1)}, bf16[12,32,128]{2,1,0:T(8,128)(2,1)S(1)}, u32[]{:S(2)}, u32[]{:S(2)}) collective-permute-start(bf16[12,32,128]{2,1,0:T(8,128)(2,1)S(1)} %get-tuple-element.75), channel_id=1, source_target_pairs={{8,16},{16,8},{9,17},{17,9},{10,18},{18,10},{11,19},{19,11},{12,20... | collective-permute-start | bytes 294920 | tf_op jit(solution)/shard_map/ppermute | solution.py:402
  30.4 3.8 %collective-permute-start.13 = (bf16[12,32,128]{2,1,0:T(8,128)(2,1)S(1)}, bf16[12,32,128]{2,1,0:T(8,128)(2,1)S(1)}, u32[]{:S(2)}, u32[]{:S(2)}) collective-permute-start(bf16[12,32,128]{2,1,0:T(8,128)(2,1)S(1)} %get-tuple-element.76), channel_id=1, source_target_pairs={{0,8},{8,0},{16,24},{24,16},{1,9},{9,1},{17,25},{25,17},{2,10},{10... | collective-permute-start | bytes 294920 | tf_op jit(solution)/shard_map/ppermute | solution.py:402

commit v7 on v6

--- a/solution.py
+++ b/solution.py
@@ -318,7 +318,7 @@
     return over(parts)
 
 
-def orthonormal(scale, grams_ref, wide_ref, rest_ref, out_ref):
+def orthonormal(scale, grams_ref, wide_ref, rest_ref, out_hbm, out_ref, sems):
     packed = jnp.sum(grams_ref[...], axis=0)
     n = wide_ref.shape[0]
     gram = over([packed[:, n * i : n * (i + 1)] for i in range(n // 8)])
@@ -327,19 +327,24 @@
     left = beside([a[i] for i, _ in pairs])
     width = 4 * LANES
     at = 0
+    copies = []
     for ref, first in ((rest_ref, 0), (wide_ref, 0), (rest_ref, 2 * RIM * LANES)):
         last = 2 * RIM * LANES if first == 0 else ref.shape[1]
         for start in range(first, last, width):
             y = three(ref[:, start : start + width])
             out_ref[:, at : at + width] = mm(left, over([y[j] for _, j in pairs]), ROWS_BY_COLS)
+            piece = pl.ds(at, width)
+            copies.append(fetch(out_ref.at[:, piece], out_hbm.at[:, piece], sems.at[at // width]))
             at += width
+    for copy in copies:
+        copy.wait()
 
 
 def in_vmem(x):
     return pltpu.with_memory_space_constraint(x, pltpu.VMEM)
 
 
-def kernel_call(body, name, ins, outs, scratch=(), flops=0, moved=0):
+def kernel_call(body, name, ins, outs, scratch=(), flops=0, moved=0, out_at=pltpu.VMEM):
     specs, args = [], []
     for kind, x in ins:
         if kind == "hbm":
@@ -361,7 +366,7 @@
             for s, d in outs
         ],
         in_specs=specs,
-        out_specs=[pl.BlockSpec(memory_space=pltpu.SMEM if d == jnp.int32 else pltpu.VMEM) for _, d in outs],
+        out_specs=[pl.BlockSpec(memory_space=pltpu.SMEM if d == jnp.int32 else out_at) for _, d in outs],
         scratch_shapes=list(scratch),
         compiler_params=pltpu.CompilerParams(vmem_limit_bytes=16 << 20),
         cost_estimate=pl.CostEstimate(flops=flops, bytes_accessed=moved, transcendentals=0),
@@ -487,6 +492,7 @@
     (out,) = kernel_call(
         functools.partial(orthonormal, math.sqrt(peers * docs)), "orthonormal",
         [("vmem", grams), ("vmem", y[0]), ("vmem", y[1])], [full],
+        [pltpu.VMEM(*full), pltpu.SemaphoreType.DMA((docs // (4 * LANES),))], out_at=pl.ANY,
     )
     return out[None, None]
 

time: 48.2 us -> 48.3 us (level)
  no operation moved by 1% of the time
where the time goes in v7:
time: 48.3 us; the launch traced here: 48.1 us
  Pallas kernels  19.3 us (40%)
  starting transfers between devices  17 us (35%)
  blocking collectives  11 us (23%)
    pallas_call x14, Pallas kernels, kernel_call(): pl.pallas_call(body, name=name, out_shape=[pltpu.SMEM(s, d) if d == jnp.i...  19.3 us
    ppermute x16, starting transfers between devices, exchange(): lax.ppermute(payload, ('narrow', 'wide'), pairs[m])  17 us
    all_to_all x1, blocking collectives, body(): grams = lax.all_to_all(grams, ('narrow', 'wide'), 0, 0)  11 us
  transfers between devices with their start and end apart: 16, of which 2 were waited for; matrix products, arithmetic and copies ran while one was open for 0% of the time, Pallas kernels for 30%

profile of v7, /device:TPU:0, one launch (start us, length us, event | category | flops | bytes accessed | tf_op | source)
XLA Modules:
  0.0 48.1 jit_solution(5157127490445535778)
XLA Ops:
  0.0 0.0 copy-start
  0.0 0.0 copy-start.1
  0.0 2.1 %outgoing_ones.1 = (f32[8,128]{1,0:T(8,128)S(1)}, f32[8,128]{1,0:T(8,128)S(1)}, f32[8,128]{1,0:T(8,128)S(1)}, f32[8,128]{1,0:T(8,128)S(1)}, s32[12,1,28]{2,1,0:T(1,128)S(4)}) custom-call(s32[12,1,28]{2,1,0:T(1,128)} %bitcast.25, bf16[28,12,128,128]{3,2,1,0:T(8,128)(2,1)} %bitcast.6), custom_call_target="tpu_custom_call" | custom-call | flops 75497472 | bytes 1048576 | tf_op jit(solution)/shard_map/outgoing_ones/pallas_call | solution.py:361
  2.1 3.0 %collective-permute-start = (f32[8,128]{1,0:T(8,128)S(1)}, f32[8,128]{1,0:T(8,128)S(1)}, u32[]{:S(2)}, u32[]{:S(2)}) collective-permute-start(f32[8,128]{1,0:T(8,128)S(1)} %get-tuple-element.51), channel_id=1, source_target_pairs={{0,1},{1,0},{2,3},{3,2},{4,5},{5,4},{6,7},{7,6},{8,9},{9,8},{10,11... | collective-permute-start | bytes 12296 | tf_op jit(solution)/shard_map/ppermute | solution.py:407
  5.2 0.0 collective-permute-start.1
  5.2 1.6 %collective-permute-start.2 = (f32[8,128]{1,0:T(8,128)S(1)}, f32[8,128]{1,0:T(8,128)S(1)}, u32[]{:S(2)}, u32[]{:S(2)}) collective-permute-start(f32[8,128]{1,0:T(8,128)S(1)} %get-tuple-element.54), channel_id=1, source_target_pairs={{8,16},{16,8},{9,17},{17,9},{10,18},{18,10},{11,19},{19,11},{12,20... | collective-permute-start | bytes 12296 | tf_op jit(solution)/shard_map/ppermute | solution.py:407
  6.8 0.0 collective-permute-start.3
  6.8 0.0 copy-done
  6.8 1.8 %local_degree.1.deg_ref = f32[28,128]{1,0:T(8,128)S(1)} custom-call(s32[12,1,28]{2,1,0:T(1,128)S(4)} %get-tuple-element.45.pattern_ref, bf16[28,12,128,128]{3,2,1,0:T(8,128)(2,1)S(1)} %bitcast.7), custom_call_target="tpu_custom_call" | custom-call | flops 352321536 | bytes 8388608 | tf_op jit(solution)/shard_map/local_degree/pallas_call | solution.py:361
  8.6 0.0 collective-permute-done.refs_0_
  8.6 0.0 collective-permute-done.1.refs_1_
  8.6 0.0 copy-done.1
  8.6 0.4 first_scaled.2
  9.0 3.1 %collective-permute-start.4 = (bf16[12,32,128]{2,1,0:T(8,128)(2,1)S(1)}, bf16[12,32,128]{2,1,0:T(8,128)(2,1)S(1)}, u32[]{:S(2)}, u32[]{:S(2)}) collective-permute-start(bf16[12,32,128]{2,1,0:T(8,128)(2,1)S(1)} %get-tuple-element.61), channel_id=1, source_target_pairs={{0,1},{1,0},{2,3},{3,2},{4,5},{5,4},{6,7},{7,6},{8,9},{9,8},{10,11... | collective-permute-start | bytes 294920 | tf_op jit(solution)/shard_map/ppermute | solution.py:407
  12.1 0.0 collective-permute-start.5
  12.1 0.0 collective-permute-done.2.refs_0_
  12.1 0.0 collective-permute-done.3.refs_1_
  12.1 0.4 first_scaled.3
  12.5 0.7 %collective-permute-start.6 = (bf16[12,32,128]{2,1,0:T(8,128)(2,1)S(1)}, bf16[12,32,128]{2,1,0:T(8,128)(2,1)S(1)}, u32[]{:S(2)}, u32[]{:S(2)}) collective-permute-start(bf16[12,32,128]{2,1,0:T(8,128)(2,1)S(1)} %get-tuple-element.64), channel_id=1, source_target_pairs={{8,16},{16,8},{9,17},{17,9},{10,18},{18,10},{11,19},{19,11},{12,20... | collective-permute-start | bytes 294920 | tf_op jit(solution)/shard_map/ppermute | solution.py:407
  13.3 0.0 collective-permute-start.7
  13.3 3.2 %own_terms_turning.1 = (f32[28,32,128]{2,1,0:T(8,128)S(1)}, bf16[28,12,128,128]{3,2,1,0:T(8,128)(2,1)S(1)}) custom-call(s32[12,1,28]{2,1,0:T(1,128)S(4)} %get-tuple-element.45.pattern_ref, bf16[28,12,128,128]{3,2,1,0:T(8,128)(2,1)S(1)} %bitcast.10, bf16[12,32,128]{2,1,0:T(8,128)(2,1)S(1)} %get-tuple-element.53.u_wide, ...), custom_call_target="tpu_custom_call" | custom-call | flops 704643072 | bytes 8388608 | tf_op jit(solution)/shard_map/own_terms_turning/pallas_call | solution.py:361
  16.4 0.0 collective-permute-done.4.refs_0_
  16.5 0.0 collective-permute-done.5.refs_1_
  16.5 0.6 %advance.4 = (f32[32,1536]{1,0:T(8,128)S(1)}, bf16[12,32,128]{2,1,0:T(8,128)(2,1)S(1)}, bf16[12,32,128]{2,1,0:T(8,128)(2,1)S(1)}, bf16[12,32,128]{2,1,0:T(8,128)(2,1)S(1)}) custom-call(s32[12,1,28]{2,1,0:T(1,128)S(4)} %get-tuple-element.45.pattern_ref, bf16[28,12,128,128]{3,2,1,0:T(8,128)(2,1)S(1)} %bitcast.11, ...), custom_call_target="tpu_custom_call" | custom-call | flops 75497472 | bytes 524288 | tf_op jit(solution)/shard_map/advance/pallas_call | solution.py:361
  17.1 3.1 %collective-permute-start.8 = (bf16[12,32,128]{2,1,0:T(8,128)(2,1)S(1)}, bf16[12,32,128]{2,1,0:T(8,128)(2,1)S(1)}, u32[]{:S(2)}, u32[]{:S(2)}) collective-permute-start(bf16[12,32,128]{2,1,0:T(8,128)(2,1)S(1)} %get-tuple-element.67), channel_id=1, source_target_pairs={{0,1},{1,0},{2,3},{3,2},{4,5},{5,4},{6,7},{7,6},{8,9},{9,8},{10,11... | collective-permute-start | bytes 294920 | tf_op jit(solution)/shard_map/ppermute | solution.py:407
  20.2 0.0 collective-permute-start.9
  20.2 0.0 collective-permute-done.6.refs_0_
  20.2 0.0 collective-permute-done.7.refs_1_
  20.2 0.6 %advance.5 = (f32[32,2048]{1,0:T(8,128)S(1)}, bf16[16,32,128]{2,1,0:T(8,128)(2,1)S(1)}, bf16[12,32,128]{2,1,0:T(8,128)(2,1)S(1)}, bf16[12,32,128]{2,1,0:T(8,128)(2,1)S(1)}) custom-call(s32[12,1,28]{2,1,0:T(1,128)S(4)} %get-tuple-element.45.pattern_ref, bf16[28,12,128,128]{3,2,1,0:T(8,128)(2,1)S(1)} %bitcast.12, ...), custom_call_target="tpu_custom_call" | custom-call | flops 75497472 | bytes 524288 | tf_op jit(solution)/shard_map/advance/pallas_call | solution.py:361
  20.8 1.7 %collective-permute-start.10 = (bf16[12,32,128]{2,1,0:T(8,128)(2,1)S(1)}, bf16[12,32,128]{2,1,0:T(8,128)(2,1)S(1)}, u32[]{:S(2)}, u32[]{:S(2)}) collective-permute-start(bf16[12,32,128]{2,1,0:T(8,128)(2,1)S(1)} %get-tuple-element.71), channel_id=1, source_target_pairs={{8,16},{16,8},{9,17},{17,9},{10,18},{18,10},{11,19},{19,11},{12,20... | collective-permute-start | bytes 294920 | tf_op jit(solution)/shard_map/ppermute | solution.py:407
  22.5 0.0 collective-permute-start.11
  22.5 2.7 %own_terms.2.acc_ref = f32[28,32,128]{2,1,0:T(8,128)S(1)} custom-call(s32[12,1,28]{2,1,0:T(1,128)S(4)} %get-tuple-element.45.pattern_ref, bf16[28,12,128,128]{3,2,1,0:T(8,128)(2,1)S(1)} %bitcast.13, bf16[28,12,128,128]{3,2,1,0:T(8,128)(2,1)S(1)} %get-tuple-element.57.turned_ref, bf16[12,32,128]{2,1,0:T(8,128)(2,1)S(1)} %get-tuple-element.63.u_wide, ...), custom_call_target="tpu_custom_call" | custom-call | flops 704643072 | bytes 8388608 | tf_op jit(solution)/shard_map/own_terms/pallas_call | solution.py:361
  25.2 0.0 collective-permute-done.8.refs_0_
  25.2 0.0 collective-permute-done.9.refs_1_
  25.2 0.6 %advance.6 = (f32[32,1536]{1,0:T(8,128)S(1)}, bf16[12,32,128]{2,1,0:T(8,128)(2,1)S(1)}, bf16[12,32,128]{2,1,0:T(8,128)(2,1)S(1)}, bf16[12,32,128]{2,1,0:T(8,128)(2,1)S(1)}) custom-call(s32[12,1,28]{2,1,0:T(1,128)S(4)} %get-tuple-element.45.pattern_ref, bf16[28,12,128,128]{3,2,1,0:T(8,128)(2,1)S(1)} %bitcast.14, ...), custom_call_target="tpu_custom_call" | custom-call | flops 75497472 | bytes 524288 | tf_op jit(solution)/shard_map/advance/pallas_call | solution.py:361
  25.8 3.1 %collective-permute-start.14 = (bf16[12,32,128]{2,1,0:T(8,128)(2,1)S(1)}, bf16[12,32,128]{2,1,0:T(8,128)(2,1)S(1)}, u32[]{:S(2)}, u32[]{:S(2)}) collective-permute-start(bf16[12,32,128]{2,1,0:T(8,128)(2,1)S(1)} %get-tuple-element.78), channel_id=1, source_target_pairs={{0,1},{1,0},{2,3},{3,2},{4,5},{5,4},{6,7},{7,6},{8,9},{9,8},{10,11... | collective-permute-start | bytes 294920 | tf_op jit(solution)/shard_map/ppermute | solution.py:407
  28.9 0.0 collective-permute-start.15
  28.9 0.0 collective-permute-done.10.refs_0_
  28.9 0.0 collective-permute-done.11.refs_1_
  28.9 0.8 %advance.7 = (f32[32,2048]{1,0:T(8,128)S(1)}, bf16[16,32,128]{2,1,0:T(8,128)(2,1)S(1)}, bf16[12,32,128]{2,1,0:T(8,128)(2,1)S(1)}, bf16[12,32,128]{2,1,0:T(8,128)(2,1)S(1)}) custom-call(s32[12,1,28]{2,1,0:T(1,128)S(4)} %get-tuple-element.45.pattern_ref, bf16[28,12,128,128]{3,2,1,0:T(8,128)(2,1)S(1)} %bitcast.15, ...), custom_call_target="tpu_custom_call" | custom-call | flops 75497472 | bytes 524288 | tf_op jit(solution)/shard_map/advance/pallas_call | solution.py:361
  29.7 0.7 %collective-permute-start.12 = (bf16[12,32,128]{2,1,0:T(8,128)(2,1)S(1)}, bf16[12,32,128]{2,1,0:T(8,128)(2,1)S(1)}, u32[]{:S(2)}, u32[]{:S(2)}) collective-permute-start(bf16[12,32,128]{2,1,0:T(8,128)(2,1)S(1)} %get-tuple-element.75), channel_id=1, source_target_pairs={{8,16},{16,8},{9,17},{17,9},{10,18},{18,10},{11,19},{19,11},{12,20... | collective-permute-start | bytes 294920 | tf_op jit(solution)/shard_map/ppermute | solution.py:407
  30.4 0.0 collective-permute-start.13
  30.4 2.7 %own_terms.3.acc_ref = f32[28,32,128]{2,1,0:T(8,128)S(1)} custom-call(s32[12,1,28]{2,1,0:T(1,128)S(4)} %get-tuple-element.45.pattern_ref, bf16[28,12,128,128]{3,2,1,0:T(8,128)(2,1)S(1)} %bitcast.16, bf16[28,12,128,128]{3,2,1,0:T(8,128)(2,1)S(1)} %get-tuple-element.57.turned_ref, bf16[12,32,128]{2,1,0:T(8,128)(2,1)S(1)} %get-tuple-element.70.u_wide, ...), custom_call_target="tpu_custom_call" | custom-call | flops 704643072 | bytes 8388608 | tf_op jit(solution)/shard_map/own_terms/pallas_call | solution.py:361
  33.1 0.1 collective-permute-done.14.refs_0_
  33.2 0.0 collective-permute-done.15.refs_1_
  33.2 0.7 %finish.2 = (f32[32,1536]{1,0:T(8,128)S(1)}, f32[8,128]{1,0:T(8,128)S(1)}) custom-call(s32[12,1,28]{2,1,0:T(1,128)S(4)} %get-tuple-element.45.pattern_ref, bf16[28,12,128,128]{3,2,1,0:T(8,128)(2,1)S(1)} %get-tuple-element.57.turned_ref, f32[12,128]{1,0:T(8,128)S(1)} %get-tuple-element.59.inv_ref, f32[28,32,128]{2,1,0:T(8,128)S(1)} %own_terms.3.acc_ref, ...), custom_call_target="tpu_custom_call" | custom-call | flops 37748736 | bytes 524288 | tf_op jit(solution)/shard_map/finish/pallas_call | solution.py:361
  33.9 0.3 collective-permute-done.12.refs_0_
  34.2 0.0 collective-permute-done.13.refs_1_
  34.2 0.7 %finish.3 = (f32[32,2048]{1,0:T(8,128)S(1)}, f32[32,8,128]{2,1,0:T(8,128)S(1)}) custom-call(s32[12,1,28]{2,1,0:T(1,128)S(4)} %get-tuple-element.45.pattern_ref, bf16[28,12,128,128]{3,2,1,0:T(8,128)(2,1)S(1)} %get-tuple-element.57.turned_ref, f32[16,128]{1,0:T(8,128)S(1)} %get-tuple-element.58.inv_ref, f32[28,32,128]{2,1,0:T(8,128)S(1)} %own_terms.3.acc_ref, ...), custom_call_target="tpu_custom_call" | custom-call | flops 37748736 | bytes 524288 | tf_op jit(solution)/shard_map/finish/pallas_call | solution.py:361
  35.0 11.0 %all_to_all.5.grams_ref = f32[32,8,128]{2,1,0:T(8,128)S(1)} all-to-all(f32[32,8,128]{2,1,0:T(8,128)S(1)} %get-tuple-element.82), channel_id=1, replica_groups=mesh['narrow'=4,'wide'=8] {'narrow','wide'}, dimensions={0} | all-to-all | bytes 262144 | tf_op jit(solution)/shard_map/all_to_all | solution.py:491
  46.0 2.0 %orthonormal.1 = f32[32,3584]{1,0:T(8,128)} custom-call(f32[32,8,128]{2,1,0:T(8,128)S(1)} %all_to_all.5.grams_ref, f32[32,1536]{1,0:T(8,128)S(1)} %get-tuple-element.83.wide_ref, f32[32,2048]{1,0:T(8,128)S(1)} %get-tuple-element.84.rest_ref), custom_call_target="tpu_custom_call" | custom-call | tf_op jit(solution)/shard_map/orthonormal/pallas_call | solution.py:361
Async XLA Ops:
  0.0 6.8 %copy-start = (bf16[1,1,28,12,128,128]{5,4,3,2,1,0:T(8,128)(2,1)S(1)}, bf16[1,1,28,12,128,128]{5,4,3,2,1,0:T(8,128)(2,1)}, u32[]{:S(2)}) copy-start(bf16[1,1,28,12,128,128]{5,4,3,2,1,0:T(8,128)(2,1)} %param.4) | copy-start | bytes 33030148
  0.0 8.6 %copy-start.1 = (bf16[1,1,32,3584]{3,2,1,0:T(8,128)(2,1)S(1)}, bf16[1,1,32,3584]{3,2,1,0:T(8,128)(2,1)}, u32[]{:S(2)}) copy-start(bf16[1,1,32,3584]{3,2,1,0:T(8,128)(2,1)} %param.3) | copy-start | bytes 688132
  2.1 6.5 %collective-permute-start = (f32[8,128]{1,0:T(8,128)S(1)}, f32[8,128]{1,0:T(8,128)S(1)}, u32[]{:S(2)}, u32[]{:S(2)}) collective-permute-start(f32[8,128]{1,0:T(8,128)S(1)} %get-tuple-element.51), channel_id=1, source_target_pairs={{0,1},{1,0},{2,3},{3,2},{4,5},{5,4},{6,7},{7,6},{8,9},{9,8},{10,11... | collective-permute-start | bytes 12296 | tf_op jit(solution)/shard_map/ppermute | solution.py:407
  5.2 3.5 %collective-permute-start.1 = (f32[8,128]{1,0:T(8,128)S(1)}, f32[8,128]{1,0:T(8,128)S(1)}, u32[]{:S(2)}, u32[]{:S(2)}) collective-permute-start(f32[8,128]{1,0:T(8,128)S(1)} %get-tuple-element.52), channel_id=1, source_target_pairs={{1,2},{2,1},{3,4},{4,3},{5,6},{6,5},{9,10},{10,9},{11,12},{12,11},... | collective-permute-start | bytes 12296 | tf_op jit(solution)/shard_map/ppermute | solution.py:407
  5.2 7.0 %collective-permute-start.2 = (f32[8,128]{1,0:T(8,128)S(1)}, f32[8,128]{1,0:T(8,128)S(1)}, u32[]{:S(2)}, u32[]{:S(2)}) collective-permute-start(f32[8,128]{1,0:T(8,128)S(1)} %get-tuple-element.54), channel_id=1, source_target_pairs={{8,16},{16,8},{9,17},{17,9},{10,18},{18,10},{11,19},{19,11},{12,20... | collective-permute-start | bytes 12296 | tf_op jit(solution)/shard_map/ppermute | solution.py:407
  6.8 5.4 %collective-permute-start.3 = (f32[8,128]{1,0:T(8,128)S(1)}, f32[8,128]{1,0:T(8,128)S(1)}, u32[]{:S(2)}, u32[]{:S(2)}) collective-permute-start(f32[8,128]{1,0:T(8,128)S(1)} %get-tuple-element.55), channel_id=1, source_target_pairs={{0,8},{8,0},{16,24},{24,16},{1,9},{9,1},{17,25},{25,17},{2,10},{10... | collective-permute-start | bytes 12296 | tf_op jit(solution)/shard_map/ppermute | solution.py:407
  9.0 7.4 %collective-permute-start.4 = (bf16[12,32,128]{2,1,0:T(8,128)(2,1)S(1)}, bf16[12,32,128]{2,1,0:T(8,128)(2,1)S(1)}, u32[]{:S(2)}, u32[]{:S(2)}) collective-permute-start(bf16[12,32,128]{2,1,0:T(8,128)(2,1)S(1)} %get-tuple-element.61), channel_id=1, source_target_pairs={{0,1},{1,0},{2,3},{3,2},{4,5},{5,4},{6,7},{7,6},{8,9},{9,8},{10,11... | collective-permute-start | bytes 294920 | tf_op jit(solution)/shard_map/ppermute | solution.py:407
  12.1 4.3 %collective-permute-start.5 = (bf16[12,32,128]{2,1,0:T(8,128)(2,1)S(1)}, bf16[12,32,128]{2,1,0:T(8,128)(2,1)S(1)}, u32[]{:S(2)}, u32[]{:S(2)}) collective-permute-start(bf16[12,32,128]{2,1,0:T(8,128)(2,1)S(1)} %get-tuple-element.62), channel_id=1, source_target_pairs={{1,2},{2,1},{3,4},{4,3},{5,6},{6,5},{9,10},{10,9},{11,12},{12,11},... | collective-permute-start | bytes 294920 | tf_op jit(solution)/shard_map/ppermute | solution.py:407
  12.5 7.6 %collective-permute-start.6 = (bf16[12,32,128]{2,1,0:T(8,128)(2,1)S(1)}, bf16[12,32,128]{2,1,0:T(8,128)(2,1)S(1)}, u32[]{:S(2)}, u32[]{:S(2)}) collective-permute-start(bf16[12,32,128]{2,1,0:T(8,128)(2,1)S(1)} %get-tuple-element.64), channel_id=1, source_target_pairs={{8,16},{16,8},{9,17},{17,9},{10,18},{18,10},{11,19},{19,11},{12,20... | collective-permute-start | bytes 294920 | tf_op jit(solution)/shard_map/ppermute | solution.py:407
  13.3 6.9 %collective-permute-start.7 = (bf16[12,32,128]{2,1,0:T(8,128)(2,1)S(1)}, bf16[12,32,128]{2,1,0:T(8,128)(2,1)S(1)}, u32[]{:S(2)}, u32[]{:S(2)}) collective-permute-start(bf16[12,32,128]{2,1,0:T(8,128)(2,1)S(1)} %get-tuple-element.65), channel_id=1, source_target_pairs={{0,8},{8,0},{16,24},{24,16},{1,9},{9,1},{17,25},{25,17},{2,10},{10... | collective-permute-start | bytes 294920 | tf_op jit(solution)/shard_map/ppermute | solution.py:407
  17.1 8.1 %collective-permute-start.8 = (bf16[12,32,128]{2,1,0:T(8,128)(2,1)S(1)}, bf16[12,32,128]{2,1,0:T(8,128)(2,1)S(1)}, u32[]{:S(2)}, u32[]{:S(2)}) collective-permute-start(bf16[12,32,128]{2,1,0:T(8,128)(2,1)S(1)} %get-tuple-element.67), channel_id=1, source_target_pairs={{0,1},{1,0},{2,3},{3,2},{4,5},{5,4},{6,7},{7,6},{8,9},{9,8},{10,11... | collective-permute-start | bytes 294920 | tf_op jit(solution)/shard_map/ppermute | solution.py:407
  20.2 5.0 %collective-permute-start.9 = (bf16[12,32,128]{2,1,0:T(8,128)(2,1)S(1)}, bf16[12,32,128]{2,1,0:T(8,128)(2,1)S(1)}, u32[]{:S(2)}, u32[]{:S(2)}) collective-permute-start(bf16[12,32,128]{2,1,0:T(8,128)(2,1)S(1)} %get-tuple-element.68), channel_id=1, source_target_pairs={{1,2},{2,1},{3,4},{4,3},{5,6},{6,5},{9,10},{10,9},{11,12},{12,11},... | collective-permute-start | bytes 294920 | tf_op jit(solution)/shard_map/ppermute | solution.py:407
  20.8 8.1 %collective-permute-start.10 = (bf16[12,32,128]{2,1,0:T(8,128)(2,1)S(1)}, bf16[12,32,128]{2,1,0:T(8,128)(2,1)S(1)}, u32[]{:S(2)}, u32[]{:S(2)}) collective-permute-start(bf16[12,32,128]{2,1,0:T(8,128)(2,1)S(1)} %get-tuple-element.71), channel_id=1, source_target_pairs={{8,16},{16,8},{9,17},{17,9},{10,18},{18,10},{11,19},{19,11},{12,20... | collective-permute-start | bytes 294920 | tf_op jit(solution)/shard_map/ppermute | solution.py:407
  22.5 6.4 %collective-permute-start.11 = (bf16[12,32,128]{2,1,0:T(8,128)(2,1)S(1)}, bf16[12,32,128]{2,1,0:T(8,128)(2,1)S(1)}, u32[]{:S(2)}, u32[]{:S(2)}) collective-permute-start(bf16[12,32,128]{2,1,0:T(8,128)(2,1)S(1)} %get-tuple-element.72), channel_id=1, source_target_pairs={{0,8},{8,0},{16,24},{24,16},{1,9},{9,1},{17,25},{25,17},{2,10},{10... | collective-permute-start | bytes 294920 | tf_op jit(solution)/shard_map/ppermute | solution.py:407
  25.8 7.4 %collective-permute-start.14 = (bf16[12,32,128]{2,1,0:T(8,128)(2,1)S(1)}, bf16[12,32,128]{2,1,0:T(8,128)(2,1)S(1)}, u32[]{:S(2)}, u32[]{:S(2)}) collective-permute-start(bf16[12,32,128]{2,1,0:T(8,128)(2,1)S(1)} %get-tuple-element.78), channel_id=1, source_target_pairs={{0,1},{1,0},{2,3},{3,2},{4,5},{5,4},{6,7},{7,6},{8,9},{9,8},{10,11... | collective-permute-start | bytes 294920 | tf_op jit(solution)/shard_map/ppermute | solution.py:407
  28.9 4.3 %collective-permute-start.15 = (bf16[12,32,128]{2,1,0:T(8,128)(2,1)S(1)}, bf16[12,32,128]{2,1,0:T(8,128)(2,1)S(1)}, u32[]{:S(2)}, u32[]{:S(2)}) collective-permute-start(bf16[12,32,128]{2,1,0:T(8,128)(2,1)S(1)} %get-tuple-element.79), channel_id=1, source_target_pairs={{1,2},{2,1},{3,4},{4,3},{5,6},{6,5},{9,10},{10,9},{11,12},{12,11},... | collective-permute-start | bytes 294920 | tf_op jit(solution)/shard_map/ppermute | solution.py:407
  29.7 4.5 %collective-permute-start.12 = (bf16[12,32,128]{2,1,0:T(8,128)(2,1)S(1)}, bf16[12,32,128]{2,1,0:T(8,128)(2,1)S(1)}, u32[]{:S(2)}, u32[]{:S(2)}) collective-permute-start(bf16[12,32,128]{2,1,0:T(8,128)(2,1)S(1)} %get-tuple-element.75), channel_id=1, source_target_pairs={{8,16},{16,8},{9,17},{17,9},{10,18},{18,10},{11,19},{19,11},{12,20... | collective-permute-start | bytes 294920 | tf_op jit(solution)/shard_map/ppermute | solution.py:407
  30.4 3.8 %collective-permute-start.13 = (bf16[12,32,128]{2,1,0:T(8,128)(2,1)S(1)}, bf16[12,32,128]{2,1,0:T(8,128)(2,1)S(1)}, u32[]{:S(2)}, u32[]{:S(2)}) collective-permute-start(bf16[12,32,128]{2,1,0:T(8,128)(2,1)S(1)} %get-tuple-element.76), channel_id=1, source_target_pairs={{0,8},{8,0},{16,24},{24,16},{1,9},{9,1},{17,25},{25,17},{2,10},{10... | collective-permute-start | bytes 294920 | tf_op jit(solution)/shard_map/ppermute | solution.py:407
